TPU v7x, 128 devices: a whole 4x4x4 slice. The times are simulated.
128 devices in a mesh: rows: 8 (over x_hi, y), cols: 16 (over z, x_lo, core).
Axes of the slice: x: 4 (x_hi: 2, x_lo: 2; x = x_hi * 2 + x_lo), y: 4, z: 4, core: 2. Of those that a mesh axis runs over, the one named last changes fastest.
Arguments:
- features: bfloat16 [2048, 512], P(('rows', 'cols')), may hold values from -6 to 6
- tower_weight: bfloat16 [2, 3, 512, 512], replicated, may hold values from -0.15625 to 0.15625
- tower_bias: float32 [2, 512], replicated, may hold values from -0.5 to 0.5
- pair_proj: bfloat16 [512, 64], replicated, may hold values from -0.25 to 0.25
- dist_gain: float32 [32], replicated, may hold values from -1 to 1
- map_weight: bfloat16 [3, 3, 3, 32, 32], replicated, may hold values from -0.375 to 0.375
- map_bias: float32 [3, 32], replicated, may hold values from -0.5 to 0.5
- dilations: int32 [5], replicated, may hold values from 1 to 16, as said below
- start_bin: int32 [1], replicated, may hold values from 0 to 99999
Outputs:
- pair_map: bfloat16 [32, 2048, 2048], P(None, 'rows', 'cols')
Inputs may be any that keep to these rules, and one draw needn't show every extreme that they name: `dilations`: the first 2 entries lie in 1 to 16 and at least one equals 16; the last 3 lie in 1 to 16 and at least one equals 16.
All inputs are finite; a program needn't handle non-finite values.
Results may differ from a plain program's by a relative error of at most 0.013.
Values may be sent and summed in bfloat16 or wider, within the bound.
No kernel may reach another device: no remote copies, remote signals or barrier semaphores. Data moves between devices by JAX's collectives and lax.ppermute only.
A program may use at most 192 MiB of HBM per device.

v0:
```python
import math

import jax
import jax.numpy as jnp
from jax import lax
from jax.sharding import PartitionSpec as P

DMAX1 = 16
DMAX2 = 16


def padded_2(value, sides, width):
    for axis, dim in sides:
        devices, length = (lax.axis_size(axis), value.shape[dim])
        up = [(i, (i + 1) % devices) for i in range(devices - 1)]
        down = [(j, i) for i, j in up]
        last = lax.slice_in_dim(value, length - width, length, axis=dim)
        leading = lax.slice_in_dim(value, 0, width, axis=dim)
        before = lax.ppermute(last, axis, up)
        after = lax.ppermute(leading, axis, down)
        value = jnp.concatenate([before, value, after], axis=dim)
    return value


def position_code(bin_index, start_pos, map_width):
    half_width = map_width // 2
    position = ((start_pos + bin_index) % 8192).astype(jnp.float32)
    rates = jnp.exp(-jnp.arange(half_width).astype(jnp.float32) * (math.log(1000.0) / half_width))
    phase_angle = position[:, None] * rates[None, :]
    return jnp.concatenate([jnp.cos(phase_angle), jnp.sin(phase_angle)], axis=1)


def tower_layer(widened, hidden, weight_set, bias_set, dilation, margin):
    count = hidden.shape[0]
    running = jnp.zeros((count, weight_set.shape[2]), jnp.float32)
    for tap in range(3):
        offset = margin + (tap - 1) * dilation
        tap_slice = lax.dynamic_slice_in_dim(widened, offset, count, 0)
        running = running + jnp.dot(tap_slice, weight_set[tap], preferred_element_type=jnp.float32)
    return (hidden.astype(jnp.float32) + jax.nn.relu(running + bias_set[None, :])).astype(
        jnp.bfloat16
    )


def build_pair(row_code, col_code, row_first, col_first, dist_gain):
    row_glob = row_first + jnp.arange(row_code.shape[0])
    col_glob = col_first + jnp.arange(col_code.shape[0])
    distance = (
        jnp.log(1.0 + jnp.abs(row_glob[:, None] - col_glob[None, :]).astype(jnp.float32)) * 0.125
    )
    summed = (
        row_code.T.astype(jnp.float32)[:, :, None]
        + col_code.T.astype(jnp.float32)[:, None, :]
        + dist_gain[:, None, None] * distance[None, :, :]
    )
    return jax.nn.relu(summed).astype(jnp.bfloat16)


def conv_step(padded, center, weight_set, bias_set, dilation, margin):
    chans, nrow, ncol = center.shape
    running = jnp.zeros((weight_set.shape[2], nrow * ncol), jnp.float32)
    zero_index = jnp.zeros((), jnp.int32)
    for tap_row in range(3):
        for tap_col in range(3):
            row_start = margin + (tap_row - 1) * dilation
            col_start = margin + (tap_col - 1) * dilation
            tap_slice = lax.dynamic_slice(
                padded, (zero_index, row_start, col_start), (chans, nrow, ncol)
            )
            running = running + jnp.dot(
                weight_set[tap_row, tap_col],
                tap_slice.reshape(chans, nrow * ncol),
                preferred_element_type=jnp.float32,
            )
    running = running.reshape(weight_set.shape[2], nrow, ncol) + bias_set[:, None, None]
    return (center.astype(jnp.float32) + jax.nn.relu(running)).astype(jnp.bfloat16)


def project(hidden, pair_proj, bin_index, start_pos, map_width):
    projected = jnp.dot(hidden, pair_proj, preferred_element_type=jnp.float32)
    row_code = (projected[:, :map_width] + position_code(bin_index, start_pos, map_width)).astype(
        jnp.bfloat16
    )
    col_code = projected[:, map_width:].astype(jnp.bfloat16)
    return (row_code, col_code)


def on_device(
    features,
    tower_weight,
    tower_bias,
    pair_proj,
    dist_gain,
    map_weight,
    map_bias,
    dilations,
    start_bin,
):
    row_count = lax.axis_size("rows")
    col_count = lax.axis_size("cols")
    shard_bins = features.shape[0]
    total_bins = shard_bins * row_count * col_count
    tile_rows = total_bins // row_count
    tile_cols = total_bins // col_count
    map_width = map_weight.shape[-1]
    encoder_layers = tower_weight.shape[0]
    map_layers = map_weight.shape[0]
    row_place = lax.axis_index("rows")
    col_place = lax.axis_index("cols")
    start_pos = start_bin[0]
    hidden = features
    for layer in range(encoder_layers):
        widened = padded_2(hidden, ((("rows", "cols"), 0),), DMAX1)
        hidden = tower_layer(
            widened, hidden, tower_weight[layer], tower_bias[layer], dilations[layer], DMAX1
        )
    whole = lax.all_gather(hidden, ("rows", "cols"), axis=0, tiled=True)
    row_code, col_code = project(whole, pair_proj, jnp.arange(total_bins), start_pos, map_width)
    row_first = row_place * tile_rows
    col_first = col_place * tile_cols
    rows_here = lax.dynamic_slice_in_dim(row_code, row_first, tile_rows, 0)
    cols_here = lax.dynamic_slice_in_dim(col_code, col_first, tile_cols, 0)
    field = build_pair(rows_here, cols_here, row_first, col_first, dist_gain)
    for layer in range(map_layers):
        haloed = padded_2(field, (("rows", 1), ("cols", 2)), DMAX2)
        field = conv_step(
            haloed,
            field,
            map_weight[layer],
            map_bias[layer],
            dilations[encoder_layers + layer],
            DMAX2,
        )
    return field


def solution(mesh):
    placed = (P(("rows", "cols"), None), P(), P(), P(), P(), P(), P(), P(), P())
    return jax.shard_map(
        on_device, mesh=mesh, in_specs=placed, out_specs=P(None, "rows", "cols"), check_vma=False
    )
```

profile of v0, /device:TPU:27, one launch (start us, length us, event | category | flops | bytes accessed | tf_op | source)
XLA Modules:
  0.0 529.1 jit_solution(9332194547762019802)
XLA Ops:
  6.5 2.7 collective-permute-start.1
  9.3 3.9 collective-permute-start
  15.1 1.5 fusion.129
  23.7 1.9 collective-permute-start.3
  25.6 4.5 collective-permute-start.2
  32.6 1.8 add_convert_fusion
  35.9 199.9 %all-gather.2.cloned.1.call-done = bf16[2048,512]{1,0:T(8,128)(2,1)} async-done(((bf16[16,512]{1,0:T(8,128)(2,1)}), bf16[2048,512]{1,0:T(8,128)(2,1)}) %all-gather.2.cloned.1.call-update) | async-done | bytes 2097168 | tf_op jit(solution)/shard_map/all_gather | solution.py:117
  235.8 2.3 fusion.130
  239.5 4.0 collective-permute-start.4
  243.6 1.9 collective-permute-start.5
  245.5 7.4 %collective-permute-done.5 = bf16[32,16,128]{2,1,0:T(8,128)(2,1)S(1)} collective-permute-done((bf16[32,16,128]{2,1,0:T(8,128)(2,1)S(1)}, bf16[32,16,128]{2,1,0:T(8,128)(2,1)S(1)}, u32[]{:S(2)}, u32[]{:S(2)}) %collective-permute-start.5) | collective-permute-done | bytes 131104 | tf_op jit(solution)/shard_map/ppermute | solution.py:20
  253.1 3.0 fusion.124
  256.1 2.9 copy.46
  258.9 2.2 copy.47
  261.2 4.5 collective-permute-start.7
  265.6 3.8 collective-permute-start.6
  272.1 1.6 slice_bitcast_fusion
  274.8 2.8 copy.48
  277.7 1.9 copy.49
  279.6 7.7 %pad_maximum_fusion = bf16[32,288,160]{2,1,0:T(8,128)(2,1)} fusion(bf16[32,288,16]{2,1,0:T(8,128)(2,1)} %copy.49, bf16[32,16,128]{2,1,0:T(8,128)(2,1)S(1)} %collective-permute-done.5, bf16[32,256,128]{2,1,0:T(8,128)(2,1)S(1)} %maximum_convert_fusion, bf16[32,16,128]{2,1,0:T(8,128)(2,1)S(1)} %collective-permute-done.4, bf16[32,288,16]{2,1,0:T(8,128)(2,1)} %copy.48), kind=kLoop, calls=%fused_computation.24 | loop fusion | flops 14745600 | bytes 5898240 | tf_op jit(solution)/shard_map/concatenate | solution.py:21
  287.3 27.3 %constant_dynamic-slice_fusion.16 = (bf16[32,256,128]{2,1,0:T(8,128)(2,1)}, bf16[32,256,128]{2,1,0:T(8,128)(2,1)}, bf16[32,256,128]{2,1,0:T(8,128)(2,1)}, bf16[3...) fusion(bf16[32,288,160]{2,1,0:T(8,128)(2,1)} %pad_maximum_fusio, ...), kind=kLoop, calls=%fused_computation.216 | loop fusion | bytes 33554448 | tf_op jit(solution)/shard_map/dynamic_slice | solution.py:67
  314.7 3.1 fusion.69
  317.8 1.4 convolution_add_fusion.23
  320.9 1.4 convolution_add_fusion.21
  322.4 1.5 convolution_add_fusion.20
  324.0 1.4 convolution_add_fusion.19
  325.6 1.4 convolution_add_fusion.18
  327.1 1.5 convolution_add_fusion.17
  328.7 1.9 convolution_add_fusion.16
  332.7 3.3 broadcast_add_fusion
  336.1 1.9 collective-permute-start.8
  338.0 3.4 collective-permute-start.9
  344.1 4.2 collective-permute-done.9
  348.5 3.0 fusion.123
  351.4 2.8 copy.50
  354.3 2.2 copy.51
  356.5 3.0 collective-permute-start.11
  359.5 4.5 collective-permute-start.10
  364.1 7.6 %fusion.16 = bf16[32,32768]{1,0:T(8,128)(2,1)} fusion(f32[32768,32]{0,1:T(8,128)} %copy-done.2, f32[4,8,256,128]{3,2,1,0:T(8,128)} %bitcast.323, f32[32]{0:T(128)S(1)} %get-tuple-element.51, f32[32768]{0:T(1024)S(1)} %fusion.102, f32[32]{0:T(128)S(1)} %copy-done.31), kind=kLoop, calls=%fused_computation.49 | loop fusion | flops 9437184 | bytes 10617088 | tf_op jit(solution)/shard_map/convert_element_type | solution.py:76
  371.7 3.0 copy.52
  374.7 1.9 copy.53
  376.6 7.7 %pad_maximum_fusion.1 = bf16[32,288,160]{2,1,0:T(8,128)(2,1)} fusion(bf16[32,288,16]{2,1,0:T(8,128)(2,1)} %copy.53, bf16[32,16,128]{2,1,0:T(8,128)(2,1)S(1)} %collective-permute-done.9, bf16[32,256,128]{2,1,0:T(8,128)(2,1)S(1)} %get-tuple-element.45, bf16[32,16,128]{2,1,0:T(8,128)(2,1)S(1)} %collective-permute-done.8, bf16[32,288,16]{2,1,0:T(8,128)(2,1)} %copy.52), kind=kLoop, calls=%fused_computation.25 | loop fusion | flops 14745600 | bytes 5898240 | tf_op jit(solution)/shard_map/concatenate | solution.py:21
  384.2 27.8 %constant_dynamic-slice_fusion.8 = (bf16[32,256,128]{2,1,0:T(8,128)(2,1)}, bf16[32,256,128]{2,1,0:T(8,128)(2,1)}, bf16[32,256,128]{2,1,0:T(8,128)(2,1)}, bf16[32...) fusion(bf16[32,288,160]{2,1,0:T(8,128)(2,1)} %pad_maximum_fusio, ...), kind=kLoop, calls=%fused_computation.208 | loop fusion | bytes 33554448 | tf_op jit(solution)/shard_map/dynamic_slice | solution.py:67
  412.1 3.1 fusion.50
  424.7 1.5 convolution_add_fusion.9
  426.3 1.7 convolution_add_fusion.8
  431.0 1.9 collective-permute-start.12
  432.9 3.4 collective-permute-start.13
  436.7 5.5 %collective-permute-done.13 = bf16[32,16,128]{2,1,0:T(8,128)(2,1)S(1)} collective-permute-done((bf16[32,16,128]{2,1,0:T(8,128)(2,1)S(1)}, bf16[32,16,128]{2,1,0:T(8,128)(2,1)S(1)}, u32[]{:S(2)}, u32[]{:S(2)}) %collective-permute-start.13) | collective-permute-done | bytes 131104 | tf_op jit(solution)/shard_map/ppermute | solution.py:20
  442.4 2.3 fusion.122
  444.7 2.2 copy.54
  446.9 4.7 collective-permute-start.14
  451.6 1.8 copy.55
  453.4 2.0 collective-permute-start.15
  458.3 1.9 copy.56
  460.2 3.6 collective-permute-done.15
  463.8 2.8 copy.57
  466.6 7.7 %pad_maximum_fusion.2 = bf16[32,288,160]{2,1,0:T(8,128)(2,1)} fusion(bf16[32,288,16]{2,1,0:T(8,128)(2,1)} %copy.57, bf16[32,16,128]{2,1,0:T(8,128)(2,1)S(1)} %collective-permute-done.13, bf16[32,256,128]{2,1,0:T(8,128)(2,1)S(1)} %copy-done.6, bf16[32,16,128]{2,1,0:T(8,128)(2,1)S(1)} %collective-permute-done.12, bf16[32,288,16]{2,1,0:T(8,128)(2,1)} %copy.56), kind=kLoop, calls=%fused_computation.26 | loop fusion | flops 14745600 | bytes 5898240 | tf_op jit(solution)/shard_map/concatenate | solution.py:21
  474.3 27.7 %constant_dynamic-slice_fusion = (bf16[32,256,128]{2,1,0:T(8,128)(2,1)}, bf16[32,256,128]{2,1,0:T(8,128)(2,1)}, bf16[32,256,128]{2,1,0:T(8,128)(2,1)}, bf16[32,2...) fusion(bf16[32,288,160]{2,1,0:T(8,128)(2,1)} %pad_maximum_fusio, ...), kind=kLoop, calls=%fused_computation.200 | loop fusion | bytes 33554448 | tf_op jit(solution)/shard_map/dynamic_slice | solution.py:67
  502.0 3.1 fusion.33
  505.1 1.4 convolution_add_fusion.7
  515.9 1.5 convolution_add_fusion.1
  517.5 1.5 fusion.17
  519.8 2.2 fusion.2
  (126 shorter events, 39.4 us)
Async XLA Ops:
  6.5 229.2 %copy-start = (bf16[512,64]{0,1:T(8,128)(2,1)S(1)}, bf16[512,64]{0,1:T(8,128)(2,1)}, u32[]{:S(2)}) copy-start(bf16[512,64]{0,1:T(8,128)(2,1)} %param.12) | copy-start | bytes 196612
  6.5 229.2 %all-gather.2.cloned.1.call-start = ((), (), s32[]{:S(2)}) async-start(), calls=%async_computation | async-start | bytes 2113536 | tf_op jit(solution)/shard_map/all_gather | solution.py:117
  6.5 14.7 %collective-permute-start.1 = (bf16[16,512]{1,0:T(8,128)(2,1)}, bf16[16,512]{1,0:T(8,128)(2,1)S(1)}, u32[]{:S(2)}, u32[]{:S(2)}) collective-permute-start(bf16[16,512]{1,0:T(8,128)(2,1)} %param.9), channel_id=1, source_target_pairs={{1,0},{2,1},{3,2},{4,3},{5,4},{6,5},{7,6},{8,7},{9,8},{10,9},{11,1... | collective-permute-start | bytes 49160 | tf_op jit(solution)/shard_map/ppermute | solution.py:20
  9.3 11.2 %collective-permute-start = (bf16[16,512]{1,0:T(8,128)(2,1)}, bf16[16,512]{1,0:T(8,128)(2,1)S(1)}, u32[]{:S(2)}, u32[]{:S(2)}) collective-permute-start(bf16[16,512]{1,0:T(8,128)(2,1)} %param.9), channel_id=1, source_target_pairs={{0,1},{1,2},{2,3},{3,4},{4,5},{5,6},{6,7},{7,8},{8,9},{9,10},{10,1... | collective-permute-start | bytes 49160 | tf_op jit(solution)/shard_map/ppermute | solution.py:19
  23.7 214.5 %copy-start.31 = (f32[32]{0:T(128)S(1)}, f32[32]{0:T(128)}, u32[]{:S(2)}) copy-start(f32[32]{0:T(128)} %param.13) | copy-start | bytes 388
  23.7 7.7 %collective-permute-start.3 = (bf16[16,512]{1,0:T(8,128)(2,1)S(1)}, bf16[16,512]{1,0:T(8,128)(2,1)S(1)}, u32[]{:S(2)}, u32[]{:S(2)}) collective-permute-start(bf16[16,512]{1,0:T(8,128)(2,1)S(1)} %fusion.81), channel_id=1, source_target_pairs={{1,0},{2,1},{3,2},{4,3},{5,4},{6,5},{7,6},{8,7},{9,8},{10,9},{11,1... | collective-permute-start | bytes 49160 | tf_op jit(solution)/shard_map/ppermute | solution.py:20
  25.6 5.8 %collective-permute-start.2 = (bf16[16,512]{1,0:T(8,128)(2,1)S(1)}, bf16[16,512]{1,0:T(8,128)(2,1)S(1)}, u32[]{:S(2)}, u32[]{:S(2)}) collective-permute-start(bf16[16,512]{1,0:T(8,128)(2,1)S(1)} %fusion.81), channel_id=1, source_target_pairs={{0,1},{1,2},{2,3},{3,4},{4,5},{5,6},{6,7},{7,8},{8,9},{9,10},{10,1... | collective-permute-start | bytes 49160 | tf_op jit(solution)/shard_map/ppermute | solution.py:19
  239.5 6.0 %collective-permute-start.4 = (bf16[32,16,128]{2,1,0:T(8,128)(2,1)S(1)}, bf16[32,16,128]{2,1,0:T(8,128)(2,1)S(1)}, u32[]{:S(2)}, u32[]{:S(2)}) collective-permute-start(bf16[32,16,128]{2,1,0:T(8,128)(2,1)S(1)} %get-tuple-element.39), channel_id=1, source_target_pairs={{0,16},{16,32},{32,48},{48,64},{64,80},{80,96},{96,112},{1,17},{17... | collective-permute-start | bytes 393224 | tf_op jit(solution)/shard_map/ppermute | solution.py:19
  243.6 9.3 %collective-permute-start.5 = (bf16[32,16,128]{2,1,0:T(8,128)(2,1)S(1)}, bf16[32,16,128]{2,1,0:T(8,128)(2,1)S(1)}, u32[]{:S(2)}, u32[]{:S(2)}) collective-permute-start(bf16[32,16,128]{2,1,0:T(8,128)(2,1)S(1)} %get-tuple-element.40), channel_id=1, source_target_pairs={{16,0},{32,16},{48,32},{64,48},{80,64},{96,80},{112,96},{17,1},{33... | collective-permute-start | bytes 393224 | tf_op jit(solution)/shard_map/ppermute | solution.py:20
  256.1 13.3 %copy-start.32 = (f32[3,32]{1,0:T(4,128)S(1)}, f32[3,32]{1,0:T(4,128)}, u32[]{:S(2)}) copy-start(f32[3,32]{1,0:T(4,128)} %param.15) | copy-start | bytes 1156
  261.2 16.5 %collective-permute-start.7 = (bf16[32,288,16]{1,2,0:T(8,128)(2,1)S(1)}, bf16[32,288,16]{1,2,0:T(8,128)(2,1)S(1)}, u32[]{:S(2)}, u32[]{:S(2)}) collective-permute-start(bf16[32,288,16]{1,2,0:T(8,128)(2,1)S(1)} %copy.47), channel_id=1, source_target_pairs={{1,0},{2,1},{3,2},{4,3},{5,4},{6,5},{7,6},{8,7},{9,8},{10,9},{11,1... | collective-permute-start | bytes 884744 | tf_op jit(solution)/shard_map/ppermute | solution.py:20
  265.6 9.2 %collective-permute-start.6 = (bf16[32,288,16]{1,2,0:T(8,128)(2,1)}, bf16[32,288,16]{1,2,0:T(8,128)(2,1)}, u32[]{:S(2)}, u32[]{:S(2)}) collective-permute-start(bf16[32,288,16]{1,2,0:T(8,128)(2,1)} %copy.46), channel_id=1, source_target_pairs={{0,1},{1,2},{2,3},{3,4},{4,5},{5,6},{6,7},{7,8},{8,9},{9,10},{10,1... | collective-permute-start | bytes 884744 | tf_op jit(solution)/shard_map/ppermute | solution.py:19
  287.3 27.4 %copy-start.30 = (bf16[3,3,32,32]{3,2,1,0:T(8,128)(2,1)S(1)}, bf16[3,3,32,32]{3,2,1,0:T(8,128)(2,1)}, u32[]{:S(2)}) copy-start(bf16[3,3,32,32]{3,2,1,0:T(8,128)(2,1)} %get-tuple-element.42) | copy-start | bytes 55300
  314.7 3.1 copy-start.28
  317.7 1.6 copy-start.25
  319.3 1.6 copy-start.22
  322.4 1.6 copy-start.19
  324.0 1.6 copy-start.17
  325.6 1.6 copy-start.14
  327.1 1.6 copy-start.10
  330.7 2.1 copy-start.2
  336.1 8.0 %collective-permute-start.8 = (bf16[32,16,128]{2,1,0:T(8,128)(2,1)S(1)}, bf16[32,16,128]{2,1,0:T(8,128)(2,1)S(1)}, u32[]{:S(2)}, u32[]{:S(2)}) collective-permute-start(bf16[32,16,128]{2,1,0:T(8,128)(2,1)S(1)} %get-tuple-element.37), channel_id=1, source_target_pairs={{0,16},{16,32},{32,48},{48,64},{64,80},{80,96},{96,112},{1,17},{17... | collective-permute-start | bytes 393224 | tf_op jit(solution)/shard_map/ppermute | solution.py:19
  338.0 10.3 %collective-permute-start.9 = (bf16[32,16,128]{2,1,0:T(8,128)(2,1)S(1)}, bf16[32,16,128]{2,1,0:T(8,128)(2,1)S(1)}, u32[]{:S(2)}, u32[]{:S(2)}) collective-permute-start(bf16[32,16,128]{2,1,0:T(8,128)(2,1)S(1)} %get-tuple-element.38), channel_id=1, source_target_pairs={{16,0},{32,16},{48,32},{64,48},{80,64},{96,80},{112,96},{17,1},{33... | collective-permute-start | bytes 393224 | tf_op jit(solution)/shard_map/ppermute | solution.py:20
  356.5 18.2 %collective-permute-start.11 = (bf16[32,288,16]{1,2,0:T(8,128)(2,1)S(1)}, bf16[32,288,16]{1,2,0:T(8,128)(2,1)S(1)}, u32[]{:S(2)}, u32[]{:S(2)}) collective-permute-start(bf16[32,288,16]{1,2,0:T(8,128)(2,1)S(1)} %copy.51), channel_id=1, source_target_pairs={{1,0},{2,1},{3,2},{4,3},{5,4},{6,5},{7,6},{8,7},{9,8},{10,9},{11,1... | collective-permute-start | bytes 884744 | tf_op jit(solution)/shard_map/ppermute | solution.py:20
  359.5 12.2 %collective-permute-start.10 = (bf16[32,288,16]{1,2,0:T(8,128)(2,1)}, bf16[32,288,16]{1,2,0:T(8,128)(2,1)}, u32[]{:S(2)}, u32[]{:S(2)}) collective-permute-start(bf16[32,288,16]{1,2,0:T(8,128)(2,1)} %copy.50), channel_id=1, source_target_pairs={{0,1},{1,2},{2,3},{3,4},{4,5},{5,6},{6,7},{7,8},{8,9},{9,10},{10,1... | collective-permute-start | bytes 884744 | tf_op jit(solution)/shard_map/ppermute | solution.py:19
  412.1 3.1 copy-start.29
  415.2 1.6 copy-start.26
  416.8 1.6 copy-start.23
  418.3 1.6 copy-start.7
  419.9 1.6 copy-start.20
  421.5 1.6 copy-start.18
  423.1 1.6 copy-start.15
  424.7 1.6 copy-start.12
  428.0 2.0 copy-start.3
  430.9 11.3 %copy-start.5 = (bf16[32,256,128]{2,1,0:T(8,128)(2,1)}, bf16[32,256,128]{2,1,0:T(8,128)(2,1)S(1)}, u32[]{:S(2)}) copy-start(bf16[32,256,128]{2,1,0:T(8,128)(2,1)S(1)} %fusion.5) | copy-start | bytes 6291460
  431.0 5.7 %collective-permute-start.12 = (bf16[32,16,128]{2,1,0:T(8,128)(2,1)S(1)}, bf16[32,16,128]{2,1,0:T(8,128)(2,1)S(1)}, u32[]{:S(2)}, u32[]{:S(2)}) collective-permute-start(bf16[32,16,128]{2,1,0:T(8,128)(2,1)S(1)} %get-tuple-element.35), channel_id=1, source_target_pairs={{0,16},{16,32},{32,48},{48,64},{64,80},{80,96},{96,112},{1,17},{17... | collective-permute-start | bytes 393224 | tf_op jit(solution)/shard_map/ppermute | solution.py:19
  432.9 9.3 %collective-permute-start.13 = (bf16[32,16,128]{2,1,0:T(8,128)(2,1)S(1)}, bf16[32,16,128]{2,1,0:T(8,128)(2,1)S(1)}, u32[]{:S(2)}, u32[]{:S(2)}) collective-permute-start(bf16[32,16,128]{2,1,0:T(8,128)(2,1)S(1)} %get-tuple-element.36), channel_id=1, source_target_pairs={{16,0},{32,16},{48,32},{64,48},{80,64},{96,80},{112,96},{17,1},{33... | collective-permute-start | bytes 393224 | tf_op jit(solution)/shard_map/ppermute | solution.py:20
  446.9 11.4 %collective-permute-start.14 = (bf16[32,288,16]{1,2,0:T(8,128)(2,1)S(1)}, bf16[32,288,16]{1,2,0:T(8,128)(2,1)S(1)}, u32[]{:S(2)}, u32[]{:S(2)}) collective-permute-start(bf16[32,288,16]{1,2,0:T(8,128)(2,1)S(1)} %copy.54), channel_id=1, source_target_pairs={{0,1},{1,2},{2,3},{3,4},{4,5},{5,6},{6,7},{7,8},{8,9},{9,10},{10,1... | collective-permute-start | bytes 884744 | tf_op jit(solution)/shard_map/ppermute | solution.py:19
  453.4 13.2 %copy-start.6 = (bf16[32,256,128]{2,1,0:T(8,128)(2,1)S(1)}, bf16[32,256,128]{2,1,0:T(8,128)(2,1)}, u32[]{:S(2)}) copy-start(bf16[32,256,128]{2,1,0:T(8,128)(2,1)} %copy-done.5) | copy-start | bytes 6291460
  453.4 10.4 %collective-permute-start.15 = (bf16[32,288,16]{1,2,0:T(8,128)(2,1)}, bf16[32,288,16]{1,2,0:T(8,128)(2,1)}, u32[]{:S(2)}, u32[]{:S(2)}) collective-permute-start(bf16[32,288,16]{1,2,0:T(8,128)(2,1)} %copy.55), channel_id=1, source_target_pairs={{1,0},{2,1},{3,2},{4,3},{5,4},{6,5},{7,6},{8,7},{9,8},{10,9},{11,1... | collective-permute-start | bytes 884744 | tf_op jit(solution)/shard_map/ppermute | solution.py:20
  502.0 3.1 copy-start.27
  505.1 1.6 copy-start.24
  506.6 1.6 copy-start.21
  508.2 2.2 copy-start.4
  508.2 2.9 copy-start.8
  511.1 1.6 copy-start.16
  512.7 1.6 copy-start.13
  514.3 1.6 copy-start.11
  515.9 1.6 copy-start.9
  519.7 2.2 copy-start.1
Sparse Core Ops, SparseCore 0:
  34.6 201.0 all-gather.1
where the time goes:
time: 535 us; the launch traced here: 529 us
  waiting for transfers between devices  222 us (41%)
  local copies, waits for them, and re-layouts  135 us (25%)
  matrix products  53.9 us (10%)
  starting transfers between devices  52.1 us (10%)
  other arithmetic  39.7 us (7%)
  between operations  26.4 us (5%)
    all_gather x1, waiting for transfers between devices, on_device(): whole = lax.all_gather(hidden, ('rows', 'cols'), axis=0, tiled=True)  200 us
    dynamic_slice x3, local copies, waits for them, and re-layouts, conv_step(): lax.dynamic_slice(padded, (zero_index, row_start, col_start), (chans, nro...  82.8 us
    dot_general x27, matrix products, conv_step(): jnp.dot(weight_set[tap_row, tap_col], tap_slice.reshape(chans, nrow * nco...  43.6 us
    ppermute x8, starting transfers between devices, padded_2(): before = lax.ppermute(last, axis, up)  29.3 us
    concatenate x7, other arithmetic, padded_2(): value = jnp.concatenate([before, value, after], axis=dim)  23.6 us
    ppermute x8, starting transfers between devices, padded_2(): after = lax.ppermute(leading, axis, down)  22.8 us
    ppermute x8, waiting for transfers between devices, padded_2(): after = lax.ppermute(leading, axis, down)  20.7 us
    slice x9, local copies, waits for them, and re-layouts, padded_2(): last = lax.slice_in_dim(value, length - width, length, axis=dim)  16.2 us
  transfers between devices with their start and end apart: 17, of which 8 were waited for; matrix products, arithmetic and copies ran while one was open for 5% of the time, Pallas kernels for 0%

commit v1 on v0

v1 whole, which is shorter than its diff:
```python
import functools
import math

import jax
import jax.numpy as jnp
from jax import lax
from jax.experimental import pallas as pl
from jax.experimental.pallas import tpu as pltpu
from jax.sharding import PartitionSpec as P

DMAX1 = 16
DMAX2 = 16
GROUP = 6
LANES = 256
AXES = ("rows", "cols")


def position_code(bin_index, start_pos, map_width):
    half_width = map_width // 2
    position = ((start_pos + bin_index) % 8192).astype(jnp.float32)
    rates = jnp.exp(-jnp.arange(half_width).astype(jnp.float32) * (math.log(1000.0) / half_width))
    phase_angle = position[:, None] * rates[None, :]
    return jnp.concatenate([jnp.cos(phase_angle), jnp.sin(phase_angle)], axis=1)


def encode_kernel(
    total, dil, place, up2, up1, here, down1, down2, weight, bias, proj, code, out, wide, mid
):
    count = here.shape[0]
    chunks = wide.shape[0]

    def keep(ref, first, value):
        for k in range(chunks):
            ref[k, first : first + value.shape[0], :] = value[:, k * 128 : (k + 1) * 128]

    def run(ref, first, span):
        return jnp.concatenate([ref[k, pl.ds(first, span), :] for k in range(chunks)], axis=1)

    def layer(which, ref, span):
        running = jnp.zeros((span, chunks * 128), jnp.float32)
        for tap in range(3):
            rows = run(ref, count + (tap - 1) * dil[which], span).astype(jnp.bfloat16)
            running += jnp.dot(rows, weight[which, tap], preferred_element_type=jnp.float32)
        return run(ref, count, span) + jnp.maximum(running + bias[which : which + 1, :], 0.0)

    for piece, ref in enumerate((up2, up1, here, down1, down2)):
        keep(wide, piece * count, ref[...].astype(jnp.float32))
    value = layer(0, wide, 3 * count).astype(jnp.bfloat16).astype(jnp.float32)
    index = (place[0] - 1) * count + lax.broadcasted_iota(jnp.int32, value.shape, 0)
    keep(mid, 0, jnp.where((index >= 0) & (index < total), value, 0.0))
    value = layer(1, mid, count)
    parts = jnp.dot(value.astype(jnp.bfloat16), proj[...], preferred_element_type=jnp.float32)
    parts = (parts + code[...]).astype(jnp.bfloat16)
    out[...] = jnp.broadcast_to(parts[None], out.shape)


def shifted(low, high, amount, lane):
    if amount[0] == "right":
        step = amount[1]
        low, high = pltpu.roll(low, step, 1), pltpu.roll(high, step, 1)
        edge = lane < step
    else:
        step = 128 - amount[1]
        low, high = pltpu.roll(low, step, 1), pltpu.roll(high, step, 1)
        edge = lane >= step
    return jnp.where(edge, high, low), jnp.where(edge, low, high)


def pair_kernel(
    total_shards, first_dil, dil, place, parts, gain, weight, bias, out,
    row_turned, distance, field0, field1, field2, final,
):
    shard = parts.shape[1]
    chans = gain.shape[0]
    tile_rows = out.shape[1]
    margin = 3 * DMAX2
    reach = margin // shard
    row_place, col_place = place[1], place[2]
    last_row, last_col = place[3] - 1, place[4] - 1
    row_first = row_place * tile_rows
    col_first = col_place * 128
    dils = [dil[first_dil + k] for k in range(3)]

    def pieces(first, count, wrap):
        taken = []
        for k in range(count):
            step = k - count if k >= wrap else k
            taken.append(parts[jnp.clip(first + step, 0, total_shards - 1)])
        return jnp.concatenate(taken, axis=0).astype(jnp.float32)

    cols = pieces(col_first // shard, LANES // shard, LANES // shard - reach)
    col_turned = jnp.transpose(cols)[chans : 2 * chans, :]
    span0 = tile_rows + 2 * margin
    blocks = -(-span0 // 128)
    rows = pieces(row_first // shard - reach, blocks * 128 // shard, blocks * 128)
    rows = jnp.transpose(rows)[:chans, :]
    for k in range(blocks):
        row_turned[k] = rows[:, k * 128 : (k + 1) * 128]

    lane = lax.broadcasted_iota(jnp.int32, (1, LANES), 1)
    col_local = jnp.where(lane < LANES - margin - 8, lane, lane - LANES)
    row_local = lax.broadcasted_iota(jnp.int32, (span0, LANES), 0) - margin
    apart = jnp.abs(row_first + row_local - (col_first + col_local))
    distance[...] = jnp.log(1.0 + apart.astype(jnp.float32)) * 0.125

    col_glob = col_first + col_local
    inside = (col_glob >= 0) & (col_glob < total_shards * shard)
    inside_high = jnp.where(inside[:, 128:], 1.0, 0.0)
    gain_wide = jnp.broadcast_to(gain[...], (chans, LANES))

    def first_row(i, carry):
        turned = row_turned[i // 128]
        pick = jnp.full((chans, 128), i % 128, jnp.int32)
        row_term = jnp.take_along_axis(turned, pick, axis=1)
        row_term = jnp.concatenate([row_term, row_term], axis=1)
        value = row_term + col_turned + gain_wide * distance[pl.ds(i, 1), :]
        value = jnp.maximum(value, 0.0)
        field0[i, :, :128] = value[:, :128].astype(jnp.bfloat16)
        field0[i, :, 128:] = (value[:, 128:] * inside_high).astype(jnp.bfloat16)
        return carry

    def clear(field, extra):
        @pl.when(row_place == 0)
        def _():
            @pl.loop(0, extra)
            def _(i):
                field[i] = jnp.zeros(field.shape[1:], field.dtype)

        @pl.when(row_place == last_row)
        def _():
            @pl.loop(0, extra)
            def _(i):
                field[extra + tile_rows + i] = jnp.zeros(field.shape[1:], field.dtype)

    need = dils[0] + dils[1] + dils[2]
    lax.fori_loop(margin - need, margin + tile_rows + need, first_row, 0)
    clear(field0, margin)

    lane128 = lax.broadcasted_iota(jnp.int32, (GROUP * chans, 128), 1)

    def tower(layer, source, extra, need, store):
        d = dils[layer]
        span = GROUP * d
        first = extra - need
        count = tile_rows + 2 * need
        bias_wide = jnp.broadcast_to(bias[layer], (chans, 128))

        def group(start, phase):
            base = start + phase
            taps = [source[base + DMAX2 + (k - 1) * d] for k in range(GROUP + 2)]
            stack = jnp.concatenate(taps, axis=0)
            sums = jnp.dot(weight[layer], stack, preferred_element_type=jnp.float32)
            size = GROUP * chans
            left, middle, right = (sums[b * size : (b + 1) * size] for b in range(3))
            left_low, left_high = shifted(left[:, :128], left[:, 128:], ("right", d), lane128)
            right_low, right_high = shifted(right[:, :128], right[:, 128:], ("left", d), lane128)
            low = left_low + middle[:, :128] + right_low
            high = left_high + middle[:, 128:] + right_high
            for k in range(GROUP):
                at = slice(k * chans, (k + 1) * chans)
                center = taps[k + 1].astype(jnp.float32)
                one = center[:, :128] + jnp.maximum(low[at] + bias_wide, 0.0)
                two = center[:, 128:] + jnp.maximum(high[at] + bias_wide, 0.0)
                store(base + k * d, one, two)

        @pl.loop(0, (count + span - 1) // span)
        def _(block):
            start = first + jnp.minimum(block * span, count - span)

            @pl.loop(0, d)
            def _(phase):
                group(start, phase)

    def keep(field):
        def store(i, low, high):
            field[i, :, :128] = low.astype(jnp.bfloat16)
            field[i, :, 128:] = (high * inside_high).astype(jnp.bfloat16)

        return store

    def keep_last(i, low, high):
        final[pl.ds(pl.multiple_of(i * chans, chans), chans), :] = low

    tower(0, field0, 2 * DMAX2, dils[1] + dils[2], keep(field1))
    clear(field1, 2 * DMAX2)
    tower(1, field1, DMAX2, dils[2], keep(field2))
    clear(field2, DMAX2)
    tower(2, field2, 0, 0, keep_last)

    @pl.loop(0, tile_rows // 16)
    def _(block):
        first = pl.multiple_of(block * 16, 16)
        for c in range(chans):
            taken = final[pl.ds(first * chans + c, 16, stride=chans), :]
            out[c, pl.ds(first, 16), :] = taken.astype(jnp.bfloat16)


def banded(map_weight):
    layers, _, _, outs, ins = map_weight.shape
    turned = jnp.transpose(map_weight, (0, 2, 3, 1, 4)).reshape(layers, 3, outs, 3 * ins)
    rows = [
        jnp.pad(turned, ((0, 0), (0, 0), (0, 0), (k * ins, (GROUP - 1 - k) * ins)))
        for k in range(GROUP)
    ]
    return jnp.stack(rows, axis=2).reshape(layers, 3 * GROUP * outs, (GROUP + 2) * ins)


def pair_call(dilations, place, gathered, dist_gain, bands, map_bias, tile_rows, tile_cols):
    chans = dist_gain.shape[0]
    smem = pl.BlockSpec(memory_space=pltpu.SMEM)
    vmem = pl.BlockSpec(memory_space=pltpu.VMEM)
    span = tile_rows + 6 * DMAX2
    return pl.pallas_call(
        functools.partial(pair_kernel, gathered.shape[0], dilations.shape[0] - 3),
        out_shape=jax.ShapeDtypeStruct((chans, tile_rows, tile_cols), jnp.bfloat16),
        in_specs=[smem] * 2 + [vmem] * 4,
        out_specs=vmem,
        scratch_shapes=[
            pltpu.VMEM((-(-span // 128), chans, 128), jnp.float32),
            pltpu.VMEM((span, LANES), jnp.float32),
            pltpu.VMEM((span, chans, LANES), jnp.bfloat16),
            pltpu.VMEM((span - 2 * DMAX2, chans, LANES), jnp.bfloat16),
            pltpu.VMEM((span - 4 * DMAX2, chans, LANES), jnp.bfloat16),
            pltpu.VMEM((tile_rows * chans, 128), jnp.float32),
        ],
        compiler_params=pltpu.CompilerParams(vmem_limit_bytes=48 * 2**20),
        cost_estimate=pl.CostEstimate(
            flops=3 * 2 * tile_rows * 9 * chans * chans * LANES,
            bytes_accessed=tile_rows * tile_cols * chans * 2,
            transcendentals=0,
        ),
        name="pair_tower",
    )(
        dilations, place, gathered, dist_gain.reshape(chans, 1), bands,
        map_bias.reshape(-1, chans, 1),
    )


def on_device(
    features,
    tower_weight,
    tower_bias,
    pair_proj,
    dist_gain,
    map_weight,
    map_bias,
    dilations,
    start_bin,
):
    row_count = lax.axis_size("rows")
    col_count = lax.axis_size("cols")
    shards = row_count * col_count
    shard, width = features.shape
    total = shard * shards
    tile_rows = total // row_count
    tile_cols = total // col_count
    chans = map_weight.shape[-1]
    row_place = lax.axis_index("rows")
    col_place = lax.axis_index("cols")
    mine = row_place * col_count + col_place
    place = jnp.stack(
        [mine, row_place, col_place, jnp.int32(row_count), jnp.int32(col_count)]
    ).astype(jnp.int32)

    def moved(step):
        pairs = [(i, i + step) for i in range(shards) if 0 <= i + step < shards]
        return lax.ppermute(features, AXES, pairs)

    up2, up1, down1, down2 = moved(2), moved(1), moved(-1), moved(-2)
    code = position_code(mine * shard + jnp.arange(shard), start_bin[0], chans)
    code = jnp.pad(code, ((0, 0), (0, chans)))
    bands = banded(map_weight)

    smem = pl.BlockSpec(memory_space=pltpu.SMEM)
    vmem = pl.BlockSpec(memory_space=pltpu.VMEM)
    parts = pl.pallas_call(
        functools.partial(encode_kernel, total),
        out_shape=jax.ShapeDtypeStruct((shards, shard, 2 * chans), jnp.bfloat16),
        in_specs=[smem] * 2 + [vmem] * 9,
        out_specs=vmem,
        scratch_shapes=[
            pltpu.VMEM((width // 128, 5 * shard, 128), jnp.float32),
            pltpu.VMEM((width // 128, 3 * shard, 128), jnp.float32),
        ],
        compiler_params=pltpu.CompilerParams(vmem_limit_bytes=24 * 2**20),
        cost_estimate=pl.CostEstimate(
            flops=2 * 4 * shard * 3 * width * width,
            bytes_accessed=6 * width * width * 2,
            transcendentals=0,
        ),
        name="encode",
    )(
        dilations, place, up2, up1, features, down1, down2,
        tower_weight, tower_bias, pair_proj, code,
    )

    gathered = lax.all_to_all(parts, AXES, split_axis=0, concat_axis=0, tiled=True)

    return pair_call(
        dilations, place, gathered, dist_gain, bands, map_bias, tile_rows, tile_cols
    )


def solution(mesh):
    placed = (P(AXES, None), P(), P(), P(), P(), P(), P(), P(), P())
    return jax.shard_map(
        on_device, mesh=mesh, in_specs=placed, out_specs=P(None, "rows", "cols"), check_vma=False
    )
```

time: 535 us -> 134 us (0.25)
  the two profiles are of different devices: /device:TPU:27 before, /device:TPU:1 now
where the time goes in v1:
time: 134 us
  Pallas kernels  86.2 us (64%)
  starting transfers between devices  27.7 us (21%)
  waiting for transfers between devices  10.5 us (8%)
  local copies, waits for them, and re-layouts  8.3 us (6%)
    pallas_call x1, Pallas kernels, pair_call(): pl.pallas_call(functools.partial(pair_kernel, gathered.shape[0], dilation...  84.8 us
    all_to_all x1, starting transfers between devices, on_device(): lax.all_to_all(parts, AXES, split_axis=0, concat_axis=0, tiled=True)  16 us
    ppermute x4, starting transfers between devices, moved(): return lax.ppermute(features, AXES, pairs)  11.7 us
    all_to_all x1, waiting for transfers between devices, on_device(): lax.all_to_all(parts, AXES, split_axis=0, concat_axis=0, tiled=True)  10.5 us
    unnamed x22, local copies, waits for them, and re-layouts  6.62 us
  transfers between devices with their start and end apart: 5, of which 1 were waited for; matrix products, arithmetic and copies ran while one was open for 2% of the time, Pallas kernels for 0%

profile of v1, /device:TPU:1, one launch (start us, length us, event | category | flops | bytes accessed | tf_op | source)
XLA Modules:
  0.0 133.8 jit_solution(9286588262131036879)
XLA Ops:
  0.0 3.3 %collective-permute-start.2 = (bf16[16,512]{1,0:T(8,128)(2,1)}, bf16[16,512]{1,0:T(8,128)(2,1)S(1)}, u32[]{:S(2)}, u32[]{:S(2)}) collective-permute-start(bf16[16,512]{1,0:T(8,128)(2,1)} %here.1), channel_id=1, source_target_pairs={{1,0},{2,1},{3,2},{4,3},{5,4},{6,5},{7,6},{8,7},{9,8},{10,9},{11,1... | collective-permute-start | bytes 49160 | tf_op jit(solution)/shard_map/ppermute | solution.py:267
  3.3 3.1 %collective-permute-start.1 = (bf16[16,512]{1,0:T(8,128)(2,1)}, bf16[16,512]{1,0:T(8,128)(2,1)S(1)}, u32[]{:S(2)}, u32[]{:S(2)}) collective-permute-start(bf16[16,512]{1,0:T(8,128)(2,1)} %here.1), channel_id=1, source_target_pairs={{0,1},{1,2},{2,3},{3,4},{4,5},{5,6},{6,7},{7,8},{8,9},{9,10},{10,1... | collective-permute-start | bytes 49160 | tf_op jit(solution)/shard_map/ppermute | solution.py:267
  6.4 4.0 %collective-permute-start = (bf16[16,512]{1,0:T(8,128)(2,1)}, bf16[16,512]{1,0:T(8,128)(2,1)S(1)}, u32[]{:S(2)}, u32[]{:S(2)}) collective-permute-start(bf16[16,512]{1,0:T(8,128)(2,1)} %here.1), channel_id=1, source_target_pairs={{0,2},{1,3},{2,4},{3,5},{4,6},{5,7},{6,8},{7,9},{8,10},{9,11},{10,... | collective-permute-start | bytes 49160 | tf_op jit(solution)/shard_map/ppermute | solution.py:267
  10.4 1.3 collective-permute-start.3
  12.4 1.1 copy.19
  13.5 0.2 reshape.37
  13.7 0.0 copy-start.6
  13.7 0.0 copy-start.5
  13.7 0.1 bitcast_dynamic-update-slice_fusion.4
  13.8 0.1 bitcast_dynamic-update-slice_fusion.3
  14.0 0.1 multiply_cosine_fusion
  14.1 0.1 select_maximum_fusion.code
  14.2 1.0 copy.18.proj
  15.1 0.1 stack.36.place
  15.2 0.0 collective-permute-done.2.down1
  15.2 0.0 collective-permute-done.1.up1
  15.2 0.0 collective-permute-done.up2
  15.2 0.0 collective-permute-done.3.down2
  15.2 0.0 copy-start
  15.3 1.9 %copy-done = bf16[2,3,512,512]{3,2,1,0:T(8,128)(2,1)S(1)} copy-done((bf16[2,3,512,512]{3,2,1,0:T(8,128)(2,1)S(1)}, bf16[2,3,512,512]{3,2,1,0:T(8,128)(2,1)}, u32[]{:S(2)}) %copy-start) | copy-done | bytes 3145752
  17.1 0.0 copy-start.1
  17.1 0.7 copy-done.1
  17.9 0.0 copy-start.2
  17.9 0.7 copy-done.2
  18.5 0.0 copy-start.3
  18.5 0.7 copy-done.3
  19.2 1.4 %encode.1 = bf16[128,16,64]{2,1,0:T(8,128)(2,1)S(1)} custom-call(s32[5]{0:T(128)S(1)} %copy-done.3, s32[5]{0:T(128)S(1)} %stack.36.place, bf16[16,512]{1,0:T(8,128)(2,1)S(1)} %collective-permute-done.up2, bf16[16,512]{1,0:T(8,128)(2,1)S(1)} %collective-permute-done.1.up1, bf16[16,512]{1,0:T(8,128)(2,1)S(1)} %copy-done.1, ...), custom_call_target="tpu_custom_call" | custom-call | flops 100663296 | bytes 3145728 | tf_op jit(solution)/shard_map/encode/pallas_call | solution.py:276
  20.6 0.0 copy-start.4
  20.6 1.0 reshape.40
  21.6 16.0 %all-to-all-start = ((bf16[128,2,512]{2,1,0:T(2,128)(2,1)}), bf16[128,2,512]{2,1,0:T(2,128)(2,1)S(1)}, u32[]{:S(2)}, u32[]{:S(2)}) async-start(bf16[128,2,512]{2,1,0:T(2,128)(2,1)} %reshape.40), calls=%async_computation | async-start | bytes 524288 | tf_op jit(solution)/shard_map/all_to_all | solution.py:297
  37.7 0.1 bitcast_dynamic-update-slice_fusion.2
  37.8 0.0 copy-done.6
  37.8 0.1 copy.21.gain
  37.9 0.0 copy-done.5
  37.9 0.1 copy.22.bias
  38.0 0.1 bitcast_dynamic-update-slice_fusion
  38.1 0.1 copy.20
  38.2 10.5 %all-to-all-done = bf16[128,2,512]{2,1,0:T(2,128)(2,1)S(1)} async-done(((bf16[128,2,512]{2,1,0:T(2,128)(2,1)}), bf16[128,2,512]{2,1,0:T(2,128)(2,1)S(1)}, u32[]{:S(2)}, u32[]{:S(2)}) %all-to-all-start) | async-done | bytes 262176 | tf_op jit(solution)/shard_map/all_to_all | solution.py:297
  48.6 0.3 reshape.41.parts
  49.0 0.0 copy-done.4
  49.0 84.8 %pair_tower.1 = bf16[32,256,128]{2,1,0:T(8,128)(2,1)} custom-call(s32[5]{0:T(128)S(1)} %copy-done.4, s32[5]{0:T(128)S(1)} %stack.36.place, bf16[128,16,64]{2,1,0:T(8,128)(2,1)S(1)} %reshape.41.parts, f32[32,1]{1,0:T(8,128)S(1)} %copy.21.gain, bf16[3,576,256]{2,1,0:T(8,128)(2,1)S(1)} %bitcast.21, f32[3,32,1]{2,1,0:T(8,128)S(1)} %copy.22.bias), custom_call_target="tpu_custom_call" | custom-call | flops 3623878656 | bytes 2097152 | tf_op jit(solution)/shard_map/pair_tower/pallas_call | solution.py:213
  (4 shorter events, 0.1 us)
Async XLA Ops:
  0.0 15.2 %collective-permute-start.2 = (bf16[16,512]{1,0:T(8,128)(2,1)}, bf16[16,512]{1,0:T(8,128)(2,1)S(1)}, u32[]{:S(2)}, u32[]{:S(2)}) collective-permute-start(bf16[16,512]{1,0:T(8,128)(2,1)} %here.1), channel_id=1, source_target_pairs={{1,0},{2,1},{3,2},{4,3},{5,4},{6,5},{7,6},{8,7},{9,8},{10,9},{11,1... | collective-permute-start | bytes 49160 | tf_op jit(solution)/shard_map/ppermute | solution.py:267
  3.3 11.9 %collective-permute-start.1 = (bf16[16,512]{1,0:T(8,128)(2,1)}, bf16[16,512]{1,0:T(8,128)(2,1)S(1)}, u32[]{:S(2)}, u32[]{:S(2)}) collective-permute-start(bf16[16,512]{1,0:T(8,128)(2,1)} %here.1), channel_id=1, source_target_pairs={{0,1},{1,2},{2,3},{3,4},{4,5},{5,6},{6,7},{7,8},{8,9},{9,10},{10,1... | collective-permute-start | bytes 49160 | tf_op jit(solution)/shard_map/ppermute | solution.py:267
  6.4 8.8 %collective-permute-start = (bf16[16,512]{1,0:T(8,128)(2,1)}, bf16[16,512]{1,0:T(8,128)(2,1)S(1)}, u32[]{:S(2)}, u32[]{:S(2)}) collective-permute-start(bf16[16,512]{1,0:T(8,128)(2,1)} %here.1), channel_id=1, source_target_pairs={{0,2},{1,3},{2,4},{3,5},{4,6},{5,7},{6,8},{7,9},{8,10},{9,11},{10,... | collective-permute-start | bytes 49160 | tf_op jit(solution)/shard_map/ppermute | solution.py:267
  10.4 4.8 %collective-permute-start.3 = (bf16[16,512]{1,0:T(8,128)(2,1)}, bf16[16,512]{1,0:T(8,128)(2,1)S(1)}, u32[]{:S(2)}, u32[]{:S(2)}) collective-permute-start(bf16[16,512]{1,0:T(8,128)(2,1)} %here.1), channel_id=1, source_target_pairs={{2,0},{3,1},{4,2},{5,3},{6,4},{7,5},{8,6},{9,7},{10,8},{11,9},{12,... | collective-permute-start | bytes 49160 | tf_op jit(solution)/shard_map/ppermute | solution.py:267
  13.7 24.1 %copy-start.6 = (f32[32]{0:T(128)S(1)}, f32[32]{0:T(128)}, u32[]{:S(2)}) copy-start(f32[32]{0:T(128)} %param.13) | copy-start | bytes 388
  13.7 24.2 %copy-start.5 = (f32[3,32]{1,0:T(4,128)S(1)}, f32[3,32]{1,0:T(4,128)}, u32[]{:S(2)}) copy-start(f32[3,32]{1,0:T(4,128)} %param.15) | copy-start | bytes 1156
  15.2 1.9 %copy-start = (bf16[2,3,512,512]{3,2,1,0:T(8,128)(2,1)S(1)}, bf16[2,3,512,512]{3,2,1,0:T(8,128)(2,1)}, u32[]{:S(2)}) copy-start(bf16[2,3,512,512]{3,2,1,0:T(8,128)(2,1)} %weight.1) | copy-start | bytes 9437188
  17.1 0.7 copy-start.1
  17.9 0.7 copy-start.2
  18.5 0.7 copy-start.3
  20.6 28.4 %copy-start.4 = (s32[5]{0:T(128)S(1)}, s32[5]{0:T(128)}, u32[]{:S(2)}) copy-start(s32[5]{0:T(128)} %dil.3) | copy-start | bytes 64
  21.6 27.0 %all-to-all-start = ((bf16[128,2,512]{2,1,0:T(2,128)(2,1)}), bf16[128,2,512]{2,1,0:T(2,128)(2,1)S(1)}, u32[]{:S(2)}, u32[]{:S(2)}) async-start(bf16[128,2,512]{2,1,0:T(2,128)(2,1)} %reshape.40), calls=%async_computation | async-start | bytes 524288 | tf_op jit(solution)/shard_map/all_to_all | solution.py:297

commit v2 on v1

v2 whole, which is shorter than its diff:
```python
import functools
import math

import jax
import jax.numpy as jnp
from jax import lax
from jax.experimental import pallas as pl
from jax.experimental.pallas import tpu as pltpu
from jax.sharding import PartitionSpec as P

DMAX1 = 16
DMAX2 = 16
GROUP = 3
TAIL = 32
WIDE = 2
UNROLL = 2
LANES = 256
AXES = ("rows", "cols")


def position_code(bin_index, start_pos, map_width):
    half_width = map_width // 2
    position = ((start_pos + bin_index) % 8192).astype(jnp.float32)
    rates = jnp.exp(-jnp.arange(half_width).astype(jnp.float32) * (math.log(1000.0) / half_width))
    phase_angle = position[:, None] * rates[None, :]
    return jnp.concatenate([jnp.cos(phase_angle), jnp.sin(phase_angle)], axis=1)


def encode_kernel(
    total, place, up2, up1, down1, down2, code, near, weight_far, out,
    weight, wide, mid, arrived,
):
    count = up1.shape[0]
    bias = near[count : count + 2, :]
    proj = near[count + 2 :, :].astype(jnp.bfloat16)
    fetch = [
        [
            pltpu.make_async_copy(
                weight_far.at[which, tap], weight.at[which, tap], arrived.at[which, tap]
            )
            for tap in range(3)
        ]
        for which in range(2)
    ]
    for copy in fetch[0] + fetch[1]:
        copy.start()
    chunks = wide.shape[0]

    def keep(ref, first, value):
        for k in range(chunks):
            ref[k, first : first + value.shape[0], :] = value[:, k * 128 : (k + 1) * 128]

    def run(ref, first, span):
        return jnp.concatenate([ref[k, pl.ds(first, span), :] for k in range(chunks)], axis=1)

    def layer(which, ref, span):
        running = jnp.zeros((span, chunks * 128), jnp.float32)
        for tap in range(3):
            rows = run(ref, count + (tap - 1) * place[5 + which], span).astype(jnp.bfloat16)
            fetch[which][tap].wait()
            running += jnp.dot(rows, weight[which, tap], preferred_element_type=jnp.float32)
        return run(ref, count, span) + jnp.maximum(running + bias[which : which + 1, :], 0.0)

    for piece, ref in enumerate((up2, up1, near, down1, down2)):
        keep(wide, piece * count, ref[:count, :].astype(jnp.float32))
    value = layer(0, wide, 3 * count).astype(jnp.bfloat16).astype(jnp.float32)
    index = (place[0] - 1) * count + lax.broadcasted_iota(jnp.int32, value.shape, 0)
    keep(mid, 0, jnp.where((index >= 0) & (index < total), value, 0.0))
    value = layer(1, mid, count)
    parts = lax.dot_general(
        value.astype(jnp.bfloat16),
        proj,
        (((1,), (1,)), ((), ())),
        preferred_element_type=jnp.float32,
    )
    parts = (parts + code[...]).astype(jnp.bfloat16)
    parts = jnp.concatenate([parts[: count // 2], parts[count // 2 :]], axis=1)
    out[...] = jnp.broadcast_to(parts[None], out.shape)


def pair_kernel(
    total_shards, first_dil, place, parts, gain, weight, out,
    row_turned, distance, field_a, field_b, final,
):
    shard = 2 * parts.shape[1]
    chans = gain.shape[0]
    tile_rows = out.shape[1]
    margin = 3 * DMAX2
    reach = margin // shard
    row_place, col_place = place[1], place[2]
    last_row = place[3] - 1
    row_first = row_place * tile_rows
    col_first = col_place * 128
    dils = [place[first_dil + k] for k in range(3)]

    def pieces(first, count, wrap):
        taken = []
        for k in range(count):
            step = k - count if k >= wrap else k
            both = parts[jnp.clip(first + step, 0, total_shards - 1)]
            taken += [both[:, : 2 * chans], both[:, 2 * chans :]]
        return jnp.concatenate(taken, axis=0).astype(jnp.float32)

    cols = pieces(col_first // shard, LANES // shard, LANES // shard - reach)
    col_turned = jnp.transpose(cols)[chans : 2 * chans, :]
    span0 = tile_rows + 2 * margin
    blocks = -(-span0 // 128)
    rows = pieces(row_first // shard - reach, blocks * 128 // shard, blocks * 128)
    rows = jnp.transpose(rows)[:chans, :]
    for k in range(blocks):
        row_turned[k] = rows[:, k * 128 : (k + 1) * 128]

    lane = lax.broadcasted_iota(jnp.int32, (1, LANES), 1)
    col_local = jnp.where(lane < LANES - margin - 8, lane, lane - LANES)
    row_local = lax.broadcasted_iota(jnp.int32, (span0, LANES), 0) - margin
    apart = jnp.abs(row_first + row_local - (col_first + col_local))
    distance[...] = jnp.log(1.0 + apart.astype(jnp.float32)) * 0.125

    col_glob = col_first + col_local
    inside = (col_glob >= 0) & (col_glob < total_shards * shard)
    inside_high = jnp.where(inside[:, 128:], 1.0, 0.0)
    inside_high = jnp.broadcast_to(inside_high, (chans, 128)).astype(jnp.bfloat16)
    gain_wide = jnp.broadcast_to(gain[...], (chans, LANES))
    lane16 = lax.broadcasted_iota(jnp.int16, (chans, 128), 1)

    def keep(field, d):
        back = 128 - d
        at_left = lane16 < d.astype(jnp.int16)
        at_right = lane16 >= back.astype(jnp.int16)

        def store(i, low, high):
            low = low.astype(jnp.bfloat16)
            high = high.astype(jnp.bfloat16) * inside_high
            field[i, chans : 2 * chans, :128] = low
            field[i, chans : 2 * chans, 128:] = high
            turned_low, turned_high = pltpu.roll(low, d, 1), pltpu.roll(high, d, 1)
            field[i, :chans, :128] = jnp.where(at_left, turned_high, turned_low)
            field[i, :chans, 128:] = jnp.where(at_left, turned_low, turned_high)
            turned_low, turned_high = pltpu.roll(low, back, 1), pltpu.roll(high, back, 1)
            field[i, 2 * chans :, :128] = jnp.where(at_right, turned_high, turned_low)
            field[i, 2 * chans :, 128:] = jnp.where(at_right, turned_low, turned_high)

        return store

    def clear(field, extra):
        @pl.when(row_place == 0)
        def _():
            @pl.loop(0, extra)
            def _(i):
                field[i] = jnp.zeros(field.shape[1:], field.dtype)

        @pl.when(row_place == last_row)
        def _():
            @pl.loop(0, extra)
            def _(i):
                field[extra + tile_rows + i] = jnp.zeros(field.shape[1:], field.dtype)

    need = dils[0] + dils[1] + dils[2]
    store_first = keep(field_a, dils[0])
    first, last = margin - need, margin + tile_rows + need

    @pl.loop(0, (last - first + 3) // 4)
    def _(block):
        for k in range(4):
            i = jnp.minimum(first + block * 4 + k, last - 1)
            pick = jnp.full((chans, 128), i % 128, jnp.int32)
            row_term = jnp.take_along_axis(row_turned[i // 128], pick, axis=1)
            row_term = jnp.concatenate([row_term, row_term], axis=1)
            value = row_term + col_turned + gain_wide * distance[pl.ds(i, 1), :]
            value = jnp.maximum(value, 0.0)
            store_first(i, value[:, :128], value[:, 128:])

    clear(field_a, margin)

    tail = jnp.ones((TAIL, WIDE * LANES), jnp.bfloat16)

    def tower(layer, source, extra, need, store):
        d = dils[layer]
        span = GROUP * d
        first = extra - need
        count = tile_rows + 2 * need
        final_layer = layer == 2

        def groups(bases):
            width = 128 if final_layer else LANES
            taps = []
            for k in range(GROUP + 2):
                at = [base + DMAX2 + (k - 1) * d for base in bases]
                taps.append(jnp.concatenate([source[i, :, :width] for i in at], axis=1))
            stack = jnp.concatenate(taps + [tail], axis=0)
            sums = jnp.dot(weight[layer], stack, preferred_element_type=jnp.float32)
            for n, base in enumerate(bases):
                for k in range(GROUP):
                    at = slice(n * width, (n + 1) * width)
                    center = taps[k + 1][chans : 2 * chans, at].astype(jnp.float32)
                    value = center + jnp.maximum(sums[k * chans : (k + 1) * chans, at], 0.0)
                    if final_layer:
                        store(base + k * d, value)
                    else:
                        store(base + k * d, value[:, :128], value[:, 128:])

        each = WIDE * (2 if final_layer else 1)
        total = (count + span - 1) // span * d

        @functools.partial(
            lax.fori_loop, 0, (total + UNROLL * each - 1) // (UNROLL * each),
            init_val=(jnp.int32(0), jnp.int32(0)),
        )
        def _(step, carry):
            start, phase = carry
            bases = []
            for _ in range(UNROLL * each):
                bases.append(first + jnp.minimum(start, count - span) + phase)
                wrap = phase + 1 >= d
                start = jnp.where(wrap, start + span, start)
                phase = jnp.where(wrap, 0, phase + 1)
            for k in range(UNROLL):
                groups(bases[k * each : (k + 1) * each])
            return start, phase

    def keep_last(i, low):
        final[pl.ds(pl.multiple_of(i * chans, chans), chans), :] = low

    tower(0, field_a, 2 * DMAX2, dils[1] + dils[2], keep(field_b, dils[1]))
    clear(field_b, 2 * DMAX2)
    tower(1, field_b, DMAX2, dils[2], keep(field_a, dils[2]))
    clear(field_a, DMAX2)
    tower(2, field_a, 0, 0, keep_last)

    @pl.loop(0, tile_rows // 16)
    def _(block):
        first = pl.multiple_of(block * 16, 16)
        for c in range(chans):
            taken = final[pl.ds(first * chans + c, 16, stride=chans), :]
            out[c, pl.ds(first, 16), :] = taken.astype(jnp.bfloat16)


def banded(map_weight, map_bias):
    layers, _, _, outs, ins = map_weight.shape
    taps = jnp.transpose(map_weight, (0, 3, 1, 2, 4)).reshape(layers, outs, 9 * ins)
    left = map_bias
    split = []
    for _ in range(3):
        split.append(lax.reduce_precision(left, 8, 7))
        left = left - split[-1]
    split = jnp.stack(split, axis=2).astype(jnp.bfloat16)
    rows = []
    for k in range(GROUP):
        before, after = k * 3 * ins, (GROUP - 1 - k) * 3 * ins
        row = jnp.pad(taps, ((0, 0), (0, 0), (before, after)))
        rows.append(jnp.concatenate([row, jnp.pad(split, ((0, 0), (0, 0), (0, TAIL - 3)))], axis=2))
    return jnp.concatenate(rows, axis=1)


def pair_call(place, gathered, dist_gain, bands, tile_rows, tile_cols):
    chans = dist_gain.shape[0]
    smem = pl.BlockSpec(memory_space=pltpu.SMEM)
    vmem = pl.BlockSpec(memory_space=pltpu.VMEM)
    span = tile_rows + 6 * DMAX2
    return pl.pallas_call(
        functools.partial(pair_kernel, gathered.shape[0], place.shape[0] - 3),
        out_shape=jax.ShapeDtypeStruct((chans, tile_rows, tile_cols), jnp.bfloat16),
        in_specs=[smem] + [vmem] * 3,
        out_specs=vmem,
        scratch_shapes=[
            pltpu.VMEM((-(-span // 128), chans, 128), jnp.float32),
            pltpu.VMEM((span, LANES), jnp.float32),
            pltpu.VMEM((span, 3 * chans, LANES), jnp.bfloat16),
            pltpu.VMEM((span - 2 * DMAX2, 3 * chans, LANES), jnp.bfloat16),
            pltpu.VMEM((tile_rows * chans, 128), jnp.float32),
        ],
        compiler_params=pltpu.CompilerParams(vmem_limit_bytes=48 * 2**20),
        cost_estimate=pl.CostEstimate(
            flops=3 * 2 * tile_rows * 9 * chans * chans * LANES,
            bytes_accessed=tile_rows * tile_cols * chans * 2,
            transcendentals=0,
        ),
        name="pair_tower",
    )(
        place, gathered, dist_gain.reshape(chans, 1), bands,
    )


def on_device(
    features,
    tower_weight,
    tower_bias,
    pair_proj,
    dist_gain,
    map_weight,
    map_bias,
    dilations,
    start_bin,
):
    row_count = lax.axis_size("rows")
    col_count = lax.axis_size("cols")
    shards = row_count * col_count
    shard, width = features.shape
    total = shard * shards
    tile_rows = total // row_count
    tile_cols = total // col_count
    chans = map_weight.shape[-1]
    row_place = lax.axis_index("rows")
    col_place = lax.axis_index("cols")
    mine = row_place * col_count + col_place
    place = jnp.stack([mine, row_place, col_place, row_count, col_count]).astype(jnp.int32)
    place = jnp.concatenate([place, dilations])

    def moved(step):
        pairs = [(i, i + step) for i in range(shards) if 0 <= i + step < shards]
        return lax.ppermute(features, AXES, pairs)

    up2, up1, down1, down2 = moved(2), moved(1), moved(-1), moved(-2)
    code = position_code(mine * shard + jnp.arange(shard), start_bin[0], chans)
    code = jnp.pad(code, ((0, 0), (0, chans)))
    near = [features.astype(jnp.float32), tower_bias, pair_proj.T.astype(jnp.float32)]
    near = jnp.concatenate(near, axis=0)
    bands = banded(map_weight, map_bias)

    smem = pl.BlockSpec(memory_space=pltpu.SMEM)
    vmem = pl.BlockSpec(memory_space=pltpu.VMEM)
    parts = pl.pallas_call(
        functools.partial(encode_kernel, total),
        out_shape=jax.ShapeDtypeStruct((shards, shard // 2, 4 * chans), jnp.bfloat16),
        in_specs=[smem] + [vmem] * 6 + [pl.BlockSpec(memory_space=pltpu.HBM)],
        out_specs=vmem,
        scratch_shapes=[
            pltpu.VMEM(tower_weight.shape, tower_weight.dtype),
            pltpu.VMEM((width // 128, 5 * shard, 128), jnp.float32),
            pltpu.VMEM((width // 128, 3 * shard, 128), jnp.float32),
            pltpu.SemaphoreType.DMA(tower_weight.shape[:2]),
        ],
        compiler_params=pltpu.CompilerParams(vmem_limit_bytes=52 * 2**20),
        cost_estimate=pl.CostEstimate(
            flops=2 * 4 * shard * 3 * width * width,
            bytes_accessed=6 * width * width * 2,
            transcendentals=0,
        ),
        name="encode",
    )(
        place, up2, up1, down1, down2, code, near, tower_weight,
    )

    gathered = lax.all_to_all(parts, AXES, split_axis=0, concat_axis=0, tiled=True)
    return pair_call(
        place, gathered, dist_gain, bands, tile_rows, tile_cols
    )


def solution(mesh):
    placed = (P(AXES, None), P(), P(), P(), P(), P(), P(), P(), P())
    return jax.shard_map(
        on_device, mesh=mesh, in_specs=placed, out_specs=P(None, "rows", "cols"), check_vma=False
    )
```

time: 134 us -> 94.6 us (0.71)
  Pallas kernels: 86.2 us -> 50.9 us
  local copies, waits for them, and re-layouts: 8.3 us -> 1.52 us
  other arithmetic: 0.22 us -> 2.73 us
    pallas_call x1, Pallas kernels: 84.8 us -> 47.3 us  [pair_call(): pl.pallas_call(functools.partial(pair_kernel, gathered.shape[0], place.sh...]
    unnamed x22 -> x6, local copies, waits for them, and re-layouts: 6.62 us -> 0.01 us
    pallas_call x1, Pallas kernels: 1.4 us -> 3.54 us  [on_device(): pl.pallas_call(functools.partial(encode_kernel, total), out_shape=jax.Sha...]
    convert_element_type x0 -> x2, other arithmetic: none -> 1.58 us  [the longest x1 0.85 us: on_device(): pair_proj.T.astype(jnp.float32)]
  transfers between devices with their start and end apart: 5 -> 5, of which waited for: 1 -> 1; matrix products, arithmetic and copies ran while one was open for 2% -> 5% of each run, Pallas kernels for 0% -> 0%
where the time goes in v2:
time: 94.6 us; the launch traced here: 93.3 us
  Pallas kernels  50.9 us (54%)
  starting transfers between devices  27.5 us (29%)
  waiting for transfers between devices  9.92 us (10%)
  other arithmetic  2.73 us (3%)
  local copies, waits for them, and re-layouts  1.52 us (2%)
    pallas_call x1, Pallas kernels, pair_call(): pl.pallas_call(functools.partial(pair_kernel, gathered.shape[0], place.sh...  47.3 us
    all_to_all x1, starting transfers between devices, on_device(): lax.all_to_all(parts, AXES, split_axis=0, concat_axis=0, tiled=True)  15.6 us
    ppermute x4, starting transfers between devices, moved(): return lax.ppermute(features, AXES, pairs)  11.8 us
    all_to_all x1, waiting for transfers between devices, on_device(): lax.all_to_all(parts, AXES, split_axis=0, concat_axis=0, tiled=True)  9.9 us
    pallas_call x1, Pallas kernels, on_device(): pl.pallas_call(functools.partial(encode_kernel, total), out_shape=jax.Sha...  3.54 us
  transfers between devices with their start and end apart: 5, of which 1 were waited for; matrix products, arithmetic and copies ran while one was open for 5% of the time, Pallas kernels for 0%

profile of v2, /device:TPU:1, one launch (start us, length us, event | category | flops | bytes accessed | tf_op | source)
XLA Modules:
  0.0 93.3 jit_solution(1126888807670322453)
XLA Ops:
  0.0 0.0 copy-start.1
  0.0 0.0 copy-start.2
  0.0 0.0 copy-start
  0.0 3.4 %collective-permute-start.2 = (bf16[16,512]{1,0:T(8,128)(2,1)}, bf16[16,512]{1,0:T(8,128)(2,1)S(1)}, u32[]{:S(2)}, u32[]{:S(2)}) collective-permute-start(bf16[16,512]{1,0:T(8,128)(2,1)} %param.9), channel_id=1, source_target_pairs={{1,0},{2,1},{3,2},{4,3},{5,4},{6,5},{7,6},{8,7},{9,8},{10,9},{11,1... | collective-permute-start | bytes 49160 | tf_op jit(solution)/shard_map/ppermute | solution.py:311
  3.5 3.1 %collective-permute-start.1 = (bf16[16,512]{1,0:T(8,128)(2,1)}, bf16[16,512]{1,0:T(8,128)(2,1)S(1)}, u32[]{:S(2)}, u32[]{:S(2)}) collective-permute-start(bf16[16,512]{1,0:T(8,128)(2,1)} %param.9), channel_id=1, source_target_pairs={{0,1},{1,2},{2,3},{3,4},{4,5},{5,6},{6,7},{7,8},{8,9},{9,10},{10,1... | collective-permute-start | bytes 49160 | tf_op jit(solution)/shard_map/ppermute | solution.py:311
  6.6 4.0 %collective-permute-start = (bf16[16,512]{1,0:T(8,128)(2,1)}, bf16[16,512]{1,0:T(8,128)(2,1)S(1)}, u32[]{:S(2)}, u32[]{:S(2)}) collective-permute-start(bf16[16,512]{1,0:T(8,128)(2,1)} %param.9), channel_id=1, source_target_pairs={{0,2},{1,3},{2,4},{3,5},{4,6},{5,7},{6,8},{7,9},{8,10},{9,11},{10,... | collective-permute-start | bytes 49160 | tf_op jit(solution)/shard_map/ppermute | solution.py:311
  10.6 1.3 %collective-permute-start.3 = (bf16[16,512]{1,0:T(8,128)(2,1)}, bf16[16,512]{1,0:T(8,128)(2,1)S(1)}, u32[]{:S(2)}, u32[]{:S(2)}) collective-permute-start(bf16[16,512]{1,0:T(8,128)(2,1)} %param.9), channel_id=1, source_target_pairs={{2,0},{3,1},{4,2},{5,3},{6,4},{7,5},{8,6},{9,7},{10,8},{11,9},{12,... | collective-permute-start | bytes 49160 | tf_op jit(solution)/shard_map/ppermute | solution.py:311
  11.9 0.7 convert_element_type.38
  13.3 0.9 convert_bitcast_fusion
  14.1 0.1 multiply_cosine_fusion
  14.3 0.7 pad_maximum_fusion.near
  15.0 0.1 select_maximum_fusion.code
  15.1 0.7 concatenate.21.place
  15.8 0.0 collective-permute-done.2.down1
  15.8 0.0 collective-permute-done.1.up1
  15.8 0.0 collective-permute-done.up2
  15.8 0.0 collective-permute-done.3.down2
  15.8 3.5 %encode.1 = bf16[128,8,128]{2,1,0:T(8,128)(2,1)} custom-call(s32[10]{0:T(128)S(1)} %concatenate.21.place, bf16[16,512]{1,0:T(8,128)(2,1)S(1)} %collective-permute-done.up2, bf16[16,512]{1,0:T(8,128)(2,1)S(1)} %collective-permute-done.1.up1, bf16[16,512]{1,0:T(8,128)(2,1)S(1)} %collective-permute-done.2.down1, ...), custom_call_target="tpu_custom_call" | custom-call | flops 100663296 | bytes 3145728 | tf_op jit(solution)/shard_map/encode/pallas_call | solution.py:322
  19.4 15.6 %all-to-all-start = ((bf16[128,8,128]{2,1,0:T(8,128)(2,1)}), bf16[128,8,128]{2,1,0:T(8,128)(2,1)S(1)}, u32[]{:S(2)}, u32[]{:S(2)}) async-start(bf16[128,8,128]{2,1,0:T(8,128)(2,1)} %encode.1), calls=%async_computation | async-start | bytes 524288 | tf_op jit(solution)/shard_map/all_to_all | solution.py:344
  35.0 0.0 copy-done.1
  35.0 0.0 copy-done.2
  35.0 0.1 copy.30.gain
  35.1 0.1 copy.27
  35.2 0.1 copy.29
  35.4 0.1 copy.28
  35.5 0.0 copy-done
  35.5 0.2 copy.26
  35.6 0.2 reshape.31
  35.8 0.1 fusion.19
  35.9 0.1 fusion.12.weight
  36.1 9.9 %all-to-all-done.parts = bf16[128,8,128]{2,1,0:T(8,128)(2,1)S(1)} async-done(((bf16[128,8,128]{2,1,0:T(8,128)(2,1)}), bf16[128,8,128]{2,1,0:T(8,128)(2,1)S(1)}, u32[]{:S(2)}, u32[]{:S(2)}) %all-to-all-start) | async-done | bytes 262176 | tf_op jit(solution)/shard_map/all_to_all | solution.py:344
  46.0 47.3 %pair_tower.1 = bf16[32,256,128]{2,1,0:T(8,128)(2,1)} custom-call(s32[10]{0:T(128)S(1)} %concatenate.21.place, bf16[128,8,128]{2,1,0:T(8,128)(2,1)S(1)} %all-to-all-done.parts, f32[32,1]{1,0:T(8,128)S(1)} %copy.30.gain, bf16[3,96,512]{2,1,0:T(8,128)(2,1)S(1)} %fusion.12.weight), custom_call_target="tpu_custom_call" | custom-call | flops 3623878656 | bytes 2097152 | tf_op jit(solution)/shard_map/pair_tower/pallas_call | solution.py:260
  (3 shorter events, 0.0 us)
Async XLA Ops:
  0.0 35.0 %copy-start.1 = (f32[3,32]{1,0:T(4,128)S(1)}, f32[3,32]{1,0:T(4,128)}, u32[]{:S(2)}) copy-start(f32[3,32]{1,0:T(4,128)} %param.15) | copy-start | bytes 1156
  0.0 35.0 %copy-start.2 = (f32[32]{0:T(128)S(1)}, f32[32]{0:T(128)}, u32[]{:S(2)}) copy-start(f32[32]{0:T(128)} %param.13) | copy-start | bytes 388
  0.0 35.5 %copy-start = (bf16[3,3,3,32,32]{4,3,2,1,0:T(8,128)(2,1)S(1)}, bf16[3,3,3,32,32]{4,3,2,1,0:T(8,128)(2,1)}, u32[]{:S(2)}) copy-start(bf16[3,3,3,32,32]{4,3,2,1,0:T(8,128)(2,1)} %param.14) | copy-start | bytes 165892
  0.0 15.8 %collective-permute-start.2 = (bf16[16,512]{1,0:T(8,128)(2,1)}, bf16[16,512]{1,0:T(8,128)(2,1)S(1)}, u32[]{:S(2)}, u32[]{:S(2)}) collective-permute-start(bf16[16,512]{1,0:T(8,128)(2,1)} %param.9), channel_id=1, source_target_pairs={{1,0},{2,1},{3,2},{4,3},{5,4},{6,5},{7,6},{8,7},{9,8},{10,9},{11,1... | collective-permute-start | bytes 49160 | tf_op jit(solution)/shard_map/ppermute | solution.py:311
  3.5 12.3 %collective-permute-start.1 = (bf16[16,512]{1,0:T(8,128)(2,1)}, bf16[16,512]{1,0:T(8,128)(2,1)S(1)}, u32[]{:S(2)}, u32[]{:S(2)}) collective-permute-start(bf16[16,512]{1,0:T(8,128)(2,1)} %param.9), channel_id=1, source_target_pairs={{0,1},{1,2},{2,3},{3,4},{4,5},{5,6},{6,7},{7,8},{8,9},{9,10},{10,1... | collective-permute-start | bytes 49160 | tf_op jit(solution)/shard_map/ppermute | solution.py:311
  6.6 9.2 %collective-permute-start = (bf16[16,512]{1,0:T(8,128)(2,1)}, bf16[16,512]{1,0:T(8,128)(2,1)S(1)}, u32[]{:S(2)}, u32[]{:S(2)}) collective-permute-start(bf16[16,512]{1,0:T(8,128)(2,1)} %param.9), channel_id=1, source_target_pairs={{0,2},{1,3},{2,4},{3,5},{4,6},{5,7},{6,8},{7,9},{8,10},{9,11},{10,... | collective-permute-start | bytes 49160 | tf_op jit(solution)/shard_map/ppermute | solution.py:311
  10.6 5.2 %collective-permute-start.3 = (bf16[16,512]{1,0:T(8,128)(2,1)}, bf16[16,512]{1,0:T(8,128)(2,1)S(1)}, u32[]{:S(2)}, u32[]{:S(2)}) collective-permute-start(bf16[16,512]{1,0:T(8,128)(2,1)} %param.9), channel_id=1, source_target_pairs={{2,0},{3,1},{4,2},{5,3},{6,4},{7,5},{8,6},{9,7},{10,8},{11,9},{12,... | collective-permute-start | bytes 49160 | tf_op jit(solution)/shard_map/ppermute | solution.py:311
  19.4 26.6 %all-to-all-start = ((bf16[128,8,128]{2,1,0:T(8,128)(2,1)}), bf16[128,8,128]{2,1,0:T(8,128)(2,1)S(1)}, u32[]{:S(2)}, u32[]{:S(2)}) async-start(bf16[128,8,128]{2,1,0:T(8,128)(2,1)} %encode.1), calls=%async_computation | async-start | bytes 524288 | tf_op jit(solution)/shard_map/all_to_all | solution.py:344

commit v3 on v2

--- a/solution.py
+++ b/solution.py
@@ -12,8 +12,8 @@
 DMAX2 = 16
 GROUP = 3
 TAIL = 32
-WIDE = 2
-UNROLL = 2
+WIDE = 4
+UNROLL = 1
 LANES = 256
 AXES = ("rows", "cols")
 

time: 94.6 us -> 93.7 us (level); the launches traced: 93.3 us -> 93.8 us
  no operation moved by 1% of the time
where the time goes in v3:
time: 93.7 us; the launch traced here: 93.8 us
  Pallas kernels  51.3 us (55%)
  starting transfers between devices  27.5 us (29%)
  waiting for transfers between devices  9.92 us (11%)
  other arithmetic  2.73 us (3%)
  local copies, waits for them, and re-layouts  1.52 us (2%)
    pallas_call x1, Pallas kernels, pair_call(): pl.pallas_call(functools.partial(pair_kernel, gathered.shape[0], place.sh...  47.8 us
    all_to_all x1, starting transfers between devices, on_device(): lax.all_to_all(parts, AXES, split_axis=0, concat_axis=0, tiled=True)  15.6 us
    ppermute x4, starting transfers between devices, moved(): return lax.ppermute(features, AXES, pairs)  11.8 us
    all_to_all x1, waiting for transfers between devices, on_device(): lax.all_to_all(parts, AXES, split_axis=0, concat_axis=0, tiled=True)  9.9 us
    pallas_call x1, Pallas kernels, on_device(): pl.pallas_call(functools.partial(encode_kernel, total), out_shape=jax.Sha...  3.54 us
  transfers between devices with their start and end apart: 5, of which 1 were waited for; matrix products, arithmetic and copies ran while one was open for 5% of the time, Pallas kernels for 0%

profile of v3, /device:TPU:1, one launch (start us, length us, event | category | flops | bytes accessed | tf_op | source)
XLA Modules:
  0.0 93.8 jit_solution(17447303378096973323)
XLA Ops:
  0.0 0.0 copy-start.1
  0.0 0.0 copy-start.2
  0.0 0.0 copy-start
  0.0 3.4 %collective-permute-start.2 = (bf16[16,512]{1,0:T(8,128)(2,1)}, bf16[16,512]{1,0:T(8,128)(2,1)S(1)}, u32[]{:S(2)}, u32[]{:S(2)}) collective-permute-start(bf16[16,512]{1,0:T(8,128)(2,1)} %param.9), channel_id=1, source_target_pairs={{1,0},{2,1},{3,2},{4,3},{5,4},{6,5},{7,6},{8,7},{9,8},{10,9},{11,1... | collective-permute-start | bytes 49160 | tf_op jit(solution)/shard_map/ppermute | solution.py:311
  3.5 3.1 %collective-permute-start.1 = (bf16[16,512]{1,0:T(8,128)(2,1)}, bf16[16,512]{1,0:T(8,128)(2,1)S(1)}, u32[]{:S(2)}, u32[]{:S(2)}) collective-permute-start(bf16[16,512]{1,0:T(8,128)(2,1)} %param.9), channel_id=1, source_target_pairs={{0,1},{1,2},{2,3},{3,4},{4,5},{5,6},{6,7},{7,8},{8,9},{9,10},{10,1... | collective-permute-start | bytes 49160 | tf_op jit(solution)/shard_map/ppermute | solution.py:311
  6.6 4.0 %collective-permute-start = (bf16[16,512]{1,0:T(8,128)(2,1)}, bf16[16,512]{1,0:T(8,128)(2,1)S(1)}, u32[]{:S(2)}, u32[]{:S(2)}) collective-permute-start(bf16[16,512]{1,0:T(8,128)(2,1)} %param.9), channel_id=1, source_target_pairs={{0,2},{1,3},{2,4},{3,5},{4,6},{5,7},{6,8},{7,9},{8,10},{9,11},{10,... | collective-permute-start | bytes 49160 | tf_op jit(solution)/shard_map/ppermute | solution.py:311
  10.6 1.3 %collective-permute-start.3 = (bf16[16,512]{1,0:T(8,128)(2,1)}, bf16[16,512]{1,0:T(8,128)(2,1)S(1)}, u32[]{:S(2)}, u32[]{:S(2)}) collective-permute-start(bf16[16,512]{1,0:T(8,128)(2,1)} %param.9), channel_id=1, source_target_pairs={{2,0},{3,1},{4,2},{5,3},{6,4},{7,5},{8,6},{9,7},{10,8},{11,9},{12,... | collective-permute-start | bytes 49160 | tf_op jit(solution)/shard_map/ppermute | solution.py:311
  11.9 0.7 convert_element_type.38
  13.3 0.9 convert_bitcast_fusion
  14.1 0.1 multiply_cosine_fusion
  14.3 0.7 pad_maximum_fusion.near
  15.0 0.1 select_maximum_fusion.code
  15.1 0.7 concatenate.21.place
  15.8 0.0 collective-permute-done.2.down1
  15.8 0.0 collective-permute-done.1.up1
  15.8 0.0 collective-permute-done.up2
  15.8 0.0 collective-permute-done.3.down2
  15.8 3.5 %encode.1 = bf16[128,8,128]{2,1,0:T(8,128)(2,1)} custom-call(s32[10]{0:T(128)S(1)} %concatenate.21.place, bf16[16,512]{1,0:T(8,128)(2,1)S(1)} %collective-permute-done.up2, bf16[16,512]{1,0:T(8,128)(2,1)S(1)} %collective-permute-done.1.up1, bf16[16,512]{1,0:T(8,128)(2,1)S(1)} %collective-permute-done.2.down1, ...), custom_call_target="tpu_custom_call" | custom-call | flops 100663296 | bytes 3145728 | tf_op jit(solution)/shard_map/encode/pallas_call | solution.py:322
  19.4 15.6 %all-to-all-start = ((bf16[128,8,128]{2,1,0:T(8,128)(2,1)}), bf16[128,8,128]{2,1,0:T(8,128)(2,1)S(1)}, u32[]{:S(2)}, u32[]{:S(2)}) async-start(bf16[128,8,128]{2,1,0:T(8,128)(2,1)} %encode.1), calls=%async_computation | async-start | bytes 524288 | tf_op jit(solution)/shard_map/all_to_all | solution.py:344
  35.0 0.0 copy-done.1
  35.0 0.0 copy-done.2
  35.0 0.1 copy.30.gain
  35.1 0.1 copy.27
  35.2 0.1 copy.29
  35.4 0.1 copy.28
  35.5 0.0 copy-done
  35.5 0.2 copy.26
  35.6 0.2 reshape.31
  35.8 0.1 fusion.19
  35.9 0.1 fusion.12.weight
  36.1 9.9 %all-to-all-done.parts = bf16[128,8,128]{2,1,0:T(8,128)(2,1)S(1)} async-done(((bf16[128,8,128]{2,1,0:T(8,128)(2,1)}), bf16[128,8,128]{2,1,0:T(8,128)(2,1)S(1)}, u32[]{:S(2)}, u32[]{:S(2)}) %all-to-all-start) | async-done | bytes 262176 | tf_op jit(solution)/shard_map/all_to_all | solution.py:344
  46.0 47.8 %pair_tower.1 = bf16[32,256,128]{2,1,0:T(8,128)(2,1)} custom-call(s32[10]{0:T(128)S(1)} %concatenate.21.place, bf16[128,8,128]{2,1,0:T(8,128)(2,1)S(1)} %all-to-all-done.parts, f32[32,1]{1,0:T(8,128)S(1)} %copy.30.gain, bf16[3,96,512]{2,1,0:T(8,128)(2,1)S(1)} %fusion.12.weight), custom_call_target="tpu_custom_call" | custom-call | flops 3623878656 | bytes 2097152 | tf_op jit(solution)/shard_map/pair_tower/pallas_call | solution.py:260
  (3 shorter events, 0.0 us)
Async XLA Ops:
  0.0 35.0 %copy-start.1 = (f32[3,32]{1,0:T(4,128)S(1)}, f32[3,32]{1,0:T(4,128)}, u32[]{:S(2)}) copy-start(f32[3,32]{1,0:T(4,128)} %param.15) | copy-start | bytes 1156
  0.0 35.0 %copy-start.2 = (f32[32]{0:T(128)S(1)}, f32[32]{0:T(128)}, u32[]{:S(2)}) copy-start(f32[32]{0:T(128)} %param.13) | copy-start | bytes 388
  0.0 35.5 %copy-start = (bf16[3,3,3,32,32]{4,3,2,1,0:T(8,128)(2,1)S(1)}, bf16[3,3,3,32,32]{4,3,2,1,0:T(8,128)(2,1)}, u32[]{:S(2)}) copy-start(bf16[3,3,3,32,32]{4,3,2,1,0:T(8,128)(2,1)} %param.14) | copy-start | bytes 165892
  0.0 15.8 %collective-permute-start.2 = (bf16[16,512]{1,0:T(8,128)(2,1)}, bf16[16,512]{1,0:T(8,128)(2,1)S(1)}, u32[]{:S(2)}, u32[]{:S(2)}) collective-permute-start(bf16[16,512]{1,0:T(8,128)(2,1)} %param.9), channel_id=1, source_target_pairs={{1,0},{2,1},{3,2},{4,3},{5,4},{6,5},{7,6},{8,7},{9,8},{10,9},{11,1... | collective-permute-start | bytes 49160 | tf_op jit(solution)/shard_map/ppermute | solution.py:311
  3.5 12.3 %collective-permute-start.1 = (bf16[16,512]{1,0:T(8,128)(2,1)}, bf16[16,512]{1,0:T(8,128)(2,1)S(1)}, u32[]{:S(2)}, u32[]{:S(2)}) collective-permute-start(bf16[16,512]{1,0:T(8,128)(2,1)} %param.9), channel_id=1, source_target_pairs={{0,1},{1,2},{2,3},{3,4},{4,5},{5,6},{6,7},{7,8},{8,9},{9,10},{10,1... | collective-permute-start | bytes 49160 | tf_op jit(solution)/shard_map/ppermute | solution.py:311
  6.6 9.2 %collective-permute-start = (bf16[16,512]{1,0:T(8,128)(2,1)}, bf16[16,512]{1,0:T(8,128)(2,1)S(1)}, u32[]{:S(2)}, u32[]{:S(2)}) collective-permute-start(bf16[16,512]{1,0:T(8,128)(2,1)} %param.9), channel_id=1, source_target_pairs={{0,2},{1,3},{2,4},{3,5},{4,6},{5,7},{6,8},{7,9},{8,10},{9,11},{10,... | collective-permute-start | bytes 49160 | tf_op jit(solution)/shard_map/ppermute | solution.py:311
  10.6 5.2 %collective-permute-start.3 = (bf16[16,512]{1,0:T(8,128)(2,1)}, bf16[16,512]{1,0:T(8,128)(2,1)S(1)}, u32[]{:S(2)}, u32[]{:S(2)}) collective-permute-start(bf16[16,512]{1,0:T(8,128)(2,1)} %param.9), channel_id=1, source_target_pairs={{2,0},{3,1},{4,2},{5,3},{6,4},{7,5},{8,6},{9,7},{10,8},{11,9},{12,... | collective-permute-start | bytes 49160 | tf_op jit(solution)/shard_map/ppermute | solution.py:311
  19.4 26.6 %all-to-all-start = ((bf16[128,8,128]{2,1,0:T(8,128)(2,1)}), bf16[128,8,128]{2,1,0:T(8,128)(2,1)S(1)}, u32[]{:S(2)}, u32[]{:S(2)}) async-start(bf16[128,8,128]{2,1,0:T(8,128)(2,1)} %encode.1), calls=%async_computation | async-start | bytes 524288 | tf_op jit(solution)/shard_map/all_to_all | solution.py:344

commit v4 on v2

--- a/solution.py
+++ b/solution.py
@@ -13,7 +13,7 @@
 GROUP = 3
 TAIL = 32
 WIDE = 2
-UNROLL = 2
+UNROLL = 4
 LANES = 256
 AXES = ("rows", "cols")
 

time: 94.6 us -> 83.9 us (0.89)
  Pallas kernels: 50.9 us -> 40.4 us
    pallas_call x1, Pallas kernels: 47.3 us -> 36.8 us  [pair_call(): pl.pallas_call(functools.partial(pair_kernel, gathered.shape[0], place.sh...]
where the time goes in v4:
time: 83.9 us; the launch traced here: 82.8 us
  Pallas kernels  40.4 us (48%)
  starting transfers between devices  27.5 us (33%)
  waiting for transfers between devices  9.92 us (12%)
  other arithmetic  2.73 us (3%)
  local copies, waits for them, and re-layouts  1.52 us (2%)
    pallas_call x1, Pallas kernels, pair_call(): pl.pallas_call(functools.partial(pair_kernel, gathered.shape[0], place.sh...  36.8 us
    all_to_all x1, starting transfers between devices, on_device(): lax.all_to_all(parts, AXES, split_axis=0, concat_axis=0, tiled=True)  15.6 us
    ppermute x4, starting transfers between devices, moved(): return lax.ppermute(features, AXES, pairs)  11.8 us
    all_to_all x1, waiting for transfers between devices, on_device(): lax.all_to_all(parts, AXES, split_axis=0, concat_axis=0, tiled=True)  9.9 us
    pallas_call x1, Pallas kernels, on_device(): pl.pallas_call(functools.partial(encode_kernel, total), out_shape=jax.Sha...  3.54 us
  transfers between devices with their start and end apart: 5, of which 1 were waited for; matrix products, arithmetic and copies ran while one was open for 5% of the time, Pallas kernels for 0%

profile of v4, /device:TPU:1, one launch (start us, length us, event | category | flops | bytes accessed | tf_op | source)
XLA Modules:
  0.0 82.8 jit_solution(8685791979975084871)
XLA Ops:
  0.0 0.0 copy-start.1
  0.0 0.0 copy-start.2
  0.0 0.0 copy-start
  0.0 3.4 %collective-permute-start.2 = (bf16[16,512]{1,0:T(8,128)(2,1)}, bf16[16,512]{1,0:T(8,128)(2,1)S(1)}, u32[]{:S(2)}, u32[]{:S(2)}) collective-permute-start(bf16[16,512]{1,0:T(8,128)(2,1)} %param.9), channel_id=1, source_target_pairs={{1,0},{2,1},{3,2},{4,3},{5,4},{6,5},{7,6},{8,7},{9,8},{10,9},{11,1... | collective-permute-start | bytes 49160 | tf_op jit(solution)/shard_map/ppermute | solution.py:311
  3.5 3.1 %collective-permute-start.1 = (bf16[16,512]{1,0:T(8,128)(2,1)}, bf16[16,512]{1,0:T(8,128)(2,1)S(1)}, u32[]{:S(2)}, u32[]{:S(2)}) collective-permute-start(bf16[16,512]{1,0:T(8,128)(2,1)} %param.9), channel_id=1, source_target_pairs={{0,1},{1,2},{2,3},{3,4},{4,5},{5,6},{6,7},{7,8},{8,9},{9,10},{10,1... | collective-permute-start | bytes 49160 | tf_op jit(solution)/shard_map/ppermute | solution.py:311
  6.6 4.0 %collective-permute-start = (bf16[16,512]{1,0:T(8,128)(2,1)}, bf16[16,512]{1,0:T(8,128)(2,1)S(1)}, u32[]{:S(2)}, u32[]{:S(2)}) collective-permute-start(bf16[16,512]{1,0:T(8,128)(2,1)} %param.9), channel_id=1, source_target_pairs={{0,2},{1,3},{2,4},{3,5},{4,6},{5,7},{6,8},{7,9},{8,10},{9,11},{10,... | collective-permute-start | bytes 49160 | tf_op jit(solution)/shard_map/ppermute | solution.py:311
  10.6 1.3 %collective-permute-start.3 = (bf16[16,512]{1,0:T(8,128)(2,1)}, bf16[16,512]{1,0:T(8,128)(2,1)S(1)}, u32[]{:S(2)}, u32[]{:S(2)}) collective-permute-start(bf16[16,512]{1,0:T(8,128)(2,1)} %param.9), channel_id=1, source_target_pairs={{2,0},{3,1},{4,2},{5,3},{6,4},{7,5},{8,6},{9,7},{10,8},{11,9},{12,... | collective-permute-start | bytes 49160 | tf_op jit(solution)/shard_map/ppermute | solution.py:311
  11.9 0.7 convert_element_type.38
  13.3 0.9 %convert_bitcast_fusion = f32[64,512]{1,0:T(8,128)S(1)} fusion(bf16[512,64]{0,1:T(8,128)(2,1)} %param.12), kind=kLoop, calls=%fused_computation.21 | loop fusion | flops 32768 | bytes 196608 | tf_op jit(solution)/shard_map/convert_element_type | solution.py:316
  14.1 0.1 multiply_cosine_fusion
  14.3 0.7 pad_maximum_fusion.near
  15.0 0.1 select_maximum_fusion.code
  15.1 0.7 concatenate.21.place
  15.8 0.0 collective-permute-done.2.down1
  15.8 0.0 collective-permute-done.1.up1
  15.8 0.0 collective-permute-done.up2
  15.8 0.0 collective-permute-done.3.down2
  15.8 3.5 %encode.1 = bf16[128,8,128]{2,1,0:T(8,128)(2,1)} custom-call(s32[10]{0:T(128)S(1)} %concatenate.21.place, bf16[16,512]{1,0:T(8,128)(2,1)S(1)} %collective-permute-done.up2, bf16[16,512]{1,0:T(8,128)(2,1)S(1)} %collective-permute-done.1.up1, bf16[16,512]{1,0:T(8,128)(2,1)S(1)} %collective-permute-done.2.down1, ...), custom_call_target="tpu_custom_call" | custom-call | flops 100663296 | bytes 3145728 | tf_op jit(solution)/shard_map/encode/pallas_call | solution.py:322
  19.4 15.6 %all-to-all-start = ((bf16[128,8,128]{2,1,0:T(8,128)(2,1)}), bf16[128,8,128]{2,1,0:T(8,128)(2,1)S(1)}, u32[]{:S(2)}, u32[]{:S(2)}) async-start(bf16[128,8,128]{2,1,0:T(8,128)(2,1)} %encode.1), calls=%async_computation | async-start | bytes 524288 | tf_op jit(solution)/shard_map/all_to_all | solution.py:344
  35.0 0.0 copy-done.1
  35.0 0.0 copy-done.2
  35.0 0.1 copy.30.gain
  35.1 0.1 copy.27
  35.2 0.1 copy.29
  35.4 0.1 copy.28
  35.5 0.0 copy-done
  35.5 0.2 copy.26
  35.6 0.2 reshape.31
  35.8 0.1 fusion.19
  35.9 0.1 fusion.12.weight
  36.1 9.9 %all-to-all-done.parts = bf16[128,8,128]{2,1,0:T(8,128)(2,1)S(1)} async-done(((bf16[128,8,128]{2,1,0:T(8,128)(2,1)}), bf16[128,8,128]{2,1,0:T(8,128)(2,1)S(1)}, u32[]{:S(2)}, u32[]{:S(2)}) %all-to-all-start) | async-done | bytes 262176 | tf_op jit(solution)/shard_map/all_to_all | solution.py:344
  46.0 36.8 %pair_tower.1 = bf16[32,256,128]{2,1,0:T(8,128)(2,1)} custom-call(s32[10]{0:T(128)S(1)} %concatenate.21.place, bf16[128,8,128]{2,1,0:T(8,128)(2,1)S(1)} %all-to-all-done.parts, f32[32,1]{1,0:T(8,128)S(1)} %copy.30.gain, bf16[3,96,512]{2,1,0:T(8,128)(2,1)S(1)} %fusion.12.weight), custom_call_target="tpu_custom_call" | custom-call | flops 3623878656 | bytes 2097152 | tf_op jit(solution)/shard_map/pair_tower/pallas_call | solution.py:260
  (3 shorter events, 0.0 us)
Async XLA Ops:
  0.0 35.0 %copy-start.1 = (f32[3,32]{1,0:T(4,128)S(1)}, f32[3,32]{1,0:T(4,128)}, u32[]{:S(2)}) copy-start(f32[3,32]{1,0:T(4,128)} %param.15) | copy-start | bytes 1156
  0.0 35.0 %copy-start.2 = (f32[32]{0:T(128)S(1)}, f32[32]{0:T(128)}, u32[]{:S(2)}) copy-start(f32[32]{0:T(128)} %param.13) | copy-start | bytes 388
  0.0 35.5 %copy-start = (bf16[3,3,3,32,32]{4,3,2,1,0:T(8,128)(2,1)S(1)}, bf16[3,3,3,32,32]{4,3,2,1,0:T(8,128)(2,1)}, u32[]{:S(2)}) copy-start(bf16[3,3,3,32,32]{4,3,2,1,0:T(8,128)(2,1)} %param.14) | copy-start | bytes 165892
  0.0 15.8 %collective-permute-start.2 = (bf16[16,512]{1,0:T(8,128)(2,1)}, bf16[16,512]{1,0:T(8,128)(2,1)S(1)}, u32[]{:S(2)}, u32[]{:S(2)}) collective-permute-start(bf16[16,512]{1,0:T(8,128)(2,1)} %param.9), channel_id=1, source_target_pairs={{1,0},{2,1},{3,2},{4,3},{5,4},{6,5},{7,6},{8,7},{9,8},{10,9},{11,1... | collective-permute-start | bytes 49160 | tf_op jit(solution)/shard_map/ppermute | solution.py:311
  3.5 12.3 %collective-permute-start.1 = (bf16[16,512]{1,0:T(8,128)(2,1)}, bf16[16,512]{1,0:T(8,128)(2,1)S(1)}, u32[]{:S(2)}, u32[]{:S(2)}) collective-permute-start(bf16[16,512]{1,0:T(8,128)(2,1)} %param.9), channel_id=1, source_target_pairs={{0,1},{1,2},{2,3},{3,4},{4,5},{5,6},{6,7},{7,8},{8,9},{9,10},{10,1... | collective-permute-start | bytes 49160 | tf_op jit(solution)/shard_map/ppermute | solution.py:311
  6.6 9.2 %collective-permute-start = (bf16[16,512]{1,0:T(8,128)(2,1)}, bf16[16,512]{1,0:T(8,128)(2,1)S(1)}, u32[]{:S(2)}, u32[]{:S(2)}) collective-permute-start(bf16[16,512]{1,0:T(8,128)(2,1)} %param.9), channel_id=1, source_target_pairs={{0,2},{1,3},{2,4},{3,5},{4,6},{5,7},{6,8},{7,9},{8,10},{9,11},{10,... | collective-permute-start | bytes 49160 | tf_op jit(solution)/shard_map/ppermute | solution.py:311
  10.6 5.2 %collective-permute-start.3 = (bf16[16,512]{1,0:T(8,128)(2,1)}, bf16[16,512]{1,0:T(8,128)(2,1)S(1)}, u32[]{:S(2)}, u32[]{:S(2)}) collective-permute-start(bf16[16,512]{1,0:T(8,128)(2,1)} %param.9), channel_id=1, source_target_pairs={{2,0},{3,1},{4,2},{5,3},{6,4},{7,5},{8,6},{9,7},{10,8},{11,9},{12,... | collective-permute-start | bytes 49160 | tf_op jit(solution)/shard_map/ppermute | solution.py:311
  19.4 26.6 %all-to-all-start = ((bf16[128,8,128]{2,1,0:T(8,128)(2,1)}), bf16[128,8,128]{2,1,0:T(8,128)(2,1)S(1)}, u32[]{:S(2)}, u32[]{:S(2)}) async-start(bf16[128,8,128]{2,1,0:T(8,128)(2,1)} %encode.1), calls=%async_computation | async-start | bytes 524288 | tf_op jit(solution)/shard_map/all_to_all | solution.py:344

commit v5 on v4

--- a/solution.py
+++ b/solution.py
@@ -15,6 +15,8 @@
 WIDE = 2
 UNROLL = 4
 LANES = 256
+PITCH = 40
+OUTSIDE = -1e30
 AXES = ("rows", "cols")
 
 
@@ -27,12 +29,15 @@
 
 
 def encode_kernel(
-    total, place, up2, up1, down1, down2, code, near, weight_far, out,
-    weight, wide, mid, arrived,
+    total, place, up2_far, up1_far, here_far, down1_far, down2_far, bias_far, proj_far, code_far,
+    weight_far, out, window, bias, proj, code, weight, wide, mid, near_done, arrived,
 ):
-    count = up1.shape[0]
-    bias = near[count : count + 2, :]
-    proj = near[count + 2 :, :].astype(jnp.bfloat16)
+    count = here_far.shape[0]
+    pieces = [(far, window.at[k]) for k, far in enumerate((up2_far, up1_far, here_far, down1_far, down2_far))]
+    pieces += [(bias_far, bias), (proj_far, proj), (code_far, code)]
+    near = [
+        pltpu.make_async_copy(far, here, near_done.at[k]) for k, (far, here) in enumerate(pieces)
+    ]
     fetch = [
         [
             pltpu.make_async_copy(
@@ -42,8 +47,10 @@
         ]
         for which in range(2)
     ]
-    for copy in fetch[0] + fetch[1]:
+    for copy in near + fetch[0] + fetch[1]:
         copy.start()
+    for copy in near:
+        copy.wait()
     chunks = wide.shape[0]
 
     def keep(ref, first, value):
@@ -61,15 +68,15 @@
             running += jnp.dot(rows, weight[which, tap], preferred_element_type=jnp.float32)
         return run(ref, count, span) + jnp.maximum(running + bias[which : which + 1, :], 0.0)
 
-    for piece, ref in enumerate((up2, up1, near, down1, down2)):
-        keep(wide, piece * count, ref[:count, :].astype(jnp.float32))
+    for piece in range(5):
+        keep(wide, piece * count, window[piece].astype(jnp.float32))
     value = layer(0, wide, 3 * count).astype(jnp.bfloat16).astype(jnp.float32)
     index = (place[0] - 1) * count + lax.broadcasted_iota(jnp.int32, value.shape, 0)
     keep(mid, 0, jnp.where((index >= 0) & (index < total), value, 0.0))
     value = layer(1, mid, count)
     parts = lax.dot_general(
         value.astype(jnp.bfloat16),
-        proj,
+        proj[...],
         (((1,), (1,)), ((), ())),
         preferred_element_type=jnp.float32,
     )
@@ -80,7 +87,7 @@
 
 def pair_kernel(
     total_shards, first_dil, place, parts, gain, weight, out,
-    row_turned, distance, field_a, field_b, final,
+    row_turned, distance, field_a, field_b, final, held,
 ):
     shard = 2 * parts.shape[1]
     chans = gain.shape[0]
@@ -101,36 +108,41 @@
             taken += [both[:, : 2 * chans], both[:, 2 * chans :]]
         return jnp.concatenate(taken, axis=0).astype(jnp.float32)
 
+    lane = lax.broadcasted_iota(jnp.int32, (1, LANES), 1)
+    col_local = jnp.where(lane < LANES - margin - 8, lane, lane - LANES)
+    col_glob = col_first + col_local
+    inside = (col_glob >= 0) & (col_glob < total_shards * shard)
+    inside_high = jnp.where(inside[:, 128:], 1.0, 0.0)
+    inside_high = jnp.broadcast_to(inside_high, (chans, 128)).astype(jnp.bfloat16)
+
     cols = pieces(col_first // shard, LANES // shard, LANES // shard - reach)
     col_turned = jnp.transpose(cols)[chans : 2 * chans, :]
+    col_turned = jnp.where(inside, col_turned, OUTSIDE)
     span0 = tile_rows + 2 * margin
     blocks = -(-span0 // 128)
     rows = pieces(row_first // shard - reach, blocks * 128 // shard, blocks * 128)
     rows = jnp.transpose(rows)[:chans, :]
+    row_glob = row_first - margin + lax.broadcasted_iota(jnp.int32, (1, blocks * 128), 1)
+    rows = jnp.where((row_glob >= 0) & (row_glob < total_shards * shard), rows, OUTSIDE)
     for k in range(blocks):
         row_turned[k] = rows[:, k * 128 : (k + 1) * 128]
 
-    lane = lax.broadcasted_iota(jnp.int32, (1, LANES), 1)
-    col_local = jnp.where(lane < LANES - margin - 8, lane, lane - LANES)
     row_local = lax.broadcasted_iota(jnp.int32, (span0, LANES), 0) - margin
-    apart = jnp.abs(row_first + row_local - (col_first + col_local))
+    apart = jnp.abs(row_first + row_local - col_glob)
     distance[...] = jnp.log(1.0 + apart.astype(jnp.float32)) * 0.125
-
-    col_glob = col_first + col_local
-    inside = (col_glob >= 0) & (col_glob < total_shards * shard)
-    inside_high = jnp.where(inside[:, 128:], 1.0, 0.0)
-    inside_high = jnp.broadcast_to(inside_high, (chans, 128)).astype(jnp.bfloat16)
     gain_wide = jnp.broadcast_to(gain[...], (chans, LANES))
     lane16 = lax.broadcasted_iota(jnp.int16, (chans, 128), 1)
 
-    def keep(field, d):
+    def keep(field, d, masked):
         back = 128 - d
         at_left = lane16 < d.astype(jnp.int16)
         at_right = lane16 >= back.astype(jnp.int16)
 
         def store(i, low, high):
             low = low.astype(jnp.bfloat16)
-            high = high.astype(jnp.bfloat16) * inside_high
+            high = high.astype(jnp.bfloat16)
+            if masked:
+                high = high * inside_high
             field[i, chans : 2 * chans, :128] = low
             field[i, chans : 2 * chans, 128:] = high
             turned_low, turned_high = pltpu.roll(low, d, 1), pltpu.roll(high, d, 1)
@@ -156,13 +168,12 @@
                 field[extra + tile_rows + i] = jnp.zeros(field.shape[1:], field.dtype)
 
     need = dils[0] + dils[1] + dils[2]
-    store_first = keep(field_a, dils[0])
-    first, last = margin - need, margin + tile_rows + need
-
-    @pl.loop(0, (last - first + 3) // 4)
-    def _(block):
-        for k in range(4):
-            i = jnp.minimum(first + block * 4 + k, last - 1)
+    store_first = keep(field_a, dils[0], False)
+    first_row, last_row_needed = margin - need, margin + tile_rows + need - 1
+
+    def build(index, count):
+        for k in range(count):
+            i = jnp.minimum(first_row + index + k, last_row_needed)
             pick = jnp.full((chans, 128), i % 128, jnp.int32)
             row_term = jnp.take_along_axis(row_turned[i // 128], pick, axis=1)
             row_term = jnp.concatenate([row_term, row_term], axis=1)
@@ -170,7 +181,9 @@
             value = jnp.maximum(value, 0.0)
             store_first(i, value[:, :128], value[:, 128:])
 
-    clear(field_a, margin)
+    @pl.loop(0, (last_row_needed - first_row + 8) // 8)
+    def _(block):
+        build(block * 8, 8)
 
     tail = jnp.ones((TAIL, WIDE * LANES), jnp.bfloat16)
 
@@ -180,50 +193,61 @@
         first = extra - need
         count = tile_rows + 2 * need
         final_layer = layer == 2
-
-        def groups(bases):
-            width = 128 if final_layer else LANES
+        width = 128 if final_layer else LANES
+        each = WIDE * LANES // width
+
+        def product(bases):
             taps = []
             for k in range(GROUP + 2):
                 at = [base + DMAX2 + (k - 1) * d for base in bases]
                 taps.append(jnp.concatenate([source[i, :, :width] for i in at], axis=1))
             stack = jnp.concatenate(taps + [tail], axis=0)
-            sums = jnp.dot(weight[layer], stack, preferred_element_type=jnp.float32)
+            return jnp.dot(weight[layer], stack, preferred_element_type=jnp.float32)
+
+        def finish(bases, sums):
             for n, base in enumerate(bases):
                 for k in range(GROUP):
                     at = slice(n * width, (n + 1) * width)
-                    center = taps[k + 1][chans : 2 * chans, at].astype(jnp.float32)
-                    value = center + jnp.maximum(sums[k * chans : (k + 1) * chans, at], 0.0)
+                    center = source[base + DMAX2 + k * d, chans : 2 * chans, :width]
+                    value = sums[k * chans : (k + 1) * chans, at]
+                    value = center.astype(jnp.float32) + jnp.maximum(value, 0.0)
                     if final_layer:
                         store(base + k * d, value)
                     else:
                         store(base + k * d, value[:, :128], value[:, 128:])
 
-        each = WIDE * (2 if final_layer else 1)
-        total = (count + span - 1) // span * d
-
-        @functools.partial(
-            lax.fori_loop, 0, (total + UNROLL * each - 1) // (UNROLL * each),
-            init_val=(jnp.int32(0), jnp.int32(0)),
-        )
-        def _(step, carry):
-            start, phase = carry
+        def walk(start, phase):
             bases = []
-            for _ in range(UNROLL * each):
+            for _ in range(each):
                 bases.append(first + jnp.minimum(start, count - span) + phase)
                 wrap = phase + 1 >= d
                 start = jnp.where(wrap, start + span, start)
                 phase = jnp.where(wrap, 0, phase + 1)
+            return bases, start, phase
+
+        def step(_, carry):
+            start, phase, bases = carry
+            sums = held
             for k in range(UNROLL):
-                groups(bases[k * each : (k + 1) * each])
-            return start, phase
+                next_bases, start, phase = walk(start, phase)
+                next_sums = product(next_bases)
+                finish(bases, sums)
+                bases, sums = next_bases, next_sums
+            held[...] = sums
+            return start, phase, bases
+
+        zero = jnp.int32(0)
+        total = (count + span - 1) // span * d
+        steps = (total + UNROLL * each - 1) // (UNROLL * each)
+        carry = lax.fori_loop(0, steps, step, (zero, zero, walk(zero, zero)[0]))
+        finish(carry[2], held)
 
     def keep_last(i, low):
-        final[pl.ds(pl.multiple_of(i * chans, chans), chans), :] = low
-
-    tower(0, field_a, 2 * DMAX2, dils[1] + dils[2], keep(field_b, dils[1]))
+        final[pl.ds(pl.multiple_of(i * PITCH, 8), chans), :] = low
+
+    tower(0, field_a, 2 * DMAX2, dils[1] + dils[2], keep(field_b, dils[1], True))
     clear(field_b, 2 * DMAX2)
-    tower(1, field_b, DMAX2, dils[2], keep(field_a, dils[2]))
+    tower(1, field_b, DMAX2, dils[2], keep(field_a, dils[2], True))
     clear(field_a, DMAX2)
     tower(2, field_a, 0, 0, keep_last)
 
@@ -231,7 +255,7 @@
     def _(block):
         first = pl.multiple_of(block * 16, 16)
         for c in range(chans):
-            taken = final[pl.ds(first * chans + c, 16, stride=chans), :]
+            taken = final[pl.ds(first * PITCH + c, 16, stride=PITCH), :]
             out[c, pl.ds(first, 16), :] = taken.astype(jnp.bfloat16)
 
 
@@ -267,7 +291,8 @@
             pltpu.VMEM((span, LANES), jnp.float32),
             pltpu.VMEM((span, 3 * chans, LANES), jnp.bfloat16),
             pltpu.VMEM((span - 2 * DMAX2, 3 * chans, LANES), jnp.bfloat16),
-            pltpu.VMEM((tile_rows * chans, 128), jnp.float32),
+            pltpu.VMEM((tile_rows * PITCH, 128), jnp.float32),
+            pltpu.VMEM((GROUP * chans, WIDE * LANES), jnp.float32),
         ],
         compiler_params=pltpu.CompilerParams(vmem_limit_bytes=48 * 2**20),
         cost_estimate=pl.CostEstimate(
@@ -313,8 +338,6 @@
     up2, up1, down1, down2 = moved(2), moved(1), moved(-1), moved(-2)
     code = position_code(mine * shard + jnp.arange(shard), start_bin[0], chans)
     code = jnp.pad(code, ((0, 0), (0, chans)))
-    near = [features.astype(jnp.float32), tower_bias, pair_proj.T.astype(jnp.float32)]
-    near = jnp.concatenate(near, axis=0)
     bands = banded(map_weight, map_bias)
 
     smem = pl.BlockSpec(memory_space=pltpu.SMEM)
@@ -322,15 +345,20 @@
     parts = pl.pallas_call(
         functools.partial(encode_kernel, total),
         out_shape=jax.ShapeDtypeStruct((shards, shard // 2, 4 * chans), jnp.bfloat16),
-        in_specs=[smem] + [vmem] * 6 + [pl.BlockSpec(memory_space=pltpu.HBM)],
+        in_specs=[smem] + [pl.BlockSpec(memory_space=pltpu.HBM)] * 9,
         out_specs=vmem,
         scratch_shapes=[
+            pltpu.VMEM((5, shard, width), features.dtype),
+            pltpu.VMEM(tower_bias.shape, tower_bias.dtype),
+            pltpu.VMEM(pair_proj.shape[::-1], pair_proj.dtype),
+            pltpu.VMEM(code.shape, code.dtype),
             pltpu.VMEM(tower_weight.shape, tower_weight.dtype),
             pltpu.VMEM((width // 128, 5 * shard, 128), jnp.float32),
             pltpu.VMEM((width // 128, 3 * shard, 128), jnp.float32),
+            pltpu.SemaphoreType.DMA((8,)),
             pltpu.SemaphoreType.DMA(tower_weight.shape[:2]),
         ],
-        compiler_params=pltpu.CompilerParams(vmem_limit_bytes=52 * 2**20),
+        compiler_params=pltpu.CompilerParams(vmem_limit_bytes=56 * 2**20),
         cost_estimate=pl.CostEstimate(
             flops=2 * 4 * shard * 3 * width * width,
             bytes_accessed=6 * width * width * 2,
@@ -338,7 +366,7 @@
         ),
         name="encode",
     )(
-        place, up2, up1, down1, down2, code, near, tower_weight,
+        place, up2, up1, features, down1, down2, tower_bias, pair_proj.T, code, tower_weight,
     )
 
     gathered = lax.all_to_all(parts, AXES, split_axis=0, concat_axis=0, tiled=True)

time: 83.9 us -> 76.2 us (0.908); the launches traced: 82.8 us -> 76.2 us
  Pallas kernels: 40.4 us -> 33.1 us
  other arithmetic: 2.73 us -> 1.04 us
  local copies, waits for them, and re-layouts: 1.52 us -> 2.64 us
    pallas_call x1, Pallas kernels: 36.8 us -> 29 us  [pair_call(): pl.pallas_call(functools.partial(pair_kernel, gathered.shape[0], place.sh...]
    convert_element_type x2 -> x0, other arithmetic: 1.58 us -> none  [the longest x1 0.85 us: on_device(): pair_proj.T.astype(jnp.float32)]
  transfers between devices with their start and end apart: 5 -> 5, of which waited for: 1 -> 2; matrix products, arithmetic and copies ran while one was open for 5% -> 4% of each run, Pallas kernels for 0% -> 0%
where the time goes in v5:
time: 76.2 us
  Pallas kernels  33.1 us (43%)
  starting transfers between devices  28 us (37%)
  waiting for transfers between devices  10.5 us (14%)
  local copies, waits for them, and re-layouts  2.64 us (3%)
  other arithmetic  1.04 us (1%)
  between operations  0.82 us (1%)
    pallas_call x1, Pallas kernels, pair_call(): pl.pallas_call(functools.partial(pair_kernel, gathered.shape[0], place.sh...  29 us
    all_to_all x1, starting transfers between devices, on_device(): lax.all_to_all(parts, AXES, split_axis=0, concat_axis=0, tiled=True)  16.2 us
    ppermute x4, starting transfers between devices, moved(): return lax.ppermute(features, AXES, pairs)  11.8 us
    all_to_all x1, waiting for transfers between devices, on_device(): lax.all_to_all(parts, AXES, split_axis=0, concat_axis=0, tiled=True)  9.9 us
    pallas_call x1, Pallas kernels, on_device(): pl.pallas_call(functools.partial(encode_kernel, total), out_shape=jax.Sha...  4.13 us
  transfers between devices with their start and end apart: 5, of which 2 were waited for; matrix products, arithmetic and copies ran while one was open for 4% of the time, Pallas kernels for 0%

profile of v5, /device:TPU:1, one launch (start us, length us, event | category | flops | bytes accessed | tf_op | source)
XLA Modules:
  0.0 76.2 jit_solution(17031080921656716257)
XLA Ops:
  0.0 0.0 copy-start.6
  0.0 0.0 copy-start.7
  0.0 0.0 copy-start.1
  0.0 3.4 %collective-permute-start.2 = (bf16[16,512]{1,0:T(8,128)(2,1)}, bf16[16,512]{1,0:T(8,128)(2,1)S(1)}, u32[]{:S(2)}, u32[]{:S(2)}) collective-permute-start(bf16[16,512]{1,0:T(8,128)(2,1)} %here_far.1), channel_id=1, source_target_pairs={{1,0},{2,1},{3,2},{4,3},{5,4},{6,5},{7,6},{8,7},{9,8},{10,9},{11,1... | collective-permute-start | bytes 49160 | tf_op jit(solution)/shard_map/ppermute | solution.py:336
  3.5 3.1 %collective-permute-start.1 = (bf16[16,512]{1,0:T(8,128)(2,1)}, bf16[16,512]{1,0:T(8,128)(2,1)S(1)}, u32[]{:S(2)}, u32[]{:S(2)}) collective-permute-start(bf16[16,512]{1,0:T(8,128)(2,1)} %here_far.1), channel_id=1, source_target_pairs={{0,1},{1,2},{2,3},{3,4},{4,5},{5,6},{6,7},{7,8},{8,9},{9,10},{10,1... | collective-permute-start | bytes 49160 | tf_op jit(solution)/shard_map/ppermute | solution.py:336
  6.6 4.0 %collective-permute-start = (bf16[16,512]{1,0:T(8,128)(2,1)}, bf16[16,512]{1,0:T(8,128)(2,1)S(1)}, u32[]{:S(2)}, u32[]{:S(2)}) collective-permute-start(bf16[16,512]{1,0:T(8,128)(2,1)} %here_far.1), channel_id=1, source_target_pairs={{0,2},{1,3},{2,4},{3,5},{4,6},{5,7},{6,8},{7,9},{8,10},{9,11},{10,... | collective-permute-start | bytes 49160 | tf_op jit(solution)/shard_map/ppermute | solution.py:336
  10.6 1.3 %collective-permute-start.3 = (bf16[16,512]{1,0:T(8,128)(2,1)}, bf16[16,512]{1,0:T(8,128)(2,1)S(1)}, u32[]{:S(2)}, u32[]{:S(2)}) collective-permute-start(bf16[16,512]{1,0:T(8,128)(2,1)} %here_far.1), channel_id=1, source_target_pairs={{2,0},{3,1},{4,2},{5,3},{6,4},{7,5},{8,6},{9,7},{10,8},{11,9},{12,... | collective-permute-start | bytes 49160 | tf_op jit(solution)/shard_map/ppermute | solution.py:336
  12.6 0.1 multiply_cosine_fusion
  12.7 0.7 select_maximum_fusion.code_far
  13.4 1.2 %concatenate.18.place = s32[10]{0:T(128)} concatenate(s32[1]{0:T(128)} %bitcast, s32[1]{0:T(128)} %bitcast.1, s32[1]{0:T(128)} %bitcast.2, s32[1]{0:T(128)} %constant.29.clone.1, s32[1]{0:T(128)} %constant.30.clone.1, s32[5]{0:T(128)} %param.16), dimensions={0} | concatenate | bytes 80 | tf_op jit(solution)/shard_map/concatenate | solution.py:332
  14.6 0.0 copy-start
  14.6 0.0 collective-permute-done.2.down1_far
  14.6 0.0 copy-start.2
  14.6 0.0 collective-permute-done.1.up1_far
  14.6 0.0 copy-start.3
  14.6 0.0 collective-permute-done.up2_far
  14.6 0.0 copy-start.4
  14.6 0.6 collective-permute-done.3.down2_far
  15.3 0.0 copy-start.5
  15.3 0.0 copy-done.2
  15.3 0.0 copy-done.3
  15.3 0.0 copy-done.4
  15.3 0.6 copy-done.5
  15.9 4.1 %encode.1 = bf16[128,8,128]{2,1,0:T(8,128)(2,1)} custom-call(s32[10]{0:T(128)} %concatenate.18.place, bf16[16,512]{1,0:T(8,128)(2,1)} %copy-done.4, bf16[16,512]{1,0:T(8,128)(2,1)} %copy-done.3, bf16[16,512]{1,0:T(8,128)(2,1)} %here_far.1, bf16[16,512]{1,0:T(8,128)(2,1)} %copy-done.2, bf16[16,512]{1,0:T(8,128)(2,1)} %copy-done.5, f32[2,512]{1,0:T(2,128)} %bias_far.1, ...), custom_call_target="tpu_custom_call" | custom-call | flops 100663296 | bytes 3145728 | tf_op jit(solution)/shard_map/encode/pallas_call | solution.py:345
  20.0 16.2 %all-to-all-start = ((bf16[128,8,128]{2,1,0:T(8,128)(2,1)}), bf16[128,8,128]{2,1,0:T(8,128)(2,1)S(1)}, u32[]{:S(2)}, u32[]{:S(2)}) async-start(bf16[128,8,128]{2,1,0:T(8,128)(2,1)} %encode.1), calls=%async_computation | async-start | bytes 524288 | tf_op jit(solution)/shard_map/all_to_all | solution.py:372
  36.2 0.0 copy-done.6
  36.2 0.0 copy-done.7
  36.2 0.1 copy.30.gain
  36.3 0.1 copy.27
  36.4 0.1 copy.29
  36.5 0.1 copy.28
  36.7 0.0 copy-done.1
  36.7 0.2 copy.26
  36.8 0.2 reshape.31
  37.0 0.1 fusion.19
  37.1 0.1 fusion.12.weight
  37.3 9.9 %all-to-all-done.parts = bf16[128,8,128]{2,1,0:T(8,128)(2,1)S(1)} async-done(((bf16[128,8,128]{2,1,0:T(8,128)(2,1)}), bf16[128,8,128]{2,1,0:T(8,128)(2,1)S(1)}, u32[]{:S(2)}, u32[]{:S(2)}) %all-to-all-start) | async-done | bytes 262176 | tf_op jit(solution)/shard_map/all_to_all | solution.py:372
  47.2 0.0 copy-done
  47.2 29.0 %pair_tower.1 = bf16[32,256,128]{2,1,0:T(8,128)(2,1)} custom-call(s32[10]{0:T(128)S(1)} %copy-done, bf16[128,8,128]{2,1,0:T(8,128)(2,1)S(1)} %all-to-all-done.parts, f32[32,1]{1,0:T(8,128)S(1)} %copy.30.gain, bf16[3,96,512]{2,1,0:T(8,128)(2,1)S(1)} %fusion.12.weight), custom_call_target="tpu_custom_call" | custom-call | flops 3623878656 | bytes 2097152 | tf_op jit(solution)/shard_map/pair_tower/pallas_call | solution.py:284
  (3 shorter events, 0.0 us)
Async XLA Ops:
  0.0 36.2 %copy-start.6 = (f32[3,32]{1,0:T(4,128)S(1)}, f32[3,32]{1,0:T(4,128)}, u32[]{:S(2)}) copy-start(f32[3,32]{1,0:T(4,128)} %param.15) | copy-start | bytes 1156
  0.0 36.2 %copy-start.7 = (f32[32]{0:T(128)S(1)}, f32[32]{0:T(128)}, u32[]{:S(2)}) copy-start(f32[32]{0:T(128)} %param.13) | copy-start | bytes 388
  0.0 36.7 %copy-start.1 = (bf16[3,3,3,32,32]{4,3,2,1,0:T(8,128)(2,1)S(1)}, bf16[3,3,3,32,32]{4,3,2,1,0:T(8,128)(2,1)}, u32[]{:S(2)}) copy-start(bf16[3,3,3,32,32]{4,3,2,1,0:T(8,128)(2,1)} %param.14) | copy-start | bytes 165892
  0.0 14.6 %collective-permute-start.2 = (bf16[16,512]{1,0:T(8,128)(2,1)}, bf16[16,512]{1,0:T(8,128)(2,1)S(1)}, u32[]{:S(2)}, u32[]{:S(2)}) collective-permute-start(bf16[16,512]{1,0:T(8,128)(2,1)} %here_far.1), channel_id=1, source_target_pairs={{1,0},{2,1},{3,2},{4,3},{5,4},{6,5},{7,6},{8,7},{9,8},{10,9},{11,1... | collective-permute-start | bytes 49160 | tf_op jit(solution)/shard_map/ppermute | solution.py:336
  3.5 11.1 %collective-permute-start.1 = (bf16[16,512]{1,0:T(8,128)(2,1)}, bf16[16,512]{1,0:T(8,128)(2,1)S(1)}, u32[]{:S(2)}, u32[]{:S(2)}) collective-permute-start(bf16[16,512]{1,0:T(8,128)(2,1)} %here_far.1), channel_id=1, source_target_pairs={{0,1},{1,2},{2,3},{3,4},{4,5},{5,6},{6,7},{7,8},{8,9},{9,10},{10,1... | collective-permute-start | bytes 49160 | tf_op jit(solution)/shard_map/ppermute | solution.py:336
  6.6 8.0 %collective-permute-start = (bf16[16,512]{1,0:T(8,128)(2,1)}, bf16[16,512]{1,0:T(8,128)(2,1)S(1)}, u32[]{:S(2)}, u32[]{:S(2)}) collective-permute-start(bf16[16,512]{1,0:T(8,128)(2,1)} %here_far.1), channel_id=1, source_target_pairs={{0,2},{1,3},{2,4},{3,5},{4,6},{5,7},{6,8},{7,9},{8,10},{9,11},{10,... | collective-permute-start | bytes 49160 | tf_op jit(solution)/shard_map/ppermute | solution.py:336
  10.6 4.7 %collective-permute-start.3 = (bf16[16,512]{1,0:T(8,128)(2,1)}, bf16[16,512]{1,0:T(8,128)(2,1)S(1)}, u32[]{:S(2)}, u32[]{:S(2)}) collective-permute-start(bf16[16,512]{1,0:T(8,128)(2,1)} %here_far.1), channel_id=1, source_target_pairs={{2,0},{3,1},{4,2},{5,3},{6,4},{7,5},{8,6},{9,7},{10,8},{11,9},{12,... | collective-permute-start | bytes 49160 | tf_op jit(solution)/shard_map/ppermute | solution.py:336
  14.6 32.6 %copy-start = (s32[10]{0:T(128)S(1)}, s32[10]{0:T(128)}, u32[]{:S(2)}) copy-start(s32[10]{0:T(128)} %concatenate.18.place) | copy-start | bytes 124
  14.6 0.7 copy-start.2
  14.6 0.7 copy-start.3
  14.6 0.6 copy-start.4
  15.3 0.6 copy-start.5
  20.0 27.2 %all-to-all-start = ((bf16[128,8,128]{2,1,0:T(8,128)(2,1)}), bf16[128,8,128]{2,1,0:T(8,128)(2,1)S(1)}, u32[]{:S(2)}, u32[]{:S(2)}) async-start(bf16[128,8,128]{2,1,0:T(8,128)(2,1)} %encode.1), calls=%async_computation | async-start | bytes 524288 | tf_op jit(solution)/shard_map/all_to_all | solution.py:372

commit v6 on v5

--- a/solution.py
+++ b/solution.py
@@ -10,7 +10,7 @@
 
 DMAX1 = 16
 DMAX2 = 16
-GROUP = 3
+GROUP = 4
 TAIL = 32
 WIDE = 2
 UNROLL = 4
@@ -29,15 +29,12 @@
 
 
 def encode_kernel(
-    total, place, up2_far, up1_far, here_far, down1_far, down2_far, bias_far, proj_far, code_far,
-    weight_far, out, window, bias, proj, code, weight, wide, mid, near_done, arrived,
+    total, place, up2, up1, down1, down2, near, extra, weight_far, out,
+    weight, wide, mid, arrived,
 ):
-    count = here_far.shape[0]
-    pieces = [(far, window.at[k]) for k, far in enumerate((up2_far, up1_far, here_far, down1_far, down2_far))]
-    pieces += [(bias_far, bias), (proj_far, proj), (code_far, code)]
-    near = [
-        pltpu.make_async_copy(far, here, near_done.at[k]) for k, (far, here) in enumerate(pieces)
-    ]
+    count = up1.shape[0]
+    bias = extra[:2, :]
+    proj = near[count:, :]
     fetch = [
         [
             pltpu.make_async_copy(
@@ -47,10 +44,8 @@
         ]
         for which in range(2)
     ]
-    for copy in near + fetch[0] + fetch[1]:
+    for copy in fetch[0] + fetch[1]:
         copy.start()
-    for copy in near:
-        copy.wait()
     chunks = wide.shape[0]
 
     def keep(ref, first, value):
@@ -68,19 +63,19 @@
             running += jnp.dot(rows, weight[which, tap], preferred_element_type=jnp.float32)
         return run(ref, count, span) + jnp.maximum(running + bias[which : which + 1, :], 0.0)
 
-    for piece in range(5):
-        keep(wide, piece * count, window[piece].astype(jnp.float32))
+    for piece, ref in enumerate((up2, up1, near, down1, down2)):
+        keep(wide, piece * count, ref[:count, :].astype(jnp.float32))
     value = layer(0, wide, 3 * count).astype(jnp.bfloat16).astype(jnp.float32)
     index = (place[0] - 1) * count + lax.broadcasted_iota(jnp.int32, value.shape, 0)
     keep(mid, 0, jnp.where((index >= 0) & (index < total), value, 0.0))
     value = layer(1, mid, count)
     parts = lax.dot_general(
         value.astype(jnp.bfloat16),
-        proj[...],
+        proj,
         (((1,), (1,)), ((), ())),
         preferred_element_type=jnp.float32,
     )
-    parts = (parts + code[...]).astype(jnp.bfloat16)
+    parts = (parts + extra[2 : 2 + count, : proj.shape[0]]).astype(jnp.bfloat16)
     parts = jnp.concatenate([parts[: count // 2], parts[count // 2 :]], axis=1)
     out[...] = jnp.broadcast_to(parts[None], out.shape)
 
@@ -337,7 +332,9 @@
 
     up2, up1, down1, down2 = moved(2), moved(1), moved(-1), moved(-2)
     code = position_code(mine * shard + jnp.arange(shard), start_bin[0], chans)
-    code = jnp.pad(code, ((0, 0), (0, chans)))
+    code = jnp.pad(code, ((0, 0), (0, width - chans)))
+    extra = jnp.concatenate([tower_bias, code], axis=0)
+    near = jnp.concatenate([features, pair_proj.T], axis=0)
     bands = banded(map_weight, map_bias)
 
     smem = pl.BlockSpec(memory_space=pltpu.SMEM)
@@ -345,20 +342,15 @@
     parts = pl.pallas_call(
         functools.partial(encode_kernel, total),
         out_shape=jax.ShapeDtypeStruct((shards, shard // 2, 4 * chans), jnp.bfloat16),
-        in_specs=[smem] + [pl.BlockSpec(memory_space=pltpu.HBM)] * 9,
+        in_specs=[smem] + [vmem] * 6 + [pl.BlockSpec(memory_space=pltpu.HBM)],
         out_specs=vmem,
         scratch_shapes=[
-            pltpu.VMEM((5, shard, width), features.dtype),
-            pltpu.VMEM(tower_bias.shape, tower_bias.dtype),
-            pltpu.VMEM(pair_proj.shape[::-1], pair_proj.dtype),
-            pltpu.VMEM(code.shape, code.dtype),
             pltpu.VMEM(tower_weight.shape, tower_weight.dtype),
             pltpu.VMEM((width // 128, 5 * shard, 128), jnp.float32),
             pltpu.VMEM((width // 128, 3 * shard, 128), jnp.float32),
-            pltpu.SemaphoreType.DMA((8,)),
             pltpu.SemaphoreType.DMA(tower_weight.shape[:2]),
         ],
-        compiler_params=pltpu.CompilerParams(vmem_limit_bytes=56 * 2**20),
+        compiler_params=pltpu.CompilerParams(vmem_limit_bytes=52 * 2**20),
         cost_estimate=pl.CostEstimate(
             flops=2 * 4 * shard * 3 * width * width,
             bytes_accessed=6 * width * width * 2,
@@ -366,7 +358,7 @@
         ),
         name="encode",
     )(
-        place, up2, up1, features, down1, down2, tower_bias, pair_proj.T, code, tower_weight,
+        place, up2, up1, down1, down2, near, extra, tower_weight,
     )
 
     gathered = lax.all_to_all(parts, AXES, split_axis=0, concat_axis=0, tiled=True)

time: 76.2 us -> 75.6 us (level); the launches traced: 76.2 us -> 74.5 us
  starting transfers between devices: 28 us -> 25.2 us
  other arithmetic: 1.04 us -> 2.72 us
  Pallas kernels: 33.1 us -> 32 us
    all_to_all x1, starting transfers between devices: 16.2 us -> 13.5 us  [on_device(): lax.all_to_all(parts, AXES, split_axis=0, concat_axis=0, tiled=True)]
    concatenate x0 -> x2, other arithmetic: none -> 1.55 us  [the longest x1 0.86 us: on_device(): near = jnp.concatenate([features, pair_proj.T], axis=0)]
    transpose x1, local copies, waits for them, and re-layouts: 0.15 us -> 1.09 us  [banded(): jnp.transpose(map_weight, (0, 3, 1, 2, 4)).reshape(layers, outs, 9 * ins)]
    all_to_all x1, waiting for transfers between devices: 9.9 us -> 10.8 us  [on_device(): lax.all_to_all(parts, AXES, split_axis=0, concat_axis=0, tiled=True)]
  transfers between devices with their start and end apart: 5 -> 5, of which waited for: 2 -> 1; matrix products, arithmetic and copies ran while one was open for 4% -> 8% of each run, Pallas kernels for 0% -> 0%
where the time goes in v6:
time: 75.6 us; the launch traced here: 74.5 us
  Pallas kernels  32 us (42%)
  starting transfers between devices  25.2 us (33%)
  waiting for transfers between devices  10.8 us (14%)
  local copies, waits for them, and re-layouts  3.1 us (4%)
  other arithmetic  2.72 us (4%)
  between operations  0.76 us (1%)
    pallas_call x1, Pallas kernels, pair_call(): pl.pallas_call(functools.partial(pair_kernel, gathered.shape[0], place.sh...  28.4 us
    all_to_all x1, starting transfers between devices, on_device(): lax.all_to_all(parts, AXES, split_axis=0, concat_axis=0, tiled=True)  13.5 us
    ppermute x4, starting transfers between devices, moved(): return lax.ppermute(features, AXES, pairs)  11.7 us
    all_to_all x1, waiting for transfers between devices, on_device(): lax.all_to_all(parts, AXES, split_axis=0, concat_axis=0, tiled=True)  10.8 us
    pallas_call x1, Pallas kernels, on_device(): pl.pallas_call(functools.partial(encode_kernel, total), out_shape=jax.Sha...  3.54 us
  transfers between devices with their start and end apart: 5, of which 1 were waited for; matrix products, arithmetic and copies ran while one was open for 8% of the time, Pallas kernels for 0%

profile of v6, /device:TPU:1, one launch (start us, length us, event | category | flops | bytes accessed | tf_op | source)
XLA Modules:
  0.0 74.5 jit_solution(3677486830186413255)
XLA Ops:
  0.0 3.3 %collective-permute-start.2 = (bf16[16,512]{1,0:T(8,128)(2,1)}, bf16[16,512]{1,0:T(8,128)(2,1)S(1)}, u32[]{:S(2)}, u32[]{:S(2)}) collective-permute-start(bf16[16,512]{1,0:T(8,128)(2,1)} %param.9), channel_id=1, source_target_pairs={{1,0},{2,1},{3,2},{4,3},{5,4},{6,5},{7,6},{8,7},{9,8},{10,9},{11,1... | collective-permute-start | bytes 49160 | tf_op jit(solution)/shard_map/ppermute | solution.py:331
  3.3 3.1 %collective-permute-start.1 = (bf16[16,512]{1,0:T(8,128)(2,1)}, bf16[16,512]{1,0:T(8,128)(2,1)S(1)}, u32[]{:S(2)}, u32[]{:S(2)}) collective-permute-start(bf16[16,512]{1,0:T(8,128)(2,1)} %param.9), channel_id=1, source_target_pairs={{0,1},{1,2},{2,3},{3,4},{4,5},{5,6},{6,7},{7,8},{8,9},{9,10},{10,1... | collective-permute-start | bytes 49160 | tf_op jit(solution)/shard_map/ppermute | solution.py:331
  6.4 4.0 %collective-permute-start = (bf16[16,512]{1,0:T(8,128)(2,1)}, bf16[16,512]{1,0:T(8,128)(2,1)S(1)}, u32[]{:S(2)}, u32[]{:S(2)}) collective-permute-start(bf16[16,512]{1,0:T(8,128)(2,1)} %param.9), channel_id=1, source_target_pairs={{0,2},{1,3},{2,4},{3,5},{4,6},{5,7},{6,8},{7,9},{8,10},{9,11},{10,... | collective-permute-start | bytes 49160 | tf_op jit(solution)/shard_map/ppermute | solution.py:331
  10.4 1.3 %collective-permute-start.3 = (bf16[16,512]{1,0:T(8,128)(2,1)}, bf16[16,512]{1,0:T(8,128)(2,1)S(1)}, u32[]{:S(2)}, u32[]{:S(2)}) collective-permute-start(bf16[16,512]{1,0:T(8,128)(2,1)} %param.9), channel_id=1, source_target_pairs={{2,0},{3,1},{4,2},{5,3},{6,4},{7,5},{8,6},{9,7},{10,8},{11,9},{12,... | collective-permute-start | bytes 49160 | tf_op jit(solution)/shard_map/ppermute | solution.py:331
  12.4 0.7 fusion.28
  13.1 0.1 copy.27
  13.2 0.1 copy.29
  13.3 0.1 copy.28
  13.4 0.9 %pad_maximum_fusion.near = bf16[80,512]{1,0:T(8,128)(2,1)S(1)} fusion(bf16[64,512]{1,0:T(8,128)(2,1)} %bitcast.15, bf16[16,512]{1,0:T(8,128)(2,1)} %param.9), kind=kLoop, calls=%fused_computation.28 | loop fusion | flops 163840 | bytes 163840 | tf_op jit(solution)/shard_map/concatenate | solution.py:337
  14.3 0.1 multiply_cosine_fusion
  14.4 0.1 select_maximum_fusion
  14.5 0.7 pad_maximum_fusion.1.extra
  15.2 0.1 fusion.25
  15.3 0.7 copy.30.gain
  16.0 1.1 %copy.26 = bf16[3,32,3,3,32]{4,3,2,1,0:T(4,128)(2,1)S(1)} copy(bf16[3,32,3,3,32]{4,1,3,2,0:T(8,128)(2,1)} %bitcast.14) | data formatting | bytes 110592 | tf_op jit(solution)/shard_map/transpose | solution.py:259
  17.1 0.2 reshape.31
  17.3 0.7 concatenate.27.place
  18.1 0.0 collective-permute-done.2.down1
  18.1 0.0 collective-permute-done.1.up1
  18.1 0.0 collective-permute-done.up2
  18.1 0.0 collective-permute-done.3.down2
  18.1 3.5 %encode.1 = bf16[128,8,128]{2,1,0:T(8,128)(2,1)} custom-call(s32[10]{0:T(128)S(1)} %concatenate.27.place, bf16[16,512]{1,0:T(8,128)(2,1)S(1)} %collective-permute-done.up2, bf16[16,512]{1,0:T(8,128)(2,1)S(1)} %collective-permute-done.1.up1, bf16[16,512]{1,0:T(8,128)(2,1)S(1)} %collective-permute-done.2.down1, ...), custom_call_target="tpu_custom_call" | custom-call | flops 100663296 | bytes 3145728 | tf_op jit(solution)/shard_map/encode/pallas_call | solution.py:342
  21.6 13.5 %all-to-all-start = ((bf16[128,8,128]{2,1,0:T(8,128)(2,1)}), bf16[128,8,128]{2,1,0:T(8,128)(2,1)S(1)}, u32[]{:S(2)}, u32[]{:S(2)}) async-start(bf16[128,8,128]{2,1,0:T(8,128)(2,1)} %encode.1), calls=%async_computation | async-start | bytes 524288 | tf_op jit(solution)/shard_map/all_to_all | solution.py:364
  35.1 0.2 fusion.19.weight
  35.3 10.8 %all-to-all-done.parts = bf16[128,8,128]{2,1,0:T(8,128)(2,1)S(1)} async-done(((bf16[128,8,128]{2,1,0:T(8,128)(2,1)}), bf16[128,8,128]{2,1,0:T(8,128)(2,1)S(1)}, u32[]{:S(2)}, u32[]{:S(2)}) %all-to-all-start) | async-done | bytes 262176 | tf_op jit(solution)/shard_map/all_to_all | solution.py:364
  46.1 28.4 %pair_tower.1 = bf16[32,256,128]{2,1,0:T(8,128)(2,1)} custom-call(s32[10]{0:T(128)S(1)} %concatenate.27.place, bf16[128,8,128]{2,1,0:T(8,128)(2,1)S(1)} %all-to-all-done.parts, f32[32,1]{1,0:T(8,128)S(1)} %copy.30.gain, bf16[3,128,608]{2,1,0:T(8,128)(2,1)S(1)} %fusion.19.weight), custom_call_target="tpu_custom_call" | custom-call | flops 3623878656 | bytes 2097152 | tf_op jit(solution)/shard_map/pair_tower/pallas_call | solution.py:279
  (2 shorter events, 0.0 us)
Async XLA Ops:
  0.0 18.1 %collective-permute-start.2 = (bf16[16,512]{1,0:T(8,128)(2,1)}, bf16[16,512]{1,0:T(8,128)(2,1)S(1)}, u32[]{:S(2)}, u32[]{:S(2)}) collective-permute-start(bf16[16,512]{1,0:T(8,128)(2,1)} %param.9), channel_id=1, source_target_pairs={{1,0},{2,1},{3,2},{4,3},{5,4},{6,5},{7,6},{8,7},{9,8},{10,9},{11,1... | collective-permute-start | bytes 49160 | tf_op jit(solution)/shard_map/ppermute | solution.py:331
  3.3 14.7 %collective-permute-start.1 = (bf16[16,512]{1,0:T(8,128)(2,1)}, bf16[16,512]{1,0:T(8,128)(2,1)S(1)}, u32[]{:S(2)}, u32[]{:S(2)}) collective-permute-start(bf16[16,512]{1,0:T(8,128)(2,1)} %param.9), channel_id=1, source_target_pairs={{0,1},{1,2},{2,3},{3,4},{4,5},{5,6},{6,7},{7,8},{8,9},{9,10},{10,1... | collective-permute-start | bytes 49160 | tf_op jit(solution)/shard_map/ppermute | solution.py:331
  6.4 11.6 %collective-permute-start = (bf16[16,512]{1,0:T(8,128)(2,1)}, bf16[16,512]{1,0:T(8,128)(2,1)S(1)}, u32[]{:S(2)}, u32[]{:S(2)}) collective-permute-start(bf16[16,512]{1,0:T(8,128)(2,1)} %param.9), channel_id=1, source_target_pairs={{0,2},{1,3},{2,4},{3,5},{4,6},{5,7},{6,8},{7,9},{8,10},{9,11},{10,... | collective-permute-start | bytes 49160 | tf_op jit(solution)/shard_map/ppermute | solution.py:331
  10.4 7.6 %collective-permute-start.3 = (bf16[16,512]{1,0:T(8,128)(2,1)}, bf16[16,512]{1,0:T(8,128)(2,1)S(1)}, u32[]{:S(2)}, u32[]{:S(2)}) collective-permute-start(bf16[16,512]{1,0:T(8,128)(2,1)} %param.9), channel_id=1, source_target_pairs={{2,0},{3,1},{4,2},{5,3},{6,4},{7,5},{8,6},{9,7},{10,8},{11,9},{12,... | collective-permute-start | bytes 49160 | tf_op jit(solution)/shard_map/ppermute | solution.py:331
  21.6 24.5 %all-to-all-start = ((bf16[128,8,128]{2,1,0:T(8,128)(2,1)}), bf16[128,8,128]{2,1,0:T(8,128)(2,1)S(1)}, u32[]{:S(2)}, u32[]{:S(2)}) async-start(bf16[128,8,128]{2,1,0:T(8,128)(2,1)} %encode.1), calls=%async_computation | async-start | bytes 524288 | tf_op jit(solution)/shard_map/all_to_all | solution.py:364

commit v7 on v6

--- a/solution.py
+++ b/solution.py
@@ -29,10 +29,10 @@
 
 
 def encode_kernel(
-    total, place, up2, up1, down1, down2, near, extra, weight_far, out,
+    total, place, inner1, outer1, inner2, outer2, near, extra, weight_far, out, none_16, none_32,
     weight, wide, mid, arrived,
 ):
-    count = up1.shape[0]
+    count = inner1.shape[0]
     bias = extra[:2, :]
     proj = near[count:, :]
     fetch = [
@@ -50,7 +50,7 @@
 
     def keep(ref, first, value):
         for k in range(chunks):
-            ref[k, first : first + value.shape[0], :] = value[:, k * 128 : (k + 1) * 128]
+            ref[k, pl.ds(first, value.shape[0]), :] = value[:, k * 128 : (k + 1) * 128]
 
     def run(ref, first, span):
         return jnp.concatenate([ref[k, pl.ds(first, span), :] for k in range(chunks)], axis=1)
@@ -63,8 +63,13 @@
             running += jnp.dot(rows, weight[which, tap], preferred_element_type=jnp.float32)
         return run(ref, count, span) + jnp.maximum(running + bias[which : which + 1, :], 0.0)
 
-    for piece, ref in enumerate((up2, up1, near, down1, down2)):
-        keep(wide, piece * count, ref[:count, :].astype(jnp.float32))
+    odd = place[0] % 2
+    for side, ref in ((2, near), (3 - 2 * odd, inner1), (1 + 2 * odd, outer1),
+                      (4 - 4 * odd, inner2), (4 * odd, outer2)):
+        first = side * count
+        if ref is not near:
+            first = pl.multiple_of(first, count)
+        keep(wide, first, ref[:count, :].astype(jnp.float32))
     value = layer(0, wide, 3 * count).astype(jnp.bfloat16).astype(jnp.float32)
     index = (place[0] - 1) * count + lax.broadcasted_iota(jnp.int32, value.shape, 0)
     keep(mid, 0, jnp.where((index >= 0) & (index < total), value, 0.0))
@@ -78,6 +83,8 @@
     parts = (parts + extra[2 : 2 + count, : proj.shape[0]]).astype(jnp.bfloat16)
     parts = jnp.concatenate([parts[: count // 2], parts[count // 2 :]], axis=1)
     out[...] = jnp.broadcast_to(parts[None], out.shape)
+    none_16[...] = jnp.zeros(none_16.shape, none_16.dtype)
+    none_32[...] = jnp.zeros(none_32.shape, none_32.dtype)
 
 
 def pair_kernel(
@@ -326,24 +333,28 @@
     place = jnp.stack([mine, row_place, col_place, row_count, col_count]).astype(jnp.int32)
     place = jnp.concatenate([place, dilations])
 
-    def moved(step):
-        pairs = [(i, i + step) for i in range(shards) if 0 <= i + step < shards]
-        return lax.ppermute(features, AXES, pairs)
-
-    up2, up1, down1, down2 = moved(2), moved(1), moved(-1), moved(-2)
+    inner = [(i, i ^ 1) for i in range(shards)]
+    outer = [(i, i + 1 if i % 2 else i - 1) for i in range(1, shards - 1)]
+    inner1 = lax.ppermute(features, AXES, inner)
+    outer1 = lax.ppermute(features, AXES, outer)
+    outer2 = lax.ppermute(inner1, AXES, outer)
+    inner2 = lax.ppermute(outer1, AXES, inner)
     code = position_code(mine * shard + jnp.arange(shard), start_bin[0], chans)
     code = jnp.pad(code, ((0, 0), (0, width - chans)))
     extra = jnp.concatenate([tower_bias, code], axis=0)
     near = jnp.concatenate([features, pair_proj.T], axis=0)
-    bands = banded(map_weight, map_bias)
 
     smem = pl.BlockSpec(memory_space=pltpu.SMEM)
     vmem = pl.BlockSpec(memory_space=pltpu.VMEM)
-    parts = pl.pallas_call(
+    parts, none_16, none_32 = pl.pallas_call(
         functools.partial(encode_kernel, total),
-        out_shape=jax.ShapeDtypeStruct((shards, shard // 2, 4 * chans), jnp.bfloat16),
+        out_shape=[
+            jax.ShapeDtypeStruct((shards, shard // 2, 4 * chans), jnp.bfloat16),
+            jax.ShapeDtypeStruct(map_weight.shape, map_weight.dtype),
+            jax.ShapeDtypeStruct((map_bias.shape[0] + 1, chans), jnp.float32),
+        ],
         in_specs=[smem] + [vmem] * 6 + [pl.BlockSpec(memory_space=pltpu.HBM)],
-        out_specs=vmem,
+        out_specs=[vmem] * 3,
         scratch_shapes=[
             pltpu.VMEM(tower_weight.shape, tower_weight.dtype),
             pltpu.VMEM((width // 128, 5 * shard, 128), jnp.float32),
@@ -358,10 +369,14 @@
         ),
         name="encode",
     )(
-        place, up2, up1, down1, down2, near, extra, tower_weight,
+        place, inner1, outer1, inner2, outer2, near, extra, tower_weight,
     )
 
     gathered = lax.all_to_all(parts, AXES, split_axis=0, concat_axis=0, tiled=True)
+
+    bands = banded(map_weight + none_16, map_bias + none_32[:-1])
+    dist_gain = dist_gain + none_32[-1]
+
     return pair_call(
         place, gathered, dist_gain, bands, tile_rows, tile_cols
     )

time: 75.6 us -> 67.8 us (0.90)
  starting transfers between devices: 25.2 us -> 20.5 us
  local copies, waits for them, and re-layouts: 3.1 us -> 1.52 us
    ppermute x4, starting transfers between devices: 11.7 us -> 7.05 us  [the longest x1 3.32 us: on_device(): outer1 = lax.ppermute(features, AXES, outer)]
    ppermute x4, waiting for transfers between devices: 0.01 us -> 1.29 us  [the longest x1 1.28 us: on_device(): outer2 = lax.ppermute(inner1, AXES, outer)]
    transpose x1, local copies, waits for them, and re-layouts: 1.09 us -> 0.15 us  [banded(): jnp.transpose(map_weight, (0, 3, 1, 2, 4)).reshape(layers, outs, 9 * ins)]
    all_to_all x1, waiting for transfers between devices: 10.8 us -> 9.87 us  [on_device(): lax.all_to_all(parts, AXES, split_axis=0, concat_axis=0, tiled=True)]
  transfers between devices with their start and end apart: 5 -> 5, of which waited for: 1 -> 2; matrix products, arithmetic and copies ran while one was open for 8% -> 5% of each run, Pallas kernels for 0% -> 0%
where the time goes in v7:
time: 67.8 us; the launch traced here: 67.3 us
  Pallas kernels  31.3 us (46%)
  starting transfers between devices  20.5 us (30%)
  waiting for transfers between devices  11.2 us (17%)
  other arithmetic  2.06 us (3%)
  local copies, waits for them, and re-layouts  1.52 us (2%)
  between operations  0.8 us (1%)
    pallas_call x1, Pallas kernels, pair_call(): pl.pallas_call(functools.partial(pair_kernel, gathered.shape[0], place.sh...  27.8 us
    all_to_all x1, starting transfers between devices, on_device(): lax.all_to_all(parts, AXES, split_axis=0, concat_axis=0, tiled=True)  13.4 us
    all_to_all x1, waiting for transfers between devices, on_device(): lax.all_to_all(parts, AXES, split_axis=0, concat_axis=0, tiled=True)  9.87 us
    pallas_call x1, Pallas kernels, on_device(): pl.pallas_call(functools.partial(encode_kernel, total), out_shape=[jax.Sh...  3.53 us
    ppermute x1, starting transfers between devices, on_device(): outer1 = lax.ppermute(features, AXES, outer)  3.32 us
    ppermute x1, starting transfers between devices, on_device(): outer2 = lax.ppermute(inner1, AXES, outer)  2.23 us
    ppermute x1, starting transfers between devices, on_device(): inner1 = lax.ppermute(features, AXES, inner)  1.42 us
  transfers between devices with their start and end apart: 5, of which 2 were waited for; matrix products, arithmetic and copies ran while one was open for 5% of the time, Pallas kernels for 0%

profile of v7, /device:TPU:1, one launch (start us, length us, event | category | flops | bytes accessed | tf_op | source)
XLA Modules:
  0.0 67.3 jit_solution(622563651087630145)
XLA Ops:
  0.0 0.0 copy-start.2
  0.0 0.0 copy-start.1
  0.0 0.0 copy-start
  0.0 1.4 %collective-permute-start = (bf16[16,512]{1,0:T(8,128)(2,1)}, bf16[16,512]{1,0:T(8,128)(2,1)S(1)}, u32[]{:S(2)}, u32[]{:S(2)}) collective-permute-start(bf16[16,512]{1,0:T(8,128)(2,1)} %param.9), channel_id=1, source_target_pairs={{0,1},{1,0},{2,3},{3,2},{4,5},{5,4},{6,7},{7,6},{8,9},{9,8},{10,11... | collective-permute-start | bytes 49160 | tf_op jit(solution)/shard_map/ppermute | solution.py:338
  1.4 3.3 %collective-permute-start.1 = (bf16[16,512]{1,0:T(8,128)(2,1)}, bf16[16,512]{1,0:T(8,128)(2,1)S(1)}, u32[]{:S(2)}, u32[]{:S(2)}) collective-permute-start(bf16[16,512]{1,0:T(8,128)(2,1)} %param.9), channel_id=1, source_target_pairs={{1,2},{2,1},{3,4},{4,3},{5,6},{6,5},{7,8},{8,7},{9,10},{10,9},{11,... | collective-permute-start | bytes 49160 | tf_op jit(solution)/shard_map/ppermute | solution.py:339
  5.4 0.8 %pad_maximum_fusion.near = bf16[80,512]{1,0:T(8,128)(2,1)S(1)} fusion(bf16[64,512]{1,0:T(8,128)(2,1)} %bitcast.20, bf16[16,512]{1,0:T(8,128)(2,1)} %param.9), kind=kLoop, calls=%fused_computation.29 | loop fusion | flops 163840 | bytes 163840 | tf_op jit(solution)/shard_map/concatenate | solution.py:345
  6.3 0.1 multiply_cosine_fusion
  6.4 0.1 select_maximum_fusion
  6.5 0.0 collective-permute-done.inner1
  6.5 2.2 %collective-permute-start.3 = (bf16[16,512]{1,0:T(8,128)(2,1)S(1)}, bf16[16,512]{1,0:T(8,128)(2,1)S(1)}, u32[]{:S(2)}, u32[]{:S(2)}) collective-permute-start(bf16[16,512]{1,0:T(8,128)(2,1)S(1)} %collective-permute-done.inner1), channel_id=1, source_target_pairs={{1,2},{2,1},{3,4},{4,3},{5,6},{6,5},{7,8},{8,7},{9,10},{10,9},{11,... | collective-permute-start | bytes 49160 | tf_op jit(solution)/shard_map/ppermute | solution.py:340
  8.7 0.0 collective-permute-done.1.outer1
  8.7 0.1 collective-permute-start.2
  8.8 0.7 %pad_maximum_fusion.1.extra = f32[18,512]{1,0:T(8,128)S(1)} fusion(f32[16,512]{1,0:T(8,128)S(1)} %select_maximum_fusion, f32[2,512]{1,0:T(2,128)} %param.11), kind=kLoop, calls=%fused_computation.34 | loop fusion | flops 9216 | bytes 73728 | tf_op jit(solution)/shard_map/concatenate | solution.py:344
  9.5 0.7 %concatenate.27.place = s32[10]{0:T(128)S(1)} concatenate(s32[1]{0:T(128)} %bitcast, s32[1]{0:T(128)} %bitcast.1, s32[1]{0:T(128)} %bitcast.2, s32[1]{0:T(128)} %constant.29.clone.1, s32[1]{0:T(128)} %constant.30.clone.1, s32[5]{0:T(128)} %param.16), dimensions={0} | concatenate | bytes 80 | tf_op jit(solution)/shard_map/concatenate | solution.py:334
  10.3 1.3 %collective-permute-done.3.outer2 = bf16[16,512]{1,0:T(8,128)(2,1)S(1)} collective-permute-done((bf16[16,512]{1,0:T(8,128)(2,1)S(1)}, bf16[16,512]{1,0:T(8,128)(2,1)S(1)}, u32[]{:S(2)}, u32[]{:S(2)}) %collective-permute-start.3) | collective-permute-done | bytes 16416 | tf_op jit(solution)/shard_map/ppermute | solution.py:340
  11.5 0.0 collective-permute-done.2.inner2
  11.5 3.5 %encode.1 = (bf16[128,8,128]{2,1,0:T(8,128)(2,1)}, bf16[3,3,3,32,32]{4,3,2,1,0:T(8,128)(2,1)S(1)}, f32[4,32]{1,0:T(4,128)S(1)}) custom-call(s32[10]{0:T(128)S(1)} %concatenate.27.place, bf16[16,512]{1,0:T(8,128)(2,1)S(1)} %collective-permute-done.inner1, bf16[16,512]{1,0:T(8,128)(2,1)S(1)} %collective-permute-done.1.outer1, ...), custom_call_target="tpu_custom_call" | custom-call | flops 100663296 | bytes 3145728 | tf_op jit(solution)/shard_map/encode/pallas_call | solution.py:349
  15.1 0.0 copy-done.2
  15.1 0.0 copy-done.1
  15.1 13.4 %all-to-all-start = ((bf16[128,8,128]{2,1,0:T(8,128)(2,1)}), bf16[128,8,128]{2,1,0:T(8,128)(2,1)S(1)}, u32[]{:S(2)}, u32[]{:S(2)}) async-start(bf16[128,8,128]{2,1,0:T(8,128)(2,1)} %get-tuple-element.8), calls=%async_computation | async-start | bytes 524288 | tf_op jit(solution)/shard_map/all_to_all | solution.py:375
  28.6 0.1 copy.30.gain
  28.7 0.1 copy.27
  28.8 0.1 copy.28
  28.9 0.1 copy.29
  29.0 0.0 copy-done
  29.1 0.2 copy.26
  29.2 0.2 reshape.31
  29.4 0.1 fusion.25
  29.5 0.2 fusion.19.weight
  29.7 9.9 %all-to-all-done.parts = bf16[128,8,128]{2,1,0:T(8,128)(2,1)S(1)} async-done(((bf16[128,8,128]{2,1,0:T(8,128)(2,1)}), bf16[128,8,128]{2,1,0:T(8,128)(2,1)S(1)}, u32[]{:S(2)}, u32[]{:S(2)}) %all-to-all-start) | async-done | bytes 262176 | tf_op jit(solution)/shard_map/all_to_all | solution.py:375
  39.6 27.8 %pair_tower.1 = bf16[32,256,128]{2,1,0:T(8,128)(2,1)} custom-call(s32[10]{0:T(128)S(1)} %concatenate.27.place, bf16[128,8,128]{2,1,0:T(8,128)(2,1)S(1)} %all-to-all-done.parts, f32[32,1]{1,0:T(8,128)S(1)} %copy.30.gain, bf16[3,128,608]{2,1,0:T(8,128)(2,1)S(1)} %fusion.19.weight), custom_call_target="tpu_custom_call" | custom-call | flops 3623878656 | bytes 2097152 | tf_op jit(solution)/shard_map/pair_tower/pallas_call | solution.py:286
  (5 shorter events, 0.1 us)
Async XLA Ops:
  0.0 15.1 %copy-start.2 = (f32[32]{0:T(128)S(1)}, f32[32]{0:T(128)}, u32[]{:S(2)}) copy-start(f32[32]{0:T(128)} %param.13) | copy-start | bytes 388
  0.0 15.1 %copy-start.1 = (f32[3,32]{1,0:T(4,128)S(1)}, f32[3,32]{1,0:T(4,128)}, u32[]{:S(2)}) copy-start(f32[3,32]{1,0:T(4,128)} %param.15) | copy-start | bytes 1156
  0.0 29.0 %copy-start = (bf16[3,3,3,32,32]{4,3,2,1,0:T(8,128)(2,1)S(1)}, bf16[3,3,3,32,32]{4,3,2,1,0:T(8,128)(2,1)}, u32[]{:S(2)}) copy-start(bf16[3,3,3,32,32]{4,3,2,1,0:T(8,128)(2,1)} %param.14) | copy-start | bytes 165892
  0.0 6.5 %collective-permute-start = (bf16[16,512]{1,0:T(8,128)(2,1)}, bf16[16,512]{1,0:T(8,128)(2,1)S(1)}, u32[]{:S(2)}, u32[]{:S(2)}) collective-permute-start(bf16[16,512]{1,0:T(8,128)(2,1)} %param.9), channel_id=1, source_target_pairs={{0,1},{1,0},{2,3},{3,2},{4,5},{5,4},{6,7},{7,6},{8,9},{9,8},{10,11... | collective-permute-start | bytes 49160 | tf_op jit(solution)/shard_map/ppermute | solution.py:338
  1.4 7.3 %collective-permute-start.1 = (bf16[16,512]{1,0:T(8,128)(2,1)}, bf16[16,512]{1,0:T(8,128)(2,1)S(1)}, u32[]{:S(2)}, u32[]{:S(2)}) collective-permute-start(bf16[16,512]{1,0:T(8,128)(2,1)} %param.9), channel_id=1, source_target_pairs={{1,2},{2,1},{3,4},{4,3},{5,6},{6,5},{7,8},{8,7},{9,10},{10,9},{11,... | collective-permute-start | bytes 49160 | tf_op jit(solution)/shard_map/ppermute | solution.py:339
  6.5 5.0 %collective-permute-start.3 = (bf16[16,512]{1,0:T(8,128)(2,1)S(1)}, bf16[16,512]{1,0:T(8,128)(2,1)S(1)}, u32[]{:S(2)}, u32[]{:S(2)}) collective-permute-start(bf16[16,512]{1,0:T(8,128)(2,1)S(1)} %collective-permute-done.inner1), channel_id=1, source_target_pairs={{1,2},{2,1},{3,4},{4,3},{5,6},{6,5},{7,8},{8,7},{9,10},{10,9},{11,... | collective-permute-start | bytes 49160 | tf_op jit(solution)/shard_map/ppermute | solution.py:340
  8.7 2.8 %collective-permute-start.2 = (bf16[16,512]{1,0:T(8,128)(2,1)S(1)}, bf16[16,512]{1,0:T(8,128)(2,1)S(1)}, u32[]{:S(2)}, u32[]{:S(2)}) collective-permute-start(bf16[16,512]{1,0:T(8,128)(2,1)S(1)} %collective-permute-done.1.outer1), channel_id=1, source_target_pairs={{0,1},{1,0},{2,3},{3,2},{4,5},{5,4},{6,7},{7,6},{8,9},{9,8},{10,11... | collective-permute-start | bytes 49160 | tf_op jit(solution)/shard_map/ppermute | solution.py:341
  15.1 24.4 %all-to-all-start = ((bf16[128,8,128]{2,1,0:T(8,128)(2,1)}), bf16[128,8,128]{2,1,0:T(8,128)(2,1)S(1)}, u32[]{:S(2)}, u32[]{:S(2)}) async-start(bf16[128,8,128]{2,1,0:T(8,128)(2,1)} %get-tuple-element.8), calls=%async_computation | async-start | bytes 524288 | tf_op jit(solution)/shard_map/all_to_all | solution.py:375

commit v8 on v7

--- a/solution.py
+++ b/solution.py
@@ -16,6 +16,7 @@
 UNROLL = 4
 LANES = 256
 PITCH = 40
+CHUNK = 64
 OUTSIDE = -1e30
 AXES = ("rows", "cols")
 
@@ -29,12 +30,11 @@
 
 
 def encode_kernel(
-    total, place, inner1, outer1, inner2, outer2, near, extra, weight_far, out, none_16, none_32,
+    total, place, both, outer, inner, proj, extra, weight_far, out, none_16, none_32,
     weight, wide, mid, arrived,
 ):
-    count = inner1.shape[0]
+    count = both.shape[0] // 2
     bias = extra[:2, :]
-    proj = near[count:, :]
     fetch = [
         [
             pltpu.make_async_copy(
@@ -64,32 +64,45 @@
         return run(ref, count, span) + jnp.maximum(running + bias[which : which + 1, :], 0.0)
 
     odd = place[0] % 2
-    for side, ref in ((2, near), (3 - 2 * odd, inner1), (1 + 2 * odd, outer1),
-                      (4 - 4 * odd, inner2), (4 * odd, outer2)):
+    for side, ref, half in ((2, both, 0), (3 - 2 * odd, both, 1), (1 + 2 * odd, outer, 0),
+                            (4 * odd, outer, 1), (4 - 4 * odd, inner, 0)):
         first = side * count
-        if ref is not near:
+        if ref is not both or half:
             first = pl.multiple_of(first, count)
-        keep(wide, first, ref[:count, :].astype(jnp.float32))
+        keep(wide, first, ref[half * count : (half + 1) * count, :].astype(jnp.float32))
     value = layer(0, wide, 3 * count).astype(jnp.bfloat16).astype(jnp.float32)
     index = (place[0] - 1) * count + lax.broadcasted_iota(jnp.int32, value.shape, 0)
     keep(mid, 0, jnp.where((index >= 0) & (index < total), value, 0.0))
     value = layer(1, mid, count)
     parts = lax.dot_general(
         value.astype(jnp.bfloat16),
-        proj,
+        proj[...],
         (((1,), (1,)), ((), ())),
         preferred_element_type=jnp.float32,
     )
     parts = (parts + extra[2 : 2 + count, : proj.shape[0]]).astype(jnp.bfloat16)
+    parts = parts[:, : proj.shape[0] // 2]
     parts = jnp.concatenate([parts[: count // 2], parts[count // 2 :]], axis=1)
     out[...] = jnp.broadcast_to(parts[None], out.shape)
     none_16[...] = jnp.zeros(none_16.shape, none_16.dtype)
     none_32[...] = jnp.zeros(none_32.shape, none_32.dtype)
 
 
+def local_columns(rows):
+    lane = lax.broadcasted_iota(jnp.int32, (rows, LANES), 1)
+    return jnp.where(lane < LANES - 3 * DMAX2 - 8, lane, lane - LANES)
+
+
+def distance_kernel(tile_rows, place, none, out):
+    row_first = place[1] * tile_rows - 3 * DMAX2
+    row = row_first + lax.broadcasted_iota(jnp.int32, out.shape, 0)
+    apart = jnp.abs(row - (place[2] * 128 + local_columns(out.shape[0])))
+    out[...] = jnp.log(1.0 + apart.astype(jnp.float32)) * 0.125 + none[0, 0]
+
+
 def pair_kernel(
-    total_shards, first_dil, place, parts, gain, weight, out,
-    row_turned, distance, field_a, field_b, final, held,
+    total_shards, first_dil, place, parts, distance, gain, weight, out_far,
+    row_turned, field_a, field_b, final, held, out, sent,
 ):
     shard = 2 * parts.shape[1]
     chans = gain.shape[0]
@@ -110,9 +123,7 @@
             taken += [both[:, : 2 * chans], both[:, 2 * chans :]]
         return jnp.concatenate(taken, axis=0).astype(jnp.float32)
 
-    lane = lax.broadcasted_iota(jnp.int32, (1, LANES), 1)
-    col_local = jnp.where(lane < LANES - margin - 8, lane, lane - LANES)
-    col_glob = col_first + col_local
+    col_glob = col_first + local_columns(1)
     inside = (col_glob >= 0) & (col_glob < total_shards * shard)
     inside_high = jnp.where(inside[:, 128:], 1.0, 0.0)
     inside_high = jnp.broadcast_to(inside_high, (chans, 128)).astype(jnp.bfloat16)
@@ -129,9 +140,6 @@
     for k in range(blocks):
         row_turned[k] = rows[:, k * 128 : (k + 1) * 128]
 
-    row_local = lax.broadcasted_iota(jnp.int32, (span0, LANES), 0) - margin
-    apart = jnp.abs(row_first + row_local - col_glob)
-    distance[...] = jnp.log(1.0 + apart.astype(jnp.float32)) * 0.125
     gain_wide = jnp.broadcast_to(gain[...], (chans, LANES))
     lane16 = lax.broadcasted_iota(jnp.int16, (chans, 128), 1)
 
@@ -189,7 +197,7 @@
 
     tail = jnp.ones((TAIL, WIDE * LANES), jnp.bfloat16)
 
-    def tower(layer, source, extra, need, store):
+    def tower(layer, source, extra, need, store, first_in_step=None):
         d = dils[layer]
         span = GROUP * d
         first = extra - need
@@ -227,8 +235,10 @@
                 phase = jnp.where(wrap, 0, phase + 1)
             return bases, start, phase
 
-        def step(_, carry):
+        def step(index, carry):
             start, phase, bases = carry
+            if first_in_step is not None:
+                first_in_step(index)
             sums = held
             for k in range(UNROLL):
                 next_bases, start, phase = walk(start, phase)
@@ -247,18 +257,36 @@
     def keep_last(i, low):
         final[pl.ds(pl.multiple_of(i * PITCH, 8), chans), :] = low
 
+    def turn(chunk):
+        @functools.partial(lax.fori_loop, 0, CHUNK // 16, init_val=0, unroll=True)
+        def _(block, carry):
+            first = pl.multiple_of(chunk * CHUNK + block * 16, 16)
+            for c in range(chans):
+                taken = final[pl.ds(first * PITCH + c, 16, stride=PITCH), :]
+                out[c, pl.ds(first, 16), :] = taken.astype(jnp.bfloat16)
+            return carry
+
+    def send(chunk):
+        rows = pl.ds(chunk * CHUNK, CHUNK)
+        return pltpu.make_async_copy(out.at[:, rows, :], out_far.at[:, rows, :], sent.at[chunk])
+
+    early = 2
+
+    def turn_early(step):
+        turn(jnp.clip(step - 2, 0, early - 1))
+
     tower(0, field_a, 2 * DMAX2, dils[1] + dils[2], keep(field_b, dils[1], True))
     clear(field_b, 2 * DMAX2)
     tower(1, field_b, DMAX2, dils[2], keep(field_a, dils[2], True))
     clear(field_a, DMAX2)
-    tower(2, field_a, 0, 0, keep_last)
-
-    @pl.loop(0, tile_rows // 16)
-    def _(block):
-        first = pl.multiple_of(block * 16, 16)
-        for c in range(chans):
-            taken = final[pl.ds(first * PITCH + c, 16, stride=PITCH), :]
-            out[c, pl.ds(first, 16), :] = taken.astype(jnp.bfloat16)
+    tower(2, field_a, 0, 0, keep_last, turn_early)
+
+    for k in range(tile_rows // CHUNK):
+        if k >= early:
+            turn(k)
+        send(k).start()
+    for k in range(tile_rows // CHUNK):
+        send(k).wait()
 
 
 def banded(map_weight, map_bias):
@@ -278,7 +306,20 @@
     return jnp.concatenate(rows, axis=1)
 
 
-def pair_call(place, gathered, dist_gain, bands, tile_rows, tile_cols):
+def distance_call(place, none, tile_rows):
+    return pl.pallas_call(
+        functools.partial(distance_kernel, tile_rows),
+        out_shape=jax.ShapeDtypeStruct((tile_rows + 6 * DMAX2, LANES), jnp.float32),
+        in_specs=[
+            pl.BlockSpec(memory_space=pltpu.SMEM),
+            pl.BlockSpec(memory_space=pltpu.VMEM),
+        ],
+        out_specs=pl.BlockSpec(memory_space=pltpu.VMEM),
+        name="distances",
+    )(place, none)
+
+
+def pair_call(place, gathered, distance, dist_gain, bands, tile_rows, tile_cols):
     chans = dist_gain.shape[0]
     smem = pl.BlockSpec(memory_space=pltpu.SMEM)
     vmem = pl.BlockSpec(memory_space=pltpu.VMEM)
@@ -286,15 +327,16 @@
     return pl.pallas_call(
         functools.partial(pair_kernel, gathered.shape[0], place.shape[0] - 3),
         out_shape=jax.ShapeDtypeStruct((chans, tile_rows, tile_cols), jnp.bfloat16),
-        in_specs=[smem] + [vmem] * 3,
-        out_specs=vmem,
+        in_specs=[smem] + [vmem] * 4,
+        out_specs=pl.BlockSpec(memory_space=pltpu.HBM),
         scratch_shapes=[
             pltpu.VMEM((-(-span // 128), chans, 128), jnp.float32),
-            pltpu.VMEM((span, LANES), jnp.float32),
             pltpu.VMEM((span, 3 * chans, LANES), jnp.bfloat16),
             pltpu.VMEM((span - 2 * DMAX2, 3 * chans, LANES), jnp.bfloat16),
             pltpu.VMEM((tile_rows * PITCH, 128), jnp.float32),
             pltpu.VMEM((GROUP * chans, WIDE * LANES), jnp.float32),
+            pltpu.VMEM((chans, tile_rows, tile_cols), jnp.bfloat16),
+            pltpu.SemaphoreType.DMA((tile_rows // CHUNK,)),
         ],
         compiler_params=pltpu.CompilerParams(vmem_limit_bytes=48 * 2**20),
         cost_estimate=pl.CostEstimate(
@@ -304,7 +346,7 @@
         ),
         name="pair_tower",
     )(
-        place, gathered, dist_gain.reshape(chans, 1), bands,
+        place, gathered, distance, dist_gain.reshape(chans, 1), bands,
     )
 
 
@@ -335,14 +377,13 @@
 
     inner = [(i, i ^ 1) for i in range(shards)]
     outer = [(i, i + 1 if i % 2 else i - 1) for i in range(1, shards - 1)]
-    inner1 = lax.ppermute(features, AXES, inner)
-    outer1 = lax.ppermute(features, AXES, outer)
-    outer2 = lax.ppermute(inner1, AXES, outer)
-    inner2 = lax.ppermute(outer1, AXES, inner)
+    both = jnp.concatenate([features, lax.ppermute(features, AXES, inner)], axis=0)
+    from_outer = lax.ppermute(both, AXES, outer)
+    from_inner = lax.ppermute(from_outer, AXES, inner)
     code = position_code(mine * shard + jnp.arange(shard), start_bin[0], chans)
     code = jnp.pad(code, ((0, 0), (0, width - chans)))
     extra = jnp.concatenate([tower_bias, code], axis=0)
-    near = jnp.concatenate([features, pair_proj.T], axis=0)
+    proj = jnp.pad(pair_proj.T, ((0, 2 * chans), (0, 0)))
 
     smem = pl.BlockSpec(memory_space=pltpu.SMEM)
     vmem = pl.BlockSpec(memory_space=pltpu.VMEM)
@@ -353,7 +394,7 @@
             jax.ShapeDtypeStruct(map_weight.shape, map_weight.dtype),
             jax.ShapeDtypeStruct((map_bias.shape[0] + 1, chans), jnp.float32),
         ],
-        in_specs=[smem] + [vmem] * 6 + [pl.BlockSpec(memory_space=pltpu.HBM)],
+        in_specs=[smem] + [vmem] * 5 + [pl.BlockSpec(memory_space=pltpu.HBM)],
         out_specs=[vmem] * 3,
         scratch_shapes=[
             pltpu.VMEM(tower_weight.shape, tower_weight.dtype),
@@ -369,7 +410,7 @@
         ),
         name="encode",
     )(
-        place, inner1, outer1, inner2, outer2, near, extra, tower_weight,
+        place, both, from_outer, from_inner, proj, extra, tower_weight,
     )
 
     gathered = lax.all_to_all(parts, AXES, split_axis=0, concat_axis=0, tiled=True)
@@ -377,8 +418,9 @@
     bands = banded(map_weight + none_16, map_bias + none_32[:-1])
     dist_gain = dist_gain + none_32[-1]
 
+    distance = distance_call(place, none_32, tile_rows)
     return pair_call(
-        place, gathered, dist_gain, bands, tile_rows, tile_cols
+        place, gathered, distance, dist_gain, bands, tile_rows, tile_cols
     )
 
 

time: 67.8 us -> 72.1 us (1.063)
  local copies, waits for them, and re-layouts: 1.52 us -> 5.34 us
  starting transfers between devices: 20.5 us -> 18 us
  Pallas kernels: 31.3 us -> 33.2 us
    unnamed x6 -> x15, local copies, waits for them, and re-layouts: 0.01 us -> 2.97 us
    ppermute x4 -> x3, starting transfers between devices: 7.05 us -> 4.63 us  [the longest x1 3.21 us: on_device(): from_outer = lax.ppermute(both, AXES, outer)]
    pallas_call x0 -> x1, Pallas kernels: none -> 1.54 us  [distance_call(): pl.pallas_call(functools.partial(distance_kernel, tile_rows), out_shape=j...]
    concatenate x1 -> x0, other arithmetic: 0.85 us -> none  [on_device(): near = jnp.concatenate([features, pair_proj.T], axis=0)]
    pad x0 -> x1, local copies, waits for them, and re-layouts: none -> 0.85 us  [on_device(): proj = jnp.pad(pair_proj.T, ((0, 2 * chans), (0, 0)))]
    ppermute x4 -> x3, waiting for transfers between devices: 1.29 us -> 1.93 us  [the longest x1 1.92 us: on_device(): from_outer = lax.ppermute(both, AXES, outer)]
  transfers between devices with their start and end apart: 5 -> 4, of which waited for: 2 -> 2; matrix products, arithmetic and copies ran while one was open for 5% -> 6% of each run, Pallas kernels for 0% -> 0%
where the time goes in v8:
time: 72.1 us; the launch traced here: 71.7 us
  Pallas kernels  33.2 us (46%)
  starting transfers between devices  18 us (25%)
  waiting for transfers between devices  11.8 us (16%)
  local copies, waits for them, and re-layouts  5.34 us (7%)
  other arithmetic  2.53 us (4%)
  between operations  0.76 us (1%)
    pallas_call x1, Pallas kernels, pair_call(): pl.pallas_call(functools.partial(pair_kernel, gathered.shape[0], place.sh...  28.1 us
    all_to_all x1, starting transfers between devices, on_device(): lax.all_to_all(parts, AXES, split_axis=0, concat_axis=0, tiled=True)  13.4 us
    all_to_all x1, waiting for transfers between devices, on_device(): lax.all_to_all(parts, AXES, split_axis=0, concat_axis=0, tiled=True)  9.87 us
    pallas_call x1, Pallas kernels, on_device(): pl.pallas_call(functools.partial(encode_kernel, total), out_shape=[jax.Sh...  3.57 us
    ppermute x1, starting transfers between devices, on_device(): from_outer = lax.ppermute(both, AXES, outer)  3.21 us
    unnamed x15, local copies, waits for them, and re-layouts  2.97 us
    ppermute x1, waiting for transfers between devices, on_device(): from_outer = lax.ppermute(both, AXES, outer)  1.92 us
    pallas_call x1, Pallas kernels, distance_call(): pl.pallas_call(functools.partial(distance_kernel, tile_rows), out_shape=j...  1.54 us
  transfers between devices with their start and end apart: 4, of which 2 were waited for; matrix products, arithmetic and copies ran while one was open for 6% of the time, Pallas kernels for 0%

profile of v8, /device:TPU:1, one launch (start us, length us, event | category | flops | bytes accessed | tf_op | source)
XLA Modules:
  0.0 71.7 jit_solution(3692920166733152615)
XLA Ops:
  0.0 0.0 copy-start.6
  0.0 0.0 copy-start.5
  0.0 0.0 copy-start.4
  0.0 1.4 %collective-permute-start = (bf16[16,512]{1,0:T(8,128)(2,1)}, bf16[16,512]{1,0:T(8,128)(2,1)S(1)}, u32[]{:S(2)}, u32[]{:S(2)}) collective-permute-start(bf16[16,512]{1,0:T(8,128)(2,1)} %param.9), channel_id=1, source_target_pairs={{0,1},{1,0},{2,3},{3,2},{4,5},{5,4},{6,7},{7,6},{8,9},{9,8},{10,11... | collective-permute-start | bytes 49160 | tf_op jit(solution)/shard_map/ppermute | solution.py:380
  2.1 0.1 multiply_cosine_fusion
  2.2 0.7 %constant_dynamic-update-slice_fusion.1 = bf16[32,512]{1,0:T(8,128)(2,1)S(1)} fusion(bf16[16,512]{1,0:T(8,128)(2,1)} %param.9), kind=kLoop, calls=%fused_computation.41 | loop fusion | bytes 32768
  3.0 0.0 collective-permute-done
  3.0 3.2 %collective-permute-start.1 = (bf16[32,512]{1,0:T(8,128)(2,1)S(1)}, bf16[32,512]{1,0:T(8,128)(2,1)S(1)}, u32[]{:S(2)}, u32[]{:S(2)}) collective-permute-start(bf16[32,512]{1,0:T(8,128)(2,1)S(1)} %constant_dynamic-update-slice_fusion.both), channel_id=1, source_target_pairs={{1,2},{2,1},{3,4},{4,3},{5,6},{6,5},{7,8},{8,7},{9,10},{10,9},{11,... | collective-permute-start | bytes 98312 | tf_op jit(solution)/shard_map/ppermute | solution.py:381
  6.2 0.1 select_maximum_fusion
  6.3 1.9 %collective-permute-done.1.outer = bf16[32,512]{1,0:T(8,128)(2,1)S(1)} collective-permute-done((bf16[32,512]{1,0:T(8,128)(2,1)S(1)}, bf16[32,512]{1,0:T(8,128)(2,1)S(1)}, u32[]{:S(2)}, u32[]{:S(2)}) %collective-permute-start.1) | collective-permute-done | bytes 32800 | tf_op jit(solution)/shard_map/ppermute | solution.py:381
  8.2 0.0 collective-permute-start.2
  8.2 0.7 pad_maximum_fusion.extra
  8.9 0.8 %pad.31.proj = bf16[128,512]{1,0:T(8,128)(2,1)S(1)} pad(bf16[64,512]{1,0:T(8,128)(2,1)} %bitcast.20, bf16[]{:T(256)} %constant.31.clone.1), padding=0_64x0_0 | pad | bytes 196610 | tf_op jit(solution)/shard_map/jit(_pad)/pad | solution.py:386
  9.7 0.7 %concatenate.27.place = s32[10]{0:T(128)S(1)} concatenate(s32[1]{0:T(128)} %bitcast, s32[1]{0:T(128)} %bitcast.1, s32[1]{0:T(128)} %bitcast.2, s32[1]{0:T(128)} %constant.29.clone.1, s32[1]{0:T(128)} %constant.30.clone.1, s32[5]{0:T(128)} %param.16), dimensions={0} | concatenate | bytes 80 | tf_op jit(solution)/shard_map/concatenate | solution.py:376
  10.5 0.0 copy-start.2
  10.5 0.0 collective-permute-done.2.inner
  10.5 3.6 %encode.1 = (bf16[128,8,128]{2,1,0:T(8,128)(2,1)}, bf16[3,3,3,32,32]{4,3,2,1,0:T(8,128)(2,1)S(1)}, f32[4,32]{1,0:T(4,128)S(1)}) custom-call(s32[10]{0:T(128)S(1)} %concatenate.27.place, bf16[32,512]{1,0:T(8,128)(2,1)S(1)} %constant_dynamic-update-slice_fusion.both, bf16[32,512]{1,0:T(8,128)(2,1)S(1)} %collective-permute-done.1.outer, ...), custom_call_target="tpu_custom_call" | custom-call | flops 100663296 | bytes 3145728 | tf_op jit(solution)/shard_map/encode/pallas_call | solution.py:390
  14.1 0.0 copy-start.1
  14.1 0.6 copy-done.1
  14.6 0.0 copy-done.2
  14.6 1.5 %distances.1.distance = f32[352,256]{1,0:T(8,128)} custom-call(s32[10]{0:T(128)} %copy-done.2, f32[4,32]{1,0:T(4,128)} %copy-done.1), custom_call_target="tpu_custom_call" | custom-call | tf_op jit(solution)/shard_map/distances/pallas_call | solution.py:310
  16.2 0.0 copy-done.6
  16.2 0.7 fusion.33
  16.8 0.0 copy-done.5
  16.9 0.7 fusion.28
  17.5 13.4 %all-to-all-start = ((bf16[128,8,128]{2,1,0:T(8,128)(2,1)}), bf16[128,8,128]{2,1,0:T(8,128)(2,1)S(1)}, u32[]{:S(2)}, u32[]{:S(2)}) async-start(bf16[128,8,128]{2,1,0:T(8,128)(2,1)} %get-tuple-element.8), calls=%async_computation | async-start | bytes 524288 | tf_op jit(solution)/shard_map/all_to_all | solution.py:416
  30.9 0.1 copy.30.gain
  31.0 0.1 copy.27
  31.1 0.1 copy.28
  31.3 0.1 copy.29
  31.4 0.0 copy-done.4
  31.4 0.2 copy.26
  31.6 0.2 reshape.31
  31.8 0.1 fusion.25
  31.9 0.2 fusion.19.weight
  32.0 9.9 %all-to-all-done.parts = bf16[128,8,128]{2,1,0:T(8,128)(2,1)S(1)} async-done(((bf16[128,8,128]{2,1,0:T(8,128)(2,1)}), bf16[128,8,128]{2,1,0:T(8,128)(2,1)S(1)}, u32[]{:S(2)}, u32[]{:S(2)}) %all-to-all-start) | async-done | bytes 262176 | tf_op jit(solution)/shard_map/all_to_all | solution.py:416
  41.9 0.0 copy-start
  41.9 1.0 %copy-done = f32[352,256]{1,0:T(8,128)S(1)} copy-done((f32[352,256]{1,0:T(8,128)S(1)}, f32[352,256]{1,0:T(8,128)}, u32[]{:S(2)}) %copy-start) | copy-done | bytes 360472
  42.9 0.0 copy-start.3
  42.9 0.7 copy-done.3
  43.6 28.1 %pair_tower.1 = bf16[32,256,128]{2,1,0:T(8,128)(2,1)} custom-call(s32[10]{0:T(128)S(1)} %copy-done.3, bf16[128,8,128]{2,1,0:T(8,128)(2,1)S(1)} %all-to-all-done.parts, f32[352,256]{1,0:T(8,128)S(1)} %copy-done, f32[32,1]{1,0:T(8,128)S(1)} %copy.30.gain, bf16[3,128,608]{2,1,0:T(8,128)(2,1)S(1)} %fusion.19.weight), custom_call_target="tpu_custom_call" | custom-call | flops 3623878656 | bytes 2097152 | tf_op jit(solution)/shard_map/pair_tower/pallas_call | solution.py:327
  (4 shorter events, 0.0 us)
Async XLA Ops:
  0.0 16.2 %copy-start.6 = (f32[32]{0:T(128)S(1)}, f32[32]{0:T(128)}, u32[]{:S(2)}) copy-start(f32[32]{0:T(128)} %param.13) | copy-start | bytes 388
  0.0 16.8 %copy-start.5 = (f32[3,32]{1,0:T(4,128)S(1)}, f32[3,32]{1,0:T(4,128)}, u32[]{:S(2)}) copy-start(f32[3,32]{1,0:T(4,128)} %param.15) | copy-start | bytes 1156
  0.0 31.4 %copy-start.4 = (bf16[3,3,3,32,32]{4,3,2,1,0:T(8,128)(2,1)S(1)}, bf16[3,3,3,32,32]{4,3,2,1,0:T(8,128)(2,1)}, u32[]{:S(2)}) copy-start(bf16[3,3,3,32,32]{4,3,2,1,0:T(8,128)(2,1)} %param.14) | copy-start | bytes 165892
  0.0 2.9 %collective-permute-start = (bf16[16,512]{1,0:T(8,128)(2,1)}, bf16[16,512]{1,0:T(8,128)(2,1)S(1)}, u32[]{:S(2)}, u32[]{:S(2)}) collective-permute-start(bf16[16,512]{1,0:T(8,128)(2,1)} %param.9), channel_id=1, source_target_pairs={{0,1},{1,0},{2,3},{3,2},{4,5},{5,4},{6,7},{7,6},{8,9},{9,8},{10,11... | collective-permute-start | bytes 49160 | tf_op jit(solution)/shard_map/ppermute | solution.py:380
  3.0 5.2 %collective-permute-start.1 = (bf16[32,512]{1,0:T(8,128)(2,1)S(1)}, bf16[32,512]{1,0:T(8,128)(2,1)S(1)}, u32[]{:S(2)}, u32[]{:S(2)}) collective-permute-start(bf16[32,512]{1,0:T(8,128)(2,1)S(1)} %constant_dynamic-update-slice_fusion.both), channel_id=1, source_target_pairs={{1,2},{2,1},{3,4},{4,3},{5,6},{6,5},{7,8},{8,7},{9,10},{10,9},{11,... | collective-permute-start | bytes 98312 | tf_op jit(solution)/shard_map/ppermute | solution.py:381
  8.2 2.3 %collective-permute-start.2 = (bf16[32,512]{1,0:T(8,128)(2,1)S(1)}, bf16[32,512]{1,0:T(8,128)(2,1)S(1)}, u32[]{:S(2)}, u32[]{:S(2)}) collective-permute-start(bf16[32,512]{1,0:T(8,128)(2,1)S(1)} %collective-permute-done.1.outer), channel_id=1, source_target_pairs={{0,1},{1,0},{2,3},{3,2},{4,5},{5,4},{6,7},{7,6},{8,9},{9,8},{10,11... | collective-permute-start | bytes 98312 | tf_op jit(solution)/shard_map/ppermute | solution.py:382
  10.5 4.2 %copy-start.2 = (s32[10]{0:T(128)}, s32[10]{0:T(128)S(1)}, u32[]{:S(2)}) copy-start(s32[10]{0:T(128)S(1)} %concatenate.27.place) | copy-start | bytes 124
  14.1 0.6 copy-start.1
  17.5 24.4 %all-to-all-start = ((bf16[128,8,128]{2,1,0:T(8,128)(2,1)}), bf16[128,8,128]{2,1,0:T(8,128)(2,1)S(1)}, u32[]{:S(2)}, u32[]{:S(2)}) async-start(bf16[128,8,128]{2,1,0:T(8,128)(2,1)} %get-tuple-element.8), calls=%async_computation | async-start | bytes 524288 | tf_op jit(solution)/shard_map/all_to_all | solution.py:416
  41.9 1.0 %copy-start = (f32[352,256]{1,0:T(8,128)S(1)}, f32[352,256]{1,0:T(8,128)}, u32[]{:S(2)}) copy-start(f32[352,256]{1,0:T(8,128)} %distances.1.distance) | copy-start | bytes 1081348
  42.9 0.7 copy-start.3

commit v9 on v8

--- a/solution.py
+++ b/solution.py
@@ -93,16 +93,9 @@
     return jnp.where(lane < LANES - 3 * DMAX2 - 8, lane, lane - LANES)
 
 
-def distance_kernel(tile_rows, place, none, out):
-    row_first = place[1] * tile_rows - 3 * DMAX2
-    row = row_first + lax.broadcasted_iota(jnp.int32, out.shape, 0)
-    apart = jnp.abs(row - (place[2] * 128 + local_columns(out.shape[0])))
-    out[...] = jnp.log(1.0 + apart.astype(jnp.float32)) * 0.125 + none[0, 0]
-
-
 def pair_kernel(
-    total_shards, first_dil, place, parts, distance, gain, weight, out_far,
-    row_turned, field_a, field_b, final, held, out, sent,
+    total_shards, first_dil, place, parts, gain, weight, out_far,
+    row_turned, distance, field_a, field_b, final, held, out, sent,
 ):
     shard = 2 * parts.shape[1]
     chans = gain.shape[0]
@@ -140,6 +133,9 @@
     for k in range(blocks):
         row_turned[k] = rows[:, k * 128 : (k + 1) * 128]
 
+    row_local = lax.broadcasted_iota(jnp.int32, (span0, LANES), 0) - margin
+    apart = jnp.abs(row_first + row_local - col_glob)
+    distance[...] = jnp.log(1.0 + apart.astype(jnp.float32)) * 0.125
     gain_wide = jnp.broadcast_to(gain[...], (chans, LANES))
     lane16 = lax.broadcasted_iota(jnp.int16, (chans, 128), 1)
 
@@ -306,20 +302,7 @@
     return jnp.concatenate(rows, axis=1)
 
 
-def distance_call(place, none, tile_rows):
-    return pl.pallas_call(
-        functools.partial(distance_kernel, tile_rows),
-        out_shape=jax.ShapeDtypeStruct((tile_rows + 6 * DMAX2, LANES), jnp.float32),
-        in_specs=[
-            pl.BlockSpec(memory_space=pltpu.SMEM),
-            pl.BlockSpec(memory_space=pltpu.VMEM),
-        ],
-        out_specs=pl.BlockSpec(memory_space=pltpu.VMEM),
-        name="distances",
-    )(place, none)
-
-
-def pair_call(place, gathered, distance, dist_gain, bands, tile_rows, tile_cols):
+def pair_call(place, gathered, dist_gain, bands, tile_rows, tile_cols):
     chans = dist_gain.shape[0]
     smem = pl.BlockSpec(memory_space=pltpu.SMEM)
     vmem = pl.BlockSpec(memory_space=pltpu.VMEM)
@@ -327,10 +310,11 @@
     return pl.pallas_call(
         functools.partial(pair_kernel, gathered.shape[0], place.shape[0] - 3),
         out_shape=jax.ShapeDtypeStruct((chans, tile_rows, tile_cols), jnp.bfloat16),
-        in_specs=[smem] + [vmem] * 4,
+        in_specs=[smem] + [vmem] * 3,
         out_specs=pl.BlockSpec(memory_space=pltpu.HBM),
         scratch_shapes=[
             pltpu.VMEM((-(-span // 128), chans, 128), jnp.float32),
+            pltpu.VMEM((span, LANES), jnp.float32),
             pltpu.VMEM((span, 3 * chans, LANES), jnp.bfloat16),
             pltpu.VMEM((span - 2 * DMAX2, 3 * chans, LANES), jnp.bfloat16),
             pltpu.VMEM((tile_rows * PITCH, 128), jnp.float32),
@@ -346,7 +330,7 @@
         ),
         name="pair_tower",
     )(
-        place, gathered, distance, dist_gain.reshape(chans, 1), bands,
+        place, gathered, dist_gain.reshape(chans, 1), bands,
     )
 
 
@@ -377,13 +361,16 @@
 
     inner = [(i, i ^ 1) for i in range(shards)]
     outer = [(i, i + 1 if i % 2 else i - 1) for i in range(1, shards - 1)]
-    both = jnp.concatenate([features, lax.ppermute(features, AXES, inner)], axis=0)
+    brought = lax.ppermute(features, AXES, inner)
+    brought, start_bin = lax.optimization_barrier((brought, start_bin))
+    both = jnp.concatenate([features, brought], axis=0)
     from_outer = lax.ppermute(both, AXES, outer)
-    from_inner = lax.ppermute(from_outer, AXES, inner)
     code = position_code(mine * shard + jnp.arange(shard), start_bin[0], chans)
     code = jnp.pad(code, ((0, 0), (0, width - chans)))
     extra = jnp.concatenate([tower_bias, code], axis=0)
     proj = jnp.pad(pair_proj.T, ((0, 2 * chans), (0, 0)))
+    from_outer, extra, proj, place = lax.optimization_barrier((from_outer, extra, proj, place))
+    from_inner = lax.ppermute(from_outer, AXES, inner)
 
     smem = pl.BlockSpec(memory_space=pltpu.SMEM)
     vmem = pl.BlockSpec(memory_space=pltpu.VMEM)
@@ -418,9 +405,8 @@
     bands = banded(map_weight + none_16, map_bias + none_32[:-1])
     dist_gain = dist_gain + none_32[-1]
 
-    distance = distance_call(place, none_32, tile_rows)
     return pair_call(
-        place, gathered, distance, dist_gain, bands, tile_rows, tile_cols
+        place, gathered, dist_gain, bands, tile_rows, tile_cols
     )
 
 

time: 72.1 us -> 65 us (0.902)
  local copies, waits for them, and re-layouts: 5.34 us -> 3.1 us
  Pallas kernels: 33.2 us -> 31.5 us
  other arithmetic: 2.53 us -> 1.21 us
    unnamed x15 -> x7, local copies, waits for them, and re-layouts: 2.97 us -> 0.73 us
    ppermute x1, waiting for transfers between devices: 1.92 us -> 0.01 us  [on_device(): from_outer = lax.ppermute(both, AXES, outer)]
    pallas_call x1 -> x0, Pallas kernels: 1.54 us -> none  [distance_call(): pl.pallas_call(functools.partial(distance_kernel, tile_rows), out_shape=j...]
    ppermute x1, waiting for transfers between devices: 0.01 us -> 1.19 us  [on_device(): from_inner = lax.ppermute(from_outer, AXES, inner)]
  transfers between devices with their start and end apart: 4 -> 4, of which waited for: 2 -> 2; matrix products, arithmetic and copies ran while one was open for 6% -> 7% of each run, Pallas kernels for 0% -> 0%
where the time goes in v9:
time: 65 us
  Pallas kernels  31.5 us (48%)
  starting transfers between devices  17.4 us (27%)
  waiting for transfers between devices  11.1 us (17%)
  local copies, waits for them, and re-layouts  3.1 us (5%)
  other arithmetic  1.21 us (2%)
  between operations  0.78 us (1%)
    pallas_call x1, Pallas kernels, pair_call(): pl.pallas_call(functools.partial(pair_kernel, gathered.shape[0], place.sh...  27.9 us
    all_to_all x1, starting transfers between devices, on_device(): lax.all_to_all(parts, AXES, split_axis=0, concat_axis=0, tiled=True)  12.7 us
    all_to_all x1, waiting for transfers between devices, on_device(): lax.all_to_all(parts, AXES, split_axis=0, concat_axis=0, tiled=True)  9.87 us
    pallas_call x1, Pallas kernels, on_device(): pl.pallas_call(functools.partial(encode_kernel, total), out_shape=[jax.Sh...  3.57 us
    ppermute x1, starting transfers between devices, on_device(): from_outer = lax.ppermute(both, AXES, outer)  3.21 us
    ppermute x1, starting transfers between devices, on_device(): brought = lax.ppermute(features, AXES, inner)  1.42 us
  transfers between devices with their start and end apart: 4, of which 2 were waited for; matrix products, arithmetic and copies ran while one was open for 7% of the time, Pallas kernels for 0%

profile of v9, /device:TPU:1, one launch (start us, length us, event | category | flops | bytes accessed | tf_op | source)
XLA Modules:
  0.0 65.0 jit_solution(13380726419217575787)
XLA Ops:
  0.0 0.0 copy-start.2
  0.0 0.0 copy-start.1
  0.0 0.0 copy-start
  0.0 1.4 %collective-permute-start = (bf16[16,512]{1,0:T(8,128)(2,1)}, bf16[16,512]{1,0:T(8,128)(2,1)S(1)}, u32[]{:S(2)}, u32[]{:S(2)}) collective-permute-start(bf16[16,512]{1,0:T(8,128)(2,1)} %param.9), channel_id=1, source_target_pairs={{0,1},{1,0},{2,3},{3,2},{4,5},{5,4},{6,7},{7,6},{8,9},{9,8},{10,11... | collective-permute-start | bytes 49160 | tf_op jit(solution)/shard_map/ppermute | solution.py:364
  2.1 0.1 multiply_cosine_fusion
  2.2 0.1 select_maximum_fusion
  2.3 0.7 %constant_dynamic-update-slice_fusion.1 = bf16[32,512]{1,0:T(8,128)(2,1)S(1)} fusion(bf16[16,512]{1,0:T(8,128)(2,1)} %param.9), kind=kLoop, calls=%fused_computation.41 | loop fusion | bytes 32768
  3.0 0.0 collective-permute-done
  3.0 3.2 %collective-permute-start.1 = (bf16[32,512]{1,0:T(8,128)(2,1)S(1)}, bf16[32,512]{1,0:T(8,128)(2,1)S(1)}, u32[]{:S(2)}, u32[]{:S(2)}) collective-permute-start(bf16[32,512]{1,0:T(8,128)(2,1)S(1)} %constant_dynamic-update-slice_fusion.both), channel_id=1, source_target_pairs={{1,2},{2,1},{3,4},{4,3},{5,6},{6,5},{7,8},{8,7},{9,10},{10,9},{11,... | collective-permute-start | bytes 98312 | tf_op jit(solution)/shard_map/ppermute | solution.py:367
  6.3 0.7 %pad_maximum_fusion.extra = f32[18,512]{1,0:T(8,128)S(1)} fusion(f32[16,512]{1,0:T(8,128)S(1)} %select_maximum_fusion, f32[2,512]{1,0:T(2,128)} %param.11), kind=kLoop, calls=%fused_computation.33 | loop fusion | flops 9216 | bytes 73728 | tf_op jit(solution)/shard_map/concatenate | solution.py:370
  7.0 0.8 %pad.32.proj = bf16[128,512]{1,0:T(8,128)(2,1)S(1)} pad(bf16[64,512]{1,0:T(8,128)(2,1)} %bitcast.20, bf16[]{:T(256)} %constant.34.clone.1), padding=0_64x0_0 | pad | bytes 196610 | tf_op jit(solution)/shard_map/jit(_pad)/pad | solution.py:371
  7.8 0.7 %concatenate.30.place = s32[10]{0:T(128)S(1)} concatenate(s32[1]{0:T(128)} %bitcast.2, s32[1]{0:T(128)} %bitcast.3, s32[1]{0:T(128)} %bitcast.4, s32[1]{0:T(128)} %constant.35.clone.1, s32[1]{0:T(128)} %constant.36.clone.1, s32[5]{0:T(128)} %param.16), dimensions={0} | concatenate | bytes 80 | tf_op jit(solution)/shard_map/concatenate | solution.py:360
  8.5 0.0 collective-permute-done.1.outer
  8.5 0.1 collective-permute-start.2
  8.6 1.2 %collective-permute-done.2.inner = bf16[32,512]{1,0:T(8,128)(2,1)S(1)} collective-permute-done((bf16[32,512]{1,0:T(8,128)(2,1)S(1)}, bf16[32,512]{1,0:T(8,128)(2,1)S(1)}, u32[]{:S(2)}, u32[]{:S(2)}) %collective-permute-start.2) | collective-permute-done | bytes 32800 | tf_op jit(solution)/shard_map/ppermute | solution.py:373
  9.8 3.6 %encode.1 = (bf16[128,8,128]{2,1,0:T(8,128)(2,1)}, bf16[3,3,3,32,32]{4,3,2,1,0:T(8,128)(2,1)S(1)}, f32[4,32]{1,0:T(4,128)S(1)}) custom-call(s32[10]{0:T(128)S(1)} %concatenate.30.place, bf16[32,512]{1,0:T(8,128)(2,1)S(1)} %constant_dynamic-update-slice_fusion.both, bf16[32,512]{1,0:T(8,128)(2,1)S(1)} %collective-permute-done.1.outer, ...), custom_call_target="tpu_custom_call" | custom-call | flops 100663296 | bytes 3145728 | tf_op jit(solution)/shard_map/encode/pallas_call | solution.py:377
  13.4 0.0 copy-done.2
  13.4 0.0 copy-done.1
  13.4 12.7 %all-to-all-start = ((bf16[128,8,128]{2,1,0:T(8,128)(2,1)}), bf16[128,8,128]{2,1,0:T(8,128)(2,1)S(1)}, u32[]{:S(2)}, u32[]{:S(2)}) async-start(bf16[128,8,128]{2,1,0:T(8,128)(2,1)} %get-tuple-element.20), calls=%async_computation | async-start | bytes 524288 | tf_op jit(solution)/shard_map/all_to_all | solution.py:403
  26.2 0.1 copy.30.gain
  26.3 0.1 copy.27
  26.4 0.1 copy.28
  26.5 0.1 copy.29
  26.6 0.0 copy-done
  26.6 0.2 copy.26
  26.8 0.2 reshape.31
  27.0 0.1 fusion.25
  27.1 0.2 fusion.19.weight
  27.3 9.9 %all-to-all-done.parts = bf16[128,8,128]{2,1,0:T(8,128)(2,1)S(1)} async-done(((bf16[128,8,128]{2,1,0:T(8,128)(2,1)}), bf16[128,8,128]{2,1,0:T(8,128)(2,1)S(1)}, u32[]{:S(2)}, u32[]{:S(2)}) %all-to-all-start) | async-done | bytes 262176 | tf_op jit(solution)/shard_map/all_to_all | solution.py:403
  37.1 27.9 %pair_tower.1 = bf16[32,256,128]{2,1,0:T(8,128)(2,1)} custom-call(s32[10]{0:T(128)S(1)} %concatenate.30.place, bf16[128,8,128]{2,1,0:T(8,128)(2,1)S(1)} %all-to-all-done.parts, f32[32,1]{1,0:T(8,128)S(1)} %copy.30.gain, bf16[3,128,608]{2,1,0:T(8,128)(2,1)S(1)} %fusion.19.weight), custom_call_target="tpu_custom_call" | custom-call | flops 3623878656 | bytes 2097152 | tf_op jit(solution)/shard_map/pair_tower/pallas_call | solution.py:310
  (6 shorter events, 0.1 us)
Async XLA Ops:
  0.0 13.4 %copy-start.2 = (f32[32]{0:T(128)S(1)}, f32[32]{0:T(128)}, u32[]{:S(2)}) copy-start(f32[32]{0:T(128)} %param.13) | copy-start | bytes 388
  0.0 13.4 %copy-start.1 = (f32[3,32]{1,0:T(4,128)S(1)}, f32[3,32]{1,0:T(4,128)}, u32[]{:S(2)}) copy-start(f32[3,32]{1,0:T(4,128)} %param.15) | copy-start | bytes 1156
  0.0 26.6 %copy-start = (bf16[3,3,3,32,32]{4,3,2,1,0:T(8,128)(2,1)S(1)}, bf16[3,3,3,32,32]{4,3,2,1,0:T(8,128)(2,1)}, u32[]{:S(2)}) copy-start(bf16[3,3,3,32,32]{4,3,2,1,0:T(8,128)(2,1)} %param.14) | copy-start | bytes 165892
  0.0 3.0 %collective-permute-start = (bf16[16,512]{1,0:T(8,128)(2,1)}, bf16[16,512]{1,0:T(8,128)(2,1)S(1)}, u32[]{:S(2)}, u32[]{:S(2)}) collective-permute-start(bf16[16,512]{1,0:T(8,128)(2,1)} %param.9), channel_id=1, source_target_pairs={{0,1},{1,0},{2,3},{3,2},{4,5},{5,4},{6,7},{7,6},{8,9},{9,8},{10,11... | collective-permute-start | bytes 49160 | tf_op jit(solution)/shard_map/ppermute | solution.py:364
  3.0 5.5 %collective-permute-start.1 = (bf16[32,512]{1,0:T(8,128)(2,1)S(1)}, bf16[32,512]{1,0:T(8,128)(2,1)S(1)}, u32[]{:S(2)}, u32[]{:S(2)}) collective-permute-start(bf16[32,512]{1,0:T(8,128)(2,1)S(1)} %constant_dynamic-update-slice_fusion.both), channel_id=1, source_target_pairs={{1,2},{2,1},{3,4},{4,3},{5,6},{6,5},{7,8},{8,7},{9,10},{10,9},{11,... | collective-permute-start | bytes 98312 | tf_op jit(solution)/shard_map/ppermute | solution.py:367
  8.5 1.3 %collective-permute-start.2 = (bf16[32,512]{1,0:T(8,128)(2,1)S(1)}, bf16[32,512]{1,0:T(8,128)(2,1)S(1)}, u32[]{:S(2)}, u32[]{:S(2)}) collective-permute-start(bf16[32,512]{1,0:T(8,128)(2,1)S(1)} %collective-permute-done.1.outer), channel_id=1, source_target_pairs={{0,1},{1,0},{2,3},{3,2},{4,5},{5,4},{6,7},{7,6},{8,9},{9,8},{10,11... | collective-permute-start | bytes 98312 | tf_op jit(solution)/shard_map/ppermute | solution.py:373
  13.4 23.7 %all-to-all-start = ((bf16[128,8,128]{2,1,0:T(8,128)(2,1)}), bf16[128,8,128]{2,1,0:T(8,128)(2,1)S(1)}, u32[]{:S(2)}, u32[]{:S(2)}) async-start(bf16[128,8,128]{2,1,0:T(8,128)(2,1)} %get-tuple-element.20), calls=%async_computation | async-start | bytes 524288 | tf_op jit(solution)/shard_map/all_to_all | solution.py:403

commit v10 on v9

--- a/solution.py
+++ b/solution.py
@@ -16,6 +16,7 @@
 UNROLL = 4
 LANES = 256
 PITCH = 40
+FETCH_LIMIT = 50
 CHUNK = 64
 OUTSIDE = -1e30
 AXES = ("rows", "cols")
@@ -29,23 +30,35 @@
     return jnp.concatenate([jnp.cos(phase_angle), jnp.sin(phase_angle)], axis=1)
 
 
+def fetch_kernel(far, near, arrived):
+    copies = [
+        pltpu.make_async_copy(far.at[which, tap], near.at[which, tap], arrived.at[which, tap])
+        for which in range(far.shape[0])
+        for tap in range(far.shape[1])
+    ]
+    for copy in copies:
+        copy.start()
+    for copy in copies:
+        copy.wait()
+
+
+def fetch_call(far):
+    return pl.pallas_call(
+        fetch_kernel,
+        out_shape=jax.ShapeDtypeStruct(far.shape, far.dtype),
+        in_specs=[pl.BlockSpec(memory_space=pltpu.HBM)],
+        out_specs=pl.BlockSpec(memory_space=pltpu.VMEM),
+        scratch_shapes=[pltpu.SemaphoreType.DMA(far.shape[:2])],
+        compiler_params=pltpu.CompilerParams(vmem_limit_bytes=FETCH_LIMIT * 2**20),
+        name="fetch",
+    )(far)
+
+
 def encode_kernel(
-    total, place, both, outer, inner, proj, extra, weight_far, out, none_16, none_32,
-    weight, wide, mid, arrived,
+    total, place, both, outer, inner, proj, extra, weight, out, none_16, none_32, wide, mid,
 ):
     count = both.shape[0] // 2
     bias = extra[:2, :]
-    fetch = [
-        [
-            pltpu.make_async_copy(
-                weight_far.at[which, tap], weight.at[which, tap], arrived.at[which, tap]
-            )
-            for tap in range(3)
-        ]
-        for which in range(2)
-    ]
-    for copy in fetch[0] + fetch[1]:
-        copy.start()
     chunks = wide.shape[0]
 
     def keep(ref, first, value):
@@ -59,7 +72,6 @@
         running = jnp.zeros((span, chunks * 128), jnp.float32)
         for tap in range(3):
             rows = run(ref, count + (tap - 1) * place[5 + which], span).astype(jnp.bfloat16)
-            fetch[which][tap].wait()
             running += jnp.dot(rows, weight[which, tap], preferred_element_type=jnp.float32)
         return run(ref, count, span) + jnp.maximum(running + bias[which : which + 1, :], 0.0)
 
@@ -216,10 +228,11 @@
                     at = slice(n * width, (n + 1) * width)
                     center = source[base + DMAX2 + k * d, chans : 2 * chans, :width]
                     value = sums[k * chans : (k + 1) * chans, at]
-                    value = center.astype(jnp.float32) + jnp.maximum(value, 0.0)
                     if final_layer:
+                        value = center.astype(jnp.float32) + jnp.maximum(value, 0.0)
                         store(base + k * d, value)
                     else:
+                        value = center + jnp.maximum(value.astype(jnp.bfloat16), 0)
                         store(base + k * d, value[:, :128], value[:, 128:])
 
         def walk(start, phase):
@@ -369,7 +382,10 @@
     code = jnp.pad(code, ((0, 0), (0, width - chans)))
     extra = jnp.concatenate([tower_bias, code], axis=0)
     proj = jnp.pad(pair_proj.T, ((0, 2 * chans), (0, 0)))
-    from_outer, extra, proj, place = lax.optimization_barrier((from_outer, extra, proj, place))
+    weight = fetch_call(lax.optimization_barrier((tower_weight, both))[0])
+    from_outer, extra, proj, place, weight = lax.optimization_barrier(
+        (from_outer, extra, proj, place, weight)
+    )
     from_inner = lax.ppermute(from_outer, AXES, inner)
 
     smem = pl.BlockSpec(memory_space=pltpu.SMEM)
@@ -381,15 +397,13 @@
             jax.ShapeDtypeStruct(map_weight.shape, map_weight.dtype),
             jax.ShapeDtypeStruct((map_bias.shape[0] + 1, chans), jnp.float32),
         ],
-        in_specs=[smem] + [vmem] * 5 + [pl.BlockSpec(memory_space=pltpu.HBM)],
+        in_specs=[smem] + [vmem] * 6,
         out_specs=[vmem] * 3,
         scratch_shapes=[
-            pltpu.VMEM(tower_weight.shape, tower_weight.dtype),
             pltpu.VMEM((width // 128, 5 * shard, 128), jnp.float32),
             pltpu.VMEM((width // 128, 3 * shard, 128), jnp.float32),
-            pltpu.SemaphoreType.DMA(tower_weight.shape[:2]),
         ],
-        compiler_params=pltpu.CompilerParams(vmem_limit_bytes=52 * 2**20),
+        compiler_params=pltpu.CompilerParams(vmem_limit_bytes=16 * 2**20),
         cost_estimate=pl.CostEstimate(
             flops=2 * 4 * shard * 3 * width * width,
             bytes_accessed=6 * width * width * 2,
@@ -397,7 +411,7 @@
         ),
         name="encode",
     )(
-        place, both, from_outer, from_inner, proj, extra, tower_weight,
+        place, both, from_outer, from_inner, proj, extra, weight,
     )
 
     gathered = lax.all_to_all(parts, AXES, split_axis=0, concat_axis=0, tiled=True)

time: 65 us -> 65.5 us (level); the launches traced: 65 us -> 64.4 us
  starting transfers between devices: 17.4 us -> 15.4 us
  Pallas kernels: 31.5 us -> 32.8 us
    all_to_all x1, starting transfers between devices: 12.7 us -> 10.8 us  [on_device(): lax.all_to_all(parts, AXES, split_axis=0, concat_axis=0, tiled=True)]
    pallas_call x0 -> x1, Pallas kernels: none -> 1.88 us  [fetch_call(): pl.pallas_call(fetch_kernel, out_shape=jax.ShapeDtypeStruct(far.shape, fa...]
    pallas_call x1, Pallas kernels: 3.57 us -> 2.17 us  [on_device(): pl.pallas_call(functools.partial(encode_kernel, total), out_shape=[jax.Sh...]
    pallas_call x1, Pallas kernels: 27.9 us -> 28.8 us  [pair_call(): pl.pallas_call(functools.partial(pair_kernel, gathered.shape[0], place.sh...]
  transfers between devices with their start and end apart: 4 -> 4, of which waited for: 2 -> 2; matrix products, arithmetic and copies ran while one was open for 7% -> 7% of each run, Pallas kernels for 0% -> 3%
where the time goes in v10:
time: 65.5 us; the launch traced here: 64.4 us
  Pallas kernels  32.8 us (50%)
  starting transfers between devices  15.4 us (24%)
  waiting for transfers between devices  11.1 us (17%)
  local copies, waits for them, and re-layouts  3.11 us (5%)
  other arithmetic  1.21 us (2%)
  between operations  0.79 us (1%)
    pallas_call x1, Pallas kernels, pair_call(): pl.pallas_call(functools.partial(pair_kernel, gathered.shape[0], place.sh...  28.8 us
    all_to_all x1, starting transfers between devices, on_device(): lax.all_to_all(parts, AXES, split_axis=0, concat_axis=0, tiled=True)  10.8 us
    all_to_all x1, waiting for transfers between devices, on_device(): lax.all_to_all(parts, AXES, split_axis=0, concat_axis=0, tiled=True)  9.87 us
    ppermute x1, starting transfers between devices, on_device(): from_outer = lax.ppermute(both, AXES, outer)  3.08 us
    pallas_call x1, Pallas kernels, on_device(): pl.pallas_call(functools.partial(encode_kernel, total), out_shape=[jax.Sh...  2.17 us
    pallas_call x1, Pallas kernels, fetch_call(): pl.pallas_call(fetch_kernel, out_shape=jax.ShapeDtypeStruct(far.shape, fa...  1.88 us
    ppermute x1, starting transfers between devices, on_device(): brought = lax.ppermute(features, AXES, inner)  1.42 us
  transfers between devices with their start and end apart: 4, of which 2 were waited for; matrix products, arithmetic and copies ran while one was open for 7% of the time, Pallas kernels for 3%

profile of v10, /device:TPU:1, one launch (start us, length us, event | category | flops | bytes accessed | tf_op | source)
XLA Modules:
  0.0 64.4 jit_solution(12093627716551823712)
XLA Ops:
  0.0 1.4 %collective-permute-start = (bf16[16,512]{1,0:T(8,128)(2,1)}, bf16[16,512]{1,0:T(8,128)(2,1)S(1)}, u32[]{:S(2)}, u32[]{:S(2)}) collective-permute-start(bf16[16,512]{1,0:T(8,128)(2,1)} %param.9), channel_id=1, source_target_pairs={{0,1},{1,0},{2,3},{3,2},{4,5},{5,4},{6,7},{7,6},{8,9},{9,8},{10,11... | collective-permute-start | bytes 49160 | tf_op jit(solution)/shard_map/ppermute | solution.py:377
  2.1 0.1 multiply_cosine_fusion
  2.2 0.1 select_maximum_fusion
  2.3 0.7 %constant_dynamic-update-slice_fusion.1 = bf16[32,512]{1,0:T(8,128)(2,1)S(1)} fusion(bf16[16,512]{1,0:T(8,128)(2,1)} %param.9), kind=kLoop, calls=%fused_computation.41 | loop fusion | bytes 32768
  3.0 0.0 collective-permute-done
  3.0 3.1 %collective-permute-start.1 = (bf16[32,512]{1,0:T(8,128)(2,1)S(1)}, bf16[32,512]{1,0:T(8,128)(2,1)S(1)}, u32[]{:S(2)}, u32[]{:S(2)}) collective-permute-start(bf16[32,512]{1,0:T(8,128)(2,1)S(1)} %constant_dynamic-update-slice_fusion.both), channel_id=1, source_target_pairs={{1,2},{2,1},{3,4},{4,3},{5,6},{6,5},{7,8},{8,7},{9,10},{10,9},{11,... | collective-permute-start | bytes 98312 | tf_op jit(solution)/shard_map/ppermute | solution.py:380
  6.1 0.7 %pad_maximum_fusion.extra = f32[18,512]{1,0:T(8,128)S(1)} fusion(f32[16,512]{1,0:T(8,128)S(1)} %select_maximum_fusion, f32[2,512]{1,0:T(2,128)} %param.11), kind=kLoop, calls=%fused_computation.33 | loop fusion | flops 9216 | bytes 73728 | tf_op jit(solution)/shard_map/concatenate | solution.py:383
  6.8 0.8 %pad.32.proj = bf16[128,512]{1,0:T(8,128)(2,1)S(1)} pad(bf16[64,512]{1,0:T(8,128)(2,1)} %bitcast.20, bf16[]{:T(256)} %constant.34.clone.1), padding=0_64x0_0 | pad | bytes 196610 | tf_op jit(solution)/shard_map/jit(_pad)/pad | solution.py:384
  7.7 0.7 %concatenate.30.place = s32[10]{0:T(128)S(1)} concatenate(s32[1]{0:T(128)} %bitcast.2, s32[1]{0:T(128)} %bitcast.3, s32[1]{0:T(128)} %bitcast.4, s32[1]{0:T(128)} %constant.35.clone.1, s32[1]{0:T(128)} %constant.36.clone.1, s32[5]{0:T(128)} %param.16), dimensions={0} | concatenate | bytes 80 | tf_op jit(solution)/shard_map/concatenate | solution.py:373
  8.4 1.9 %fetch.1.weight = bf16[2,3,512,512]{3,2,1,0:T(8,128)(2,1)S(1)} custom-call(bf16[2,3,512,512]{3,2,1,0:T(8,128)(2,1)} %far), custom_call_target="tpu_custom_call" | custom-call | tf_op jit(solution)/shard_map/fetch/pallas_call | solution.py:46
  10.3 0.0 copy-start.2
  10.3 0.0 copy-start.1
  10.3 0.0 copy-start
  10.3 0.0 collective-permute-done.1.outer
  10.3 0.1 collective-permute-start.2
  10.4 1.2 %collective-permute-done.2.inner = bf16[32,512]{1,0:T(8,128)(2,1)S(1)} collective-permute-done((bf16[32,512]{1,0:T(8,128)(2,1)S(1)}, bf16[32,512]{1,0:T(8,128)(2,1)S(1)}, u32[]{:S(2)}, u32[]{:S(2)}) %collective-permute-start.2) | collective-permute-done | bytes 32800 | tf_op jit(solution)/shard_map/ppermute | solution.py:389
  11.6 2.2 %encode.1 = (bf16[128,8,128]{2,1,0:T(8,128)(2,1)}, bf16[3,3,3,32,32]{4,3,2,1,0:T(8,128)(2,1)S(1)}, f32[4,32]{1,0:T(4,128)S(1)}) custom-call(s32[10]{0:T(128)S(1)} %concatenate.30.place, bf16[32,512]{1,0:T(8,128)(2,1)S(1)} %constant_dynamic-update-slice_fusion.both, bf16[32,512]{1,0:T(8,128)(2,1)S(1)} %collective-permute-done.1.outer, ...), custom_call_target="tpu_custom_call" | custom-call | flops 100663296 | bytes 3145728 | tf_op jit(solution)/shard_map/encode/pallas_call | solution.py:393
  13.8 0.0 copy-done.2
  13.8 0.0 copy-done.1
  13.8 10.8 %all-to-all-start = ((bf16[128,8,128]{2,1,0:T(8,128)(2,1)}), bf16[128,8,128]{2,1,0:T(8,128)(2,1)S(1)}, u32[]{:S(2)}, u32[]{:S(2)}) async-start(bf16[128,8,128]{2,1,0:T(8,128)(2,1)} %get-tuple-element.24), calls=%async_computation | async-start | bytes 524288 | tf_op jit(solution)/shard_map/all_to_all | solution.py:417
  24.6 0.1 copy.30.gain
  24.7 0.1 copy.27
  24.9 0.1 copy.28
  25.0 0.1 copy.29
  25.1 0.0 copy-done
  25.1 0.2 copy.26
  25.3 0.2 reshape.31
  25.5 0.1 fusion.25
  25.6 0.2 fusion.19.weight
  25.8 9.9 %all-to-all-done.parts = bf16[128,8,128]{2,1,0:T(8,128)(2,1)S(1)} async-done(((bf16[128,8,128]{2,1,0:T(8,128)(2,1)}), bf16[128,8,128]{2,1,0:T(8,128)(2,1)S(1)}, u32[]{:S(2)}, u32[]{:S(2)}) %all-to-all-start) | async-done | bytes 262176 | tf_op jit(solution)/shard_map/all_to_all | solution.py:417
  35.6 28.8 %pair_tower.1 = bf16[32,256,128]{2,1,0:T(8,128)(2,1)} custom-call(s32[10]{0:T(128)S(1)} %concatenate.30.place, bf16[128,8,128]{2,1,0:T(8,128)(2,1)S(1)} %all-to-all-done.parts, f32[32,1]{1,0:T(8,128)S(1)} %copy.30.gain, bf16[3,128,608]{2,1,0:T(8,128)(2,1)S(1)} %fusion.19.weight), custom_call_target="tpu_custom_call" | custom-call | flops 3623878656 | bytes 2097152 | tf_op jit(solution)/shard_map/pair_tower/pallas_call | solution.py:323
  (6 shorter events, 0.1 us)
Async XLA Ops:
  0.0 3.0 %collective-permute-start = (bf16[16,512]{1,0:T(8,128)(2,1)}, bf16[16,512]{1,0:T(8,128)(2,1)S(1)}, u32[]{:S(2)}, u32[]{:S(2)}) collective-permute-start(bf16[16,512]{1,0:T(8,128)(2,1)} %param.9), channel_id=1, source_target_pairs={{0,1},{1,0},{2,3},{3,2},{4,5},{5,4},{6,7},{7,6},{8,9},{9,8},{10,11... | collective-permute-start | bytes 49160 | tf_op jit(solution)/shard_map/ppermute | solution.py:377
  3.0 7.3 %collective-permute-start.1 = (bf16[32,512]{1,0:T(8,128)(2,1)S(1)}, bf16[32,512]{1,0:T(8,128)(2,1)S(1)}, u32[]{:S(2)}, u32[]{:S(2)}) collective-permute-start(bf16[32,512]{1,0:T(8,128)(2,1)S(1)} %constant_dynamic-update-slice_fusion.both), channel_id=1, source_target_pairs={{1,2},{2,1},{3,4},{4,3},{5,6},{6,5},{7,8},{8,7},{9,10},{10,9},{11,... | collective-permute-start | bytes 98312 | tf_op jit(solution)/shard_map/ppermute | solution.py:380
  10.3 3.5 %copy-start.2 = (f32[32]{0:T(128)S(1)}, f32[32]{0:T(128)}, u32[]{:S(2)}) copy-start(f32[32]{0:T(128)} %param.13) | copy-start | bytes 388
  10.3 3.5 %copy-start.1 = (f32[3,32]{1,0:T(4,128)S(1)}, f32[3,32]{1,0:T(4,128)}, u32[]{:S(2)}) copy-start(f32[3,32]{1,0:T(4,128)} %param.15) | copy-start | bytes 1156
  10.3 14.8 %copy-start = (bf16[3,3,3,32,32]{4,3,2,1,0:T(8,128)(2,1)S(1)}, bf16[3,3,3,32,32]{4,3,2,1,0:T(8,128)(2,1)}, u32[]{:S(2)}) copy-start(bf16[3,3,3,32,32]{4,3,2,1,0:T(8,128)(2,1)} %param.14) | copy-start | bytes 165892
  10.3 1.3 %collective-permute-start.2 = (bf16[32,512]{1,0:T(8,128)(2,1)S(1)}, bf16[32,512]{1,0:T(8,128)(2,1)S(1)}, u32[]{:S(2)}, u32[]{:S(2)}) collective-permute-start(bf16[32,512]{1,0:T(8,128)(2,1)S(1)} %collective-permute-done.1.outer), channel_id=1, source_target_pairs={{0,1},{1,0},{2,3},{3,2},{4,5},{5,4},{6,7},{7,6},{8,9},{9,8},{10,11... | collective-permute-start | bytes 98312 | tf_op jit(solution)/shard_map/ppermute | solution.py:389
  13.8 21.8 %all-to-all-start = ((bf16[128,8,128]{2,1,0:T(8,128)(2,1)}), bf16[128,8,128]{2,1,0:T(8,128)(2,1)S(1)}, u32[]{:S(2)}, u32[]{:S(2)}) async-start(bf16[128,8,128]{2,1,0:T(8,128)(2,1)} %get-tuple-element.24), calls=%async_computation | async-start | bytes 524288 | tf_op jit(solution)/shard_map/all_to_all | solution.py:417

commit v11 on v10

--- a/solution.py
+++ b/solution.py
@@ -11,7 +11,6 @@
 DMAX1 = 16
 DMAX2 = 16
 GROUP = 4
-TAIL = 32
 WIDE = 2
 UNROLL = 4
 LANES = 256
@@ -106,7 +105,7 @@
 
 
 def pair_kernel(
-    total_shards, first_dil, place, parts, gain, weight, out_far,
+    total_shards, first_dil, place, parts, gain, weight, bias, out_far,
     row_turned, distance, field_a, field_b, final, held, out, sent,
 ):
     shard = 2 * parts.shape[1]
@@ -137,13 +136,20 @@
     col_turned = jnp.transpose(cols)[chans : 2 * chans, :]
     col_turned = jnp.where(inside, col_turned, OUTSIDE)
     span0 = tile_rows + 2 * margin
-    blocks = -(-span0 // 128)
-    rows = pieces(row_first // shard - reach, blocks * 128 // shard, blocks * 128)
-    rows = jnp.transpose(rows)[:chans, :]
-    row_glob = row_first - margin + lax.broadcasted_iota(jnp.int32, (1, blocks * 128), 1)
-    rows = jnp.where((row_glob >= 0) & (row_glob < total_shards * shard), rows, OUTSIDE)
-    for k in range(blocks):
-        row_turned[k] = rows[:, k * 128 : (k + 1) * 128]
+    count = -(-span0 // shard)
+    half = shard // 2
+    rows = [
+        parts[jnp.clip(row_first // shard - reach + k, 0, total_shards - 1)] for k in range(count)
+    ]
+    rows = jnp.transpose(jnp.concatenate(rows, axis=0).astype(jnp.float32))
+    spot = lax.broadcasted_iota(jnp.int32, (1, count * half), 1)
+    for side in range(2):
+        row_glob = row_first - margin + spot // half * shard + side * half + spot % half
+        valid = (row_glob >= 0) & (row_glob < total_shards * shard)
+        turned = rows[side * 2 * chans : (side * 2 + 1) * chans, :]
+        turned = jnp.where(valid, turned, OUTSIDE)
+        row_turned[2 * side] = turned[:, :128]
+        row_turned[2 * side + 1, :, : count * half - 128] = turned[:, 128:]
 
     row_local = lax.broadcasted_iota(jnp.int32, (span0, LANES), 0) - margin
     apart = jnp.abs(row_first + row_local - col_glob)
@@ -192,8 +198,10 @@
     def build(index, count):
         for k in range(count):
             i = jnp.minimum(first_row + index + k, last_row_needed)
-            pick = jnp.full((chans, 128), i % 128, jnp.int32)
-            row_term = jnp.take_along_axis(row_turned[i // 128], pick, axis=1)
+            spot = i // shard * half + i % half
+            pick = jnp.full((chans, 128), spot % 128, jnp.int32)
+            turned = row_turned[i // half % 2 * 2 + spot // 128]
+            row_term = jnp.take_along_axis(turned, pick, axis=1)
             row_term = jnp.concatenate([row_term, row_term], axis=1)
             value = row_term + col_turned + gain_wide * distance[pl.ds(i, 1), :]
             value = jnp.maximum(value, 0.0)
@@ -202,8 +210,6 @@
     @pl.loop(0, (last_row_needed - first_row + 8) // 8)
     def _(block):
         build(block * 8, 8)
-
-    tail = jnp.ones((TAIL, WIDE * LANES), jnp.bfloat16)
 
     def tower(layer, source, extra, need, store, first_in_step=None):
         d = dils[layer]
@@ -214,12 +220,14 @@
         width = 128 if final_layer else LANES
         each = WIDE * LANES // width
 
+        bias_wide = jnp.broadcast_to(bias[layer], (chans, width))
+
         def product(bases):
             taps = []
             for k in range(GROUP + 2):
                 at = [base + DMAX2 + (k - 1) * d for base in bases]
                 taps.append(jnp.concatenate([source[i, :, :width] for i in at], axis=1))
-            stack = jnp.concatenate(taps + [tail], axis=0)
+            stack = jnp.concatenate(taps, axis=0)
             return jnp.dot(weight[layer], stack, preferred_element_type=jnp.float32)
 
         def finish(bases, sums):
@@ -227,7 +235,7 @@
                 for k in range(GROUP):
                     at = slice(n * width, (n + 1) * width)
                     center = source[base + DMAX2 + k * d, chans : 2 * chans, :width]
-                    value = sums[k * chans : (k + 1) * chans, at]
+                    value = sums[k * chans : (k + 1) * chans, at] + bias_wide
                     if final_layer:
                         value = center.astype(jnp.float32) + jnp.maximum(value, 0.0)
                         store(base + k * d, value)
@@ -298,24 +306,17 @@
         send(k).wait()
 
 
-def banded(map_weight, map_bias):
+def banded(map_weight):
     layers, _, _, outs, ins = map_weight.shape
     taps = jnp.transpose(map_weight, (0, 3, 1, 2, 4)).reshape(layers, outs, 9 * ins)
-    left = map_bias
-    split = []
-    for _ in range(3):
-        split.append(lax.reduce_precision(left, 8, 7))
-        left = left - split[-1]
-    split = jnp.stack(split, axis=2).astype(jnp.bfloat16)
-    rows = []
-    for k in range(GROUP):
-        before, after = k * 3 * ins, (GROUP - 1 - k) * 3 * ins
-        row = jnp.pad(taps, ((0, 0), (0, 0), (before, after)))
-        rows.append(jnp.concatenate([row, jnp.pad(split, ((0, 0), (0, 0), (0, TAIL - 3)))], axis=2))
+    rows = [
+        jnp.pad(taps, ((0, 0), (0, 0), (k * 3 * ins, (GROUP - 1 - k) * 3 * ins)))
+        for k in range(GROUP)
+    ]
     return jnp.concatenate(rows, axis=1)
 
 
-def pair_call(place, gathered, dist_gain, bands, tile_rows, tile_cols):
+def pair_call(place, gathered, dist_gain, bands, map_bias, tile_rows, tile_cols):
     chans = dist_gain.shape[0]
     smem = pl.BlockSpec(memory_space=pltpu.SMEM)
     vmem = pl.BlockSpec(memory_space=pltpu.VMEM)
@@ -323,10 +324,10 @@
     return pl.pallas_call(
         functools.partial(pair_kernel, gathered.shape[0], place.shape[0] - 3),
         out_shape=jax.ShapeDtypeStruct((chans, tile_rows, tile_cols), jnp.bfloat16),
-        in_specs=[smem] + [vmem] * 3,
+        in_specs=[smem] + [vmem] * 4,
         out_specs=pl.BlockSpec(memory_space=pltpu.HBM),
         scratch_shapes=[
-            pltpu.VMEM((-(-span // 128), chans, 128), jnp.float32),
+            pltpu.VMEM((4, chans, 128), jnp.float32),
             pltpu.VMEM((span, LANES), jnp.float32),
             pltpu.VMEM((span, 3 * chans, LANES), jnp.bfloat16),
             pltpu.VMEM((span - 2 * DMAX2, 3 * chans, LANES), jnp.bfloat16),
@@ -343,7 +344,7 @@
         ),
         name="pair_tower",
     )(
-        place, gathered, dist_gain.reshape(chans, 1), bands,
+        place, gathered, dist_gain.reshape(chans, 1), bands, map_bias.reshape(-1, chans, 1),
     )
 
 
@@ -416,11 +417,12 @@
 
     gathered = lax.all_to_all(parts, AXES, split_axis=0, concat_axis=0, tiled=True)
 
-    bands = banded(map_weight + none_16, map_bias + none_32[:-1])
+    bands = banded(map_weight + none_16)
+    map_bias = map_bias + none_32[:-1]
     dist_gain = dist_gain + none_32[-1]
 
     return pair_call(
-        place, gathered, dist_gain, bands, tile_rows, tile_cols
+        place, gathered, dist_gain, bands, map_bias, tile_rows, tile_cols
     )
 
 

time: 65.5 us -> 68.5 us (1.046); the launches traced: 64.4 us -> 69.3 us
  Pallas kernels: 32.8 us -> 37.7 us
    pallas_call x1, Pallas kernels: 28.8 us -> 33.7 us  [pair_call(): pl.pallas_call(functools.partial(pair_kernel, gathered.shape[0], place.sh...]
  transfers between devices with their start and end apart: 4 -> 4, of which waited for: 2 -> 2; matrix products, arithmetic and copies ran while one was open for 7% -> 6% of each run, Pallas kernels for 3% -> 3%
where the time goes in v11:
time: 68.5 us; the launch traced here: 69.3 us
  Pallas kernels  37.7 us (55%)
  starting transfers between devices  15.4 us (22%)
  waiting for transfers between devices  11.5 us (17%)
  local copies, waits for them, and re-layouts  2.86 us (4%)
  other arithmetic  1.09 us (2%)
  between operations  0.77 us (1%)
    pallas_call x1, Pallas kernels, pair_call(): pl.pallas_call(functools.partial(pair_kernel, gathered.shape[0], place.sh...  33.7 us
    all_to_all x1, starting transfers between devices, on_device(): lax.all_to_all(parts, AXES, split_axis=0, concat_axis=0, tiled=True)  10.8 us
    all_to_all x1, waiting for transfers between devices, on_device(): lax.all_to_all(parts, AXES, split_axis=0, concat_axis=0, tiled=True)  10.3 us
    ppermute x1, starting transfers between devices, on_device(): from_outer = lax.ppermute(both, AXES, outer)  3.08 us
    pallas_call x1, Pallas kernels, on_device(): pl.pallas_call(functools.partial(encode_kernel, total), out_shape=[jax.Sh...  2.17 us
    pallas_call x1, Pallas kernels, fetch_call(): pl.pallas_call(fetch_kernel, out_shape=jax.ShapeDtypeStruct(far.shape, fa...  1.88 us
    ppermute x1, starting transfers between devices, on_device(): brought = lax.ppermute(features, AXES, inner)  1.42 us
  transfers between devices with their start and end apart: 4, of which 2 were waited for; matrix products, arithmetic and copies ran while one was open for 6% of the time, Pallas kernels for 3%

profile of v11, /device:TPU:1, one launch (start us, length us, event | category | flops | bytes accessed | tf_op | source)
XLA Modules:
  0.0 69.3 jit_solution(5376702411658288368)
XLA Ops:
  0.0 1.4 %collective-permute-start = (bf16[16,512]{1,0:T(8,128)(2,1)}, bf16[16,512]{1,0:T(8,128)(2,1)S(1)}, u32[]{:S(2)}, u32[]{:S(2)}) collective-permute-start(bf16[16,512]{1,0:T(8,128)(2,1)} %param.9), channel_id=1, source_target_pairs={{0,1},{1,0},{2,3},{3,2},{4,5},{5,4},{6,7},{7,6},{8,9},{9,8},{10,11... | collective-permute-start | bytes 49160 | tf_op jit(solution)/shard_map/ppermute | solution.py:378
  2.1 0.1 multiply_cosine_fusion
  2.2 0.1 select_maximum_fusion
  2.3 0.7 %constant_dynamic-update-slice_fusion.1 = bf16[32,512]{1,0:T(8,128)(2,1)S(1)} fusion(bf16[16,512]{1,0:T(8,128)(2,1)} %param.9), kind=kLoop, calls=%fused_computation.22 | loop fusion | bytes 32768
  3.0 0.0 collective-permute-done
  3.0 3.1 %collective-permute-start.1 = (bf16[32,512]{1,0:T(8,128)(2,1)S(1)}, bf16[32,512]{1,0:T(8,128)(2,1)S(1)}, u32[]{:S(2)}, u32[]{:S(2)}) collective-permute-start(bf16[32,512]{1,0:T(8,128)(2,1)S(1)} %constant_dynamic-update-slice_fusion.both), channel_id=1, source_target_pairs={{1,2},{2,1},{3,4},{4,3},{5,6},{6,5},{7,8},{8,7},{9,10},{10,9},{11,... | collective-permute-start | bytes 98312 | tf_op jit(solution)/shard_map/ppermute | solution.py:381
  6.1 0.7 %pad_maximum_fusion.extra = f32[18,512]{1,0:T(8,128)S(1)} fusion(f32[16,512]{1,0:T(8,128)S(1)} %select_maximum_fusion, f32[2,512]{1,0:T(2,128)} %param.11), kind=kLoop, calls=%fused_computation.16 | loop fusion | flops 9216 | bytes 73728 | tf_op jit(solution)/shard_map/concatenate | solution.py:384
  6.8 0.8 %pad.25.proj = bf16[128,512]{1,0:T(8,128)(2,1)S(1)} pad(bf16[64,512]{1,0:T(8,128)(2,1)} %bitcast.16, bf16[]{:T(256)} %constant.34.clone.1), padding=0_64x0_0 | pad | bytes 196610 | tf_op jit(solution)/shard_map/jit(_pad)/pad | solution.py:385
  7.7 0.7 %concatenate.18.place = s32[10]{0:T(128)S(1)} concatenate(s32[1]{0:T(128)} %bitcast.2, s32[1]{0:T(128)} %bitcast.3, s32[1]{0:T(128)} %bitcast.4, s32[1]{0:T(128)} %constant.35.clone.1, s32[1]{0:T(128)} %constant.36.clone.1, s32[5]{0:T(128)} %param.16), dimensions={0} | concatenate | bytes 80 | tf_op jit(solution)/shard_map/concatenate | solution.py:374
  8.4 1.9 %fetch.1.weight = bf16[2,3,512,512]{3,2,1,0:T(8,128)(2,1)S(1)} custom-call(bf16[2,3,512,512]{3,2,1,0:T(8,128)(2,1)} %far), custom_call_target="tpu_custom_call" | custom-call | tf_op jit(solution)/shard_map/fetch/pallas_call | solution.py:45
  10.3 0.0 copy-start.2
  10.3 0.0 copy-start.1
  10.3 0.0 copy-start
  10.3 0.0 collective-permute-done.1.outer
  10.3 0.1 collective-permute-start.2
  10.4 1.2 %collective-permute-done.2.inner = bf16[32,512]{1,0:T(8,128)(2,1)S(1)} collective-permute-done((bf16[32,512]{1,0:T(8,128)(2,1)S(1)}, bf16[32,512]{1,0:T(8,128)(2,1)S(1)}, u32[]{:S(2)}, u32[]{:S(2)}) %collective-permute-start.2) | collective-permute-done | bytes 32800 | tf_op jit(solution)/shard_map/ppermute | solution.py:390
  11.6 2.2 %encode.1 = (bf16[128,8,128]{2,1,0:T(8,128)(2,1)}, bf16[3,3,3,32,32]{4,3,2,1,0:T(8,128)(2,1)S(1)}, f32[4,32]{1,0:T(4,128)S(1)}) custom-call(s32[10]{0:T(128)S(1)} %concatenate.18.place, bf16[32,512]{1,0:T(8,128)(2,1)S(1)} %constant_dynamic-update-slice_fusion.both, bf16[32,512]{1,0:T(8,128)(2,1)S(1)} %collective-permute-done.1.outer, ...), custom_call_target="tpu_custom_call" | custom-call | flops 100663296 | bytes 3145728 | tf_op jit(solution)/shard_map/encode/pallas_call | solution.py:394
  13.8 0.0 copy-done.2
  13.8 0.0 copy-done.1
  13.8 10.8 %all-to-all-start = ((bf16[128,8,128]{2,1,0:T(8,128)(2,1)}), bf16[128,8,128]{2,1,0:T(8,128)(2,1)S(1)}, u32[]{:S(2)}, u32[]{:S(2)}) async-start(bf16[128,8,128]{2,1,0:T(8,128)(2,1)} %get-tuple-element.24), calls=%async_computation | async-start | bytes 524288 | tf_op jit(solution)/shard_map/all_to_all | solution.py:418
  24.6 0.1 copy.14.gain
  24.7 0.1 copy.15.bias
  24.8 0.0 copy-done
  24.9 0.2 copy.13
  25.0 0.2 reshape.34
  25.2 0.1 fusion.7.weight
  25.4 10.3 %all-to-all-done.parts = bf16[128,8,128]{2,1,0:T(8,128)(2,1)S(1)} async-done(((bf16[128,8,128]{2,1,0:T(8,128)(2,1)}), bf16[128,8,128]{2,1,0:T(8,128)(2,1)S(1)}, u32[]{:S(2)}, u32[]{:S(2)}) %all-to-all-start) | async-done | bytes 262176 | tf_op jit(solution)/shard_map/all_to_all | solution.py:418
  35.6 33.7 %pair_tower.1 = bf16[32,256,128]{2,1,0:T(8,128)(2,1)} custom-call(s32[10]{0:T(128)S(1)} %concatenate.18.place, bf16[128,8,128]{2,1,0:T(8,128)(2,1)S(1)} %all-to-all-done.parts, f32[32,1]{1,0:T(8,128)S(1)} %copy.14.gain, bf16[3,128,576]{2,1,0:T(8,128)(2,1)S(1)} %fusion.7.weight, f32[3,32,1]{2,1,0:T(8,128)S(1)} %copy.15.bias), custom_call_target="tpu_custom_call" | custom-call | flops 3623878656 | bytes 2097152 | tf_op jit(solution)/shard_map/pair_tower/pallas_call | solution.py:324
  (6 shorter events, 0.1 us)
Async XLA Ops:
  0.0 3.0 %collective-permute-start = (bf16[16,512]{1,0:T(8,128)(2,1)}, bf16[16,512]{1,0:T(8,128)(2,1)S(1)}, u32[]{:S(2)}, u32[]{:S(2)}) collective-permute-start(bf16[16,512]{1,0:T(8,128)(2,1)} %param.9), channel_id=1, source_target_pairs={{0,1},{1,0},{2,3},{3,2},{4,5},{5,4},{6,7},{7,6},{8,9},{9,8},{10,11... | collective-permute-start | bytes 49160 | tf_op jit(solution)/shard_map/ppermute | solution.py:378
  3.0 7.3 %collective-permute-start.1 = (bf16[32,512]{1,0:T(8,128)(2,1)S(1)}, bf16[32,512]{1,0:T(8,128)(2,1)S(1)}, u32[]{:S(2)}, u32[]{:S(2)}) collective-permute-start(bf16[32,512]{1,0:T(8,128)(2,1)S(1)} %constant_dynamic-update-slice_fusion.both), channel_id=1, source_target_pairs={{1,2},{2,1},{3,4},{4,3},{5,6},{6,5},{7,8},{8,7},{9,10},{10,9},{11,... | collective-permute-start | bytes 98312 | tf_op jit(solution)/shard_map/ppermute | solution.py:381
  10.3 3.5 %copy-start.2 = (f32[32]{0:T(128)S(1)}, f32[32]{0:T(128)}, u32[]{:S(2)}) copy-start(f32[32]{0:T(128)} %param.13) | copy-start | bytes 388
  10.3 3.5 %copy-start.1 = (f32[3,32]{1,0:T(4,128)S(1)}, f32[3,32]{1,0:T(4,128)}, u32[]{:S(2)}) copy-start(f32[3,32]{1,0:T(4,128)} %param.15) | copy-start | bytes 1156
  10.3 14.5 %copy-start = (bf16[3,3,3,32,32]{4,3,2,1,0:T(8,128)(2,1)S(1)}, bf16[3,3,3,32,32]{4,3,2,1,0:T(8,128)(2,1)}, u32[]{:S(2)}) copy-start(bf16[3,3,3,32,32]{4,3,2,1,0:T(8,128)(2,1)} %param.14) | copy-start | bytes 165892
  10.3 1.3 %collective-permute-start.2 = (bf16[32,512]{1,0:T(8,128)(2,1)S(1)}, bf16[32,512]{1,0:T(8,128)(2,1)S(1)}, u32[]{:S(2)}, u32[]{:S(2)}) collective-permute-start(bf16[32,512]{1,0:T(8,128)(2,1)S(1)} %collective-permute-done.1.outer), channel_id=1, source_target_pairs={{0,1},{1,0},{2,3},{3,2},{4,5},{5,4},{6,7},{7,6},{8,9},{9,8},{10,11... | collective-permute-start | bytes 98312 | tf_op jit(solution)/shard_map/ppermute | solution.py:390
  13.8 21.8 %all-to-all-start = ((bf16[128,8,128]{2,1,0:T(8,128)(2,1)}), bf16[128,8,128]{2,1,0:T(8,128)(2,1)S(1)}, u32[]{:S(2)}, u32[]{:S(2)}) async-start(bf16[128,8,128]{2,1,0:T(8,128)(2,1)} %get-tuple-element.24), calls=%async_computation | async-start | bytes 524288 | tf_op jit(solution)/shard_map/all_to_all | solution.py:418

commit v12 on v10

--- a/solution.py
+++ b/solution.py
@@ -220,7 +220,8 @@
                 at = [base + DMAX2 + (k - 1) * d for base in bases]
                 taps.append(jnp.concatenate([source[i, :, :width] for i in at], axis=1))
             stack = jnp.concatenate(taps + [tail], axis=0)
-            return jnp.dot(weight[layer], stack, preferred_element_type=jnp.float32)
+            sums = jnp.dot(weight[layer], stack, preferred_element_type=jnp.float32)
+            return sums.astype(jnp.bfloat16)
 
         def finish(bases, sums):
             for n, base in enumerate(bases):
@@ -228,11 +229,10 @@
                     at = slice(n * width, (n + 1) * width)
                     center = source[base + DMAX2 + k * d, chans : 2 * chans, :width]
                     value = sums[k * chans : (k + 1) * chans, at]
+                    value = center + jnp.maximum(value, 0)
                     if final_layer:
-                        value = center.astype(jnp.float32) + jnp.maximum(value, 0.0)
-                        store(base + k * d, value)
+                        store(base + k * d, value.astype(jnp.float32))
                     else:
-                        value = center + jnp.maximum(value.astype(jnp.bfloat16), 0)
                         store(base + k * d, value[:, :128], value[:, 128:])
 
         def walk(start, phase):
@@ -331,7 +331,7 @@
             pltpu.VMEM((span, 3 * chans, LANES), jnp.bfloat16),
             pltpu.VMEM((span - 2 * DMAX2, 3 * chans, LANES), jnp.bfloat16),
             pltpu.VMEM((tile_rows * PITCH, 128), jnp.float32),
-            pltpu.VMEM((GROUP * chans, WIDE * LANES), jnp.float32),
+            pltpu.VMEM((GROUP * chans, WIDE * LANES), jnp.bfloat16),
             pltpu.VMEM((chans, tile_rows, tile_cols), jnp.bfloat16),
             pltpu.SemaphoreType.DMA((tile_rows // CHUNK,)),
         ],

time: 65.5 us -> 63.8 us (0.974); the launches traced: 64.4 us -> 63.8 us
  no operation moved by 1% of the time
where the time goes in v12:
time: 63.8 us
  Pallas kernels  32.2 us (50%)
  starting transfers between devices  15.4 us (24%)
  waiting for transfers between devices  11.1 us (17%)
  local copies, waits for them, and re-layouts  3.11 us (5%)
  other arithmetic  1.21 us (2%)
  between operations  0.79 us (1%)
    pallas_call x1, Pallas kernels, pair_call(): pl.pallas_call(functools.partial(pair_kernel, gathered.shape[0], place.sh...  28.2 us
    all_to_all x1, starting transfers between devices, on_device(): lax.all_to_all(parts, AXES, split_axis=0, concat_axis=0, tiled=True)  10.8 us
    all_to_all x1, waiting for transfers between devices, on_device(): lax.all_to_all(parts, AXES, split_axis=0, concat_axis=0, tiled=True)  9.87 us
    ppermute x1, starting transfers between devices, on_device(): from_outer = lax.ppermute(both, AXES, outer)  3.08 us
    pallas_call x1, Pallas kernels, on_device(): pl.pallas_call(functools.partial(encode_kernel, total), out_shape=[jax.Sh...  2.17 us
    pallas_call x1, Pallas kernels, fetch_call(): pl.pallas_call(fetch_kernel, out_shape=jax.ShapeDtypeStruct(far.shape, fa...  1.88 us
    ppermute x1, starting transfers between devices, on_device(): brought = lax.ppermute(features, AXES, inner)  1.42 us
  transfers between devices with their start and end apart: 4, of which 2 were waited for; matrix products, arithmetic and copies ran while one was open for 7% of the time, Pallas kernels for 3%

profile of v12, /device:TPU:1, one launch (start us, length us, event | category | flops | bytes accessed | tf_op | source)
XLA Modules:
  0.0 63.8 jit_solution(458194968087165696)
XLA Ops:
  0.0 1.4 %collective-permute-start = (bf16[16,512]{1,0:T(8,128)(2,1)}, bf16[16,512]{1,0:T(8,128)(2,1)S(1)}, u32[]{:S(2)}, u32[]{:S(2)}) collective-permute-start(bf16[16,512]{1,0:T(8,128)(2,1)} %param.9), channel_id=1, source_target_pairs={{0,1},{1,0},{2,3},{3,2},{4,5},{5,4},{6,7},{7,6},{8,9},{9,8},{10,11... | collective-permute-start | bytes 49160 | tf_op jit(solution)/shard_map/ppermute | solution.py:377
  2.1 0.1 multiply_cosine_fusion
  2.2 0.1 select_maximum_fusion
  2.3 0.7 %constant_dynamic-update-slice_fusion.1 = bf16[32,512]{1,0:T(8,128)(2,1)S(1)} fusion(bf16[16,512]{1,0:T(8,128)(2,1)} %param.9), kind=kLoop, calls=%fused_computation.41 | loop fusion | bytes 32768
  3.0 0.0 collective-permute-done
  3.0 3.1 %collective-permute-start.1 = (bf16[32,512]{1,0:T(8,128)(2,1)S(1)}, bf16[32,512]{1,0:T(8,128)(2,1)S(1)}, u32[]{:S(2)}, u32[]{:S(2)}) collective-permute-start(bf16[32,512]{1,0:T(8,128)(2,1)S(1)} %constant_dynamic-update-slice_fusion.both), channel_id=1, source_target_pairs={{1,2},{2,1},{3,4},{4,3},{5,6},{6,5},{7,8},{8,7},{9,10},{10,9},{11,... | collective-permute-start | bytes 98312 | tf_op jit(solution)/shard_map/ppermute | solution.py:380
  6.1 0.7 %pad_maximum_fusion.extra = f32[18,512]{1,0:T(8,128)S(1)} fusion(f32[16,512]{1,0:T(8,128)S(1)} %select_maximum_fusion, f32[2,512]{1,0:T(2,128)} %param.11), kind=kLoop, calls=%fused_computation.33 | loop fusion | flops 9216 | bytes 73728 | tf_op jit(solution)/shard_map/concatenate | solution.py:383
  6.8 0.8 %pad.32.proj = bf16[128,512]{1,0:T(8,128)(2,1)S(1)} pad(bf16[64,512]{1,0:T(8,128)(2,1)} %bitcast.20, bf16[]{:T(256)} %constant.34.clone.1), padding=0_64x0_0 | pad | bytes 196610 | tf_op jit(solution)/shard_map/jit(_pad)/pad | solution.py:384
  7.7 0.7 %concatenate.30.place = s32[10]{0:T(128)S(1)} concatenate(s32[1]{0:T(128)} %bitcast.2, s32[1]{0:T(128)} %bitcast.3, s32[1]{0:T(128)} %bitcast.4, s32[1]{0:T(128)} %constant.35.clone.1, s32[1]{0:T(128)} %constant.36.clone.1, s32[5]{0:T(128)} %param.16), dimensions={0} | concatenate | bytes 80 | tf_op jit(solution)/shard_map/concatenate | solution.py:373
  8.4 1.9 %fetch.1.weight = bf16[2,3,512,512]{3,2,1,0:T(8,128)(2,1)S(1)} custom-call(bf16[2,3,512,512]{3,2,1,0:T(8,128)(2,1)} %far), custom_call_target="tpu_custom_call" | custom-call | tf_op jit(solution)/shard_map/fetch/pallas_call | solution.py:46
  10.3 0.0 copy-start.2
  10.3 0.0 copy-start.1
  10.3 0.0 copy-start
  10.3 0.0 collective-permute-done.1.outer
  10.3 0.1 collective-permute-start.2
  10.4 1.2 %collective-permute-done.2.inner = bf16[32,512]{1,0:T(8,128)(2,1)S(1)} collective-permute-done((bf16[32,512]{1,0:T(8,128)(2,1)S(1)}, bf16[32,512]{1,0:T(8,128)(2,1)S(1)}, u32[]{:S(2)}, u32[]{:S(2)}) %collective-permute-start.2) | collective-permute-done | bytes 32800 | tf_op jit(solution)/shard_map/ppermute | solution.py:389
  11.6 2.2 %encode.1 = (bf16[128,8,128]{2,1,0:T(8,128)(2,1)}, bf16[3,3,3,32,32]{4,3,2,1,0:T(8,128)(2,1)S(1)}, f32[4,32]{1,0:T(4,128)S(1)}) custom-call(s32[10]{0:T(128)S(1)} %concatenate.30.place, bf16[32,512]{1,0:T(8,128)(2,1)S(1)} %constant_dynamic-update-slice_fusion.both, bf16[32,512]{1,0:T(8,128)(2,1)S(1)} %collective-permute-done.1.outer, ...), custom_call_target="tpu_custom_call" | custom-call | flops 100663296 | bytes 3145728 | tf_op jit(solution)/shard_map/encode/pallas_call | solution.py:393
  13.8 0.0 copy-done.2
  13.8 0.0 copy-done.1
  13.8 10.8 %all-to-all-start = ((bf16[128,8,128]{2,1,0:T(8,128)(2,1)}), bf16[128,8,128]{2,1,0:T(8,128)(2,1)S(1)}, u32[]{:S(2)}, u32[]{:S(2)}) async-start(bf16[128,8,128]{2,1,0:T(8,128)(2,1)} %get-tuple-element.24), calls=%async_computation | async-start | bytes 524288 | tf_op jit(solution)/shard_map/all_to_all | solution.py:417
  24.7 0.1 copy.30.gain
  24.7 0.1 copy.27
  24.9 0.1 copy.28
  25.0 0.1 copy.29
  25.1 0.0 copy-done
  25.1 0.2 copy.26
  25.3 0.2 reshape.31
  25.5 0.1 fusion.25
  25.6 0.2 fusion.19.weight
  25.8 9.9 %all-to-all-done.parts = bf16[128,8,128]{2,1,0:T(8,128)(2,1)S(1)} async-done(((bf16[128,8,128]{2,1,0:T(8,128)(2,1)}), bf16[128,8,128]{2,1,0:T(8,128)(2,1)S(1)}, u32[]{:S(2)}, u32[]{:S(2)}) %all-to-all-start) | async-done | bytes 262176 | tf_op jit(solution)/shard_map/all_to_all | solution.py:417
  35.6 28.2 %pair_tower.1 = bf16[32,256,128]{2,1,0:T(8,128)(2,1)} custom-call(s32[10]{0:T(128)S(1)} %concatenate.30.place, bf16[128,8,128]{2,1,0:T(8,128)(2,1)S(1)} %all-to-all-done.parts, f32[32,1]{1,0:T(8,128)S(1)} %copy.30.gain, bf16[3,128,608]{2,1,0:T(8,128)(2,1)S(1)} %fusion.19.weight), custom_call_target="tpu_custom_call" | custom-call | flops 3623878656 | bytes 2097152 | tf_op jit(solution)/shard_map/pair_tower/pallas_call | solution.py:323
  (6 shorter events, 0.1 us)
Async XLA Ops:
  0.0 3.0 %collective-permute-start = (bf16[16,512]{1,0:T(8,128)(2,1)}, bf16[16,512]{1,0:T(8,128)(2,1)S(1)}, u32[]{:S(2)}, u32[]{:S(2)}) collective-permute-start(bf16[16,512]{1,0:T(8,128)(2,1)} %param.9), channel_id=1, source_target_pairs={{0,1},{1,0},{2,3},{3,2},{4,5},{5,4},{6,7},{7,6},{8,9},{9,8},{10,11... | collective-permute-start | bytes 49160 | tf_op jit(solution)/shard_map/ppermute | solution.py:377
  3.0 7.3 %collective-permute-start.1 = (bf16[32,512]{1,0:T(8,128)(2,1)S(1)}, bf16[32,512]{1,0:T(8,128)(2,1)S(1)}, u32[]{:S(2)}, u32[]{:S(2)}) collective-permute-start(bf16[32,512]{1,0:T(8,128)(2,1)S(1)} %constant_dynamic-update-slice_fusion.both), channel_id=1, source_target_pairs={{1,2},{2,1},{3,4},{4,3},{5,6},{6,5},{7,8},{8,7},{9,10},{10,9},{11,... | collective-permute-start | bytes 98312 | tf_op jit(solution)/shard_map/ppermute | solution.py:380
  10.3 3.5 %copy-start.2 = (f32[32]{0:T(128)S(1)}, f32[32]{0:T(128)}, u32[]{:S(2)}) copy-start(f32[32]{0:T(128)} %param.13) | copy-start | bytes 388
  10.3 3.5 %copy-start.1 = (f32[3,32]{1,0:T(4,128)S(1)}, f32[3,32]{1,0:T(4,128)}, u32[]{:S(2)}) copy-start(f32[3,32]{1,0:T(4,128)} %param.15) | copy-start | bytes 1156
  10.3 14.8 %copy-start = (bf16[3,3,3,32,32]{4,3,2,1,0:T(8,128)(2,1)S(1)}, bf16[3,3,3,32,32]{4,3,2,1,0:T(8,128)(2,1)}, u32[]{:S(2)}) copy-start(bf16[3,3,3,32,32]{4,3,2,1,0:T(8,128)(2,1)} %param.14) | copy-start | bytes 165892
  10.3 1.3 %collective-permute-start.2 = (bf16[32,512]{1,0:T(8,128)(2,1)S(1)}, bf16[32,512]{1,0:T(8,128)(2,1)S(1)}, u32[]{:S(2)}, u32[]{:S(2)}) collective-permute-start(bf16[32,512]{1,0:T(8,128)(2,1)S(1)} %collective-permute-done.1.outer), channel_id=1, source_target_pairs={{0,1},{1,0},{2,3},{3,2},{4,5},{5,4},{6,7},{7,6},{8,9},{9,8},{10,11... | collective-permute-start | bytes 98312 | tf_op jit(solution)/shard_map/ppermute | solution.py:389
  13.8 21.8 %all-to-all-start = ((bf16[128,8,128]{2,1,0:T(8,128)(2,1)}), bf16[128,8,128]{2,1,0:T(8,128)(2,1)S(1)}, u32[]{:S(2)}, u32[]{:S(2)}) async-start(bf16[128,8,128]{2,1,0:T(8,128)(2,1)} %get-tuple-element.24), calls=%async_computation | async-start | bytes 524288 | tf_op jit(solution)/shard_map/all_to_all | solution.py:417

commit v13 on v10

--- a/solution.py
+++ b/solution.py
@@ -137,13 +137,20 @@
     col_turned = jnp.transpose(cols)[chans : 2 * chans, :]
     col_turned = jnp.where(inside, col_turned, OUTSIDE)
     span0 = tile_rows + 2 * margin
-    blocks = -(-span0 // 128)
-    rows = pieces(row_first // shard - reach, blocks * 128 // shard, blocks * 128)
-    rows = jnp.transpose(rows)[:chans, :]
-    row_glob = row_first - margin + lax.broadcasted_iota(jnp.int32, (1, blocks * 128), 1)
-    rows = jnp.where((row_glob >= 0) & (row_glob < total_shards * shard), rows, OUTSIDE)
-    for k in range(blocks):
-        row_turned[k] = rows[:, k * 128 : (k + 1) * 128]
+    count = -(-span0 // shard)
+    half = shard // 2
+    rows = [
+        parts[jnp.clip(row_first // shard - reach + k, 0, total_shards - 1)] for k in range(count)
+    ]
+    rows = jnp.transpose(jnp.concatenate(rows, axis=0).astype(jnp.float32))
+    spot = lax.broadcasted_iota(jnp.int32, (1, count * half), 1)
+    for side in range(2):
+        row_glob = row_first - margin + spot // half * shard + side * half + spot % half
+        valid = (row_glob >= 0) & (row_glob < total_shards * shard)
+        turned = rows[side * 2 * chans : (side * 2 + 1) * chans, :]
+        turned = jnp.where(valid, turned, OUTSIDE)
+        row_turned[2 * side] = turned[:, :128]
+        row_turned[2 * side + 1, :, : count * half - 128] = turned[:, 128:]
 
     row_local = lax.broadcasted_iota(jnp.int32, (span0, LANES), 0) - margin
     apart = jnp.abs(row_first + row_local - col_glob)
@@ -189,19 +196,19 @@
     store_first = keep(field_a, dils[0], False)
     first_row, last_row_needed = margin - need, margin + tile_rows + need - 1
 
-    def build(index, count):
-        for k in range(count):
-            i = jnp.minimum(first_row + index + k, last_row_needed)
-            pick = jnp.full((chans, 128), i % 128, jnp.int32)
-            row_term = jnp.take_along_axis(row_turned[i // 128], pick, axis=1)
+    @pl.loop(first_row // half, last_row_needed // half + 1)
+    def _(block):
+        first = pl.multiple_of(block * half, half)
+        spot = block // 2 * half
+        turned = row_turned[block % 2 * 2 + spot // 128]
+        apart = distance[pl.ds(first, half), :]
+        for k in range(half):
+            pick = jnp.full((chans, 128), spot % 128 + k, jnp.int32)
+            row_term = jnp.take_along_axis(turned, pick, axis=1)
             row_term = jnp.concatenate([row_term, row_term], axis=1)
-            value = row_term + col_turned + gain_wide * distance[pl.ds(i, 1), :]
+            value = row_term + col_turned + gain_wide * apart[k : k + 1, :]
             value = jnp.maximum(value, 0.0)
-            store_first(i, value[:, :128], value[:, 128:])
-
-    @pl.loop(0, (last_row_needed - first_row + 8) // 8)
-    def _(block):
-        build(block * 8, 8)
+            store_first(first + k, value[:, :128], value[:, 128:])
 
     tail = jnp.ones((TAIL, WIDE * LANES), jnp.bfloat16)
 
@@ -326,7 +333,7 @@
         in_specs=[smem] + [vmem] * 3,
         out_specs=pl.BlockSpec(memory_space=pltpu.HBM),
         scratch_shapes=[
-            pltpu.VMEM((-(-span // 128), chans, 128), jnp.float32),
+            pltpu.VMEM((4, chans, 128), jnp.float32),
             pltpu.VMEM((span, LANES), jnp.float32),
             pltpu.VMEM((span, 3 * chans, LANES), jnp.bfloat16),
             pltpu.VMEM((span - 2 * DMAX2, 3 * chans, LANES), jnp.bfloat16),

time: 65.5 us -> 65.1 us (level); the launches traced: 64.4 us -> 65.5 us
  Pallas kernels: 32.8 us -> 34 us
    pallas_call x1, Pallas kernels: 28.8 us -> 29.9 us  [pair_call(): pl.pallas_call(functools.partial(pair_kernel, gathered.shape[0], place.sh...]
where the time goes in v13:
time: 65.1 us; the launch traced here: 65.5 us
  Pallas kernels  34 us (52%)
  starting transfers between devices  15.4 us (24%)
  waiting for transfers between devices  11.1 us (17%)
  local copies, waits for them, and re-layouts  3.11 us (5%)
  other arithmetic  1.21 us (2%)
  between operations  0.79 us (1%)
    pallas_call x1, Pallas kernels, pair_call(): pl.pallas_call(functools.partial(pair_kernel, gathered.shape[0], place.sh...  29.9 us
    all_to_all x1, starting transfers between devices, on_device(): lax.all_to_all(parts, AXES, split_axis=0, concat_axis=0, tiled=True)  10.8 us
    all_to_all x1, waiting for transfers between devices, on_device(): lax.all_to_all(parts, AXES, split_axis=0, concat_axis=0, tiled=True)  9.87 us
    ppermute x1, starting transfers between devices, on_device(): from_outer = lax.ppermute(both, AXES, outer)  3.08 us
    pallas_call x1, Pallas kernels, on_device(): pl.pallas_call(functools.partial(encode_kernel, total), out_shape=[jax.Sh...  2.17 us
    pallas_call x1, Pallas kernels, fetch_call(): pl.pallas_call(fetch_kernel, out_shape=jax.ShapeDtypeStruct(far.shape, fa...  1.88 us
    ppermute x1, starting transfers between devices, on_device(): brought = lax.ppermute(features, AXES, inner)  1.42 us
  transfers between devices with their start and end apart: 4, of which 2 were waited for; matrix products, arithmetic and copies ran while one was open for 7% of the time, Pallas kernels for 3%

profile of v13, /device:TPU:1, one launch (start us, length us, event | category | flops | bytes accessed | tf_op | source)
XLA Modules:
  0.0 65.5 jit_solution(16423702238140022977)
XLA Ops:
  0.0 1.4 %collective-permute-start = (bf16[16,512]{1,0:T(8,128)(2,1)}, bf16[16,512]{1,0:T(8,128)(2,1)S(1)}, u32[]{:S(2)}, u32[]{:S(2)}) collective-permute-start(bf16[16,512]{1,0:T(8,128)(2,1)} %param.9), channel_id=1, source_target_pairs={{0,1},{1,0},{2,3},{3,2},{4,5},{5,4},{6,7},{7,6},{8,9},{9,8},{10,11... | collective-permute-start | bytes 49160 | tf_op jit(solution)/shard_map/ppermute | solution.py:384
  2.1 0.1 multiply_cosine_fusion
  2.2 0.1 select_maximum_fusion
  2.3 0.7 %constant_dynamic-update-slice_fusion.1 = bf16[32,512]{1,0:T(8,128)(2,1)S(1)} fusion(bf16[16,512]{1,0:T(8,128)(2,1)} %param.9), kind=kLoop, calls=%fused_computation.41 | loop fusion | bytes 32768
  3.0 0.0 collective-permute-done
  3.0 3.1 %collective-permute-start.1 = (bf16[32,512]{1,0:T(8,128)(2,1)S(1)}, bf16[32,512]{1,0:T(8,128)(2,1)S(1)}, u32[]{:S(2)}, u32[]{:S(2)}) collective-permute-start(bf16[32,512]{1,0:T(8,128)(2,1)S(1)} %constant_dynamic-update-slice_fusion.both), channel_id=1, source_target_pairs={{1,2},{2,1},{3,4},{4,3},{5,6},{6,5},{7,8},{8,7},{9,10},{10,9},{11,... | collective-permute-start | bytes 98312 | tf_op jit(solution)/shard_map/ppermute | solution.py:387
  6.1 0.7 %pad_maximum_fusion.extra = f32[18,512]{1,0:T(8,128)S(1)} fusion(f32[16,512]{1,0:T(8,128)S(1)} %select_maximum_fusion, f32[2,512]{1,0:T(2,128)} %param.11), kind=kLoop, calls=%fused_computation.33 | loop fusion | flops 9216 | bytes 73728 | tf_op jit(solution)/shard_map/concatenate | solution.py:390
  6.8 0.8 %pad.32.proj = bf16[128,512]{1,0:T(8,128)(2,1)S(1)} pad(bf16[64,512]{1,0:T(8,128)(2,1)} %bitcast.20, bf16[]{:T(256)} %constant.34.clone.1), padding=0_64x0_0 | pad | bytes 196610 | tf_op jit(solution)/shard_map/jit(_pad)/pad | solution.py:391
  7.7 0.7 %concatenate.30.place = s32[10]{0:T(128)S(1)} concatenate(s32[1]{0:T(128)} %bitcast.2, s32[1]{0:T(128)} %bitcast.3, s32[1]{0:T(128)} %bitcast.4, s32[1]{0:T(128)} %constant.35.clone.1, s32[1]{0:T(128)} %constant.36.clone.1, s32[5]{0:T(128)} %param.16), dimensions={0} | concatenate | bytes 80 | tf_op jit(solution)/shard_map/concatenate | solution.py:380
  8.4 1.9 %fetch.1.weight = bf16[2,3,512,512]{3,2,1,0:T(8,128)(2,1)S(1)} custom-call(bf16[2,3,512,512]{3,2,1,0:T(8,128)(2,1)} %far), custom_call_target="tpu_custom_call" | custom-call | tf_op jit(solution)/shard_map/fetch/pallas_call | solution.py:46
  10.3 0.0 copy-start.2
  10.3 0.0 copy-start.1
  10.3 0.0 copy-start
  10.3 0.0 collective-permute-done.1.outer
  10.3 0.1 collective-permute-start.2
  10.4 1.2 %collective-permute-done.2.inner = bf16[32,512]{1,0:T(8,128)(2,1)S(1)} collective-permute-done((bf16[32,512]{1,0:T(8,128)(2,1)S(1)}, bf16[32,512]{1,0:T(8,128)(2,1)S(1)}, u32[]{:S(2)}, u32[]{:S(2)}) %collective-permute-start.2) | collective-permute-done | bytes 32800 | tf_op jit(solution)/shard_map/ppermute | solution.py:396
  11.6 2.2 %encode.1 = (bf16[128,8,128]{2,1,0:T(8,128)(2,1)}, bf16[3,3,3,32,32]{4,3,2,1,0:T(8,128)(2,1)S(1)}, f32[4,32]{1,0:T(4,128)S(1)}) custom-call(s32[10]{0:T(128)S(1)} %concatenate.30.place, bf16[32,512]{1,0:T(8,128)(2,1)S(1)} %constant_dynamic-update-slice_fusion.both, bf16[32,512]{1,0:T(8,128)(2,1)S(1)} %collective-permute-done.1.outer, ...), custom_call_target="tpu_custom_call" | custom-call | flops 100663296 | bytes 3145728 | tf_op jit(solution)/shard_map/encode/pallas_call | solution.py:400
  13.8 0.0 copy-done.2
  13.8 0.0 copy-done.1
  13.8 10.8 %all-to-all-start = ((bf16[128,8,128]{2,1,0:T(8,128)(2,1)}), bf16[128,8,128]{2,1,0:T(8,128)(2,1)S(1)}, u32[]{:S(2)}, u32[]{:S(2)}) async-start(bf16[128,8,128]{2,1,0:T(8,128)(2,1)} %get-tuple-element.24), calls=%async_computation | async-start | bytes 524288 | tf_op jit(solution)/shard_map/all_to_all | solution.py:424
  24.6 0.1 copy.30.gain
  24.7 0.1 copy.27
  24.9 0.1 copy.28
  25.0 0.1 copy.29
  25.1 0.0 copy-done
  25.1 0.2 copy.26
  25.3 0.2 reshape.31
  25.5 0.1 fusion.25
  25.6 0.2 fusion.19.weight
  25.8 9.9 %all-to-all-done.parts = bf16[128,8,128]{2,1,0:T(8,128)(2,1)S(1)} async-done(((bf16[128,8,128]{2,1,0:T(8,128)(2,1)}), bf16[128,8,128]{2,1,0:T(8,128)(2,1)S(1)}, u32[]{:S(2)}, u32[]{:S(2)}) %all-to-all-start) | async-done | bytes 262176 | tf_op jit(solution)/shard_map/all_to_all | solution.py:424
  35.6 29.9 %pair_tower.1 = bf16[32,256,128]{2,1,0:T(8,128)(2,1)} custom-call(s32[10]{0:T(128)S(1)} %concatenate.30.place, bf16[128,8,128]{2,1,0:T(8,128)(2,1)S(1)} %all-to-all-done.parts, f32[32,1]{1,0:T(8,128)S(1)} %copy.30.gain, bf16[3,128,608]{2,1,0:T(8,128)(2,1)S(1)} %fusion.19.weight), custom_call_target="tpu_custom_call" | custom-call | flops 3623878656 | bytes 2097152 | tf_op jit(solution)/shard_map/pair_tower/pallas_call | solution.py:330
  (6 shorter events, 0.1 us)
Async XLA Ops:
  0.0 3.0 %collective-permute-start = (bf16[16,512]{1,0:T(8,128)(2,1)}, bf16[16,512]{1,0:T(8,128)(2,1)S(1)}, u32[]{:S(2)}, u32[]{:S(2)}) collective-permute-start(bf16[16,512]{1,0:T(8,128)(2,1)} %param.9), channel_id=1, source_target_pairs={{0,1},{1,0},{2,3},{3,2},{4,5},{5,4},{6,7},{7,6},{8,9},{9,8},{10,11... | collective-permute-start | bytes 49160 | tf_op jit(solution)/shard_map/ppermute | solution.py:384
  3.0 7.3 %collective-permute-start.1 = (bf16[32,512]{1,0:T(8,128)(2,1)S(1)}, bf16[32,512]{1,0:T(8,128)(2,1)S(1)}, u32[]{:S(2)}, u32[]{:S(2)}) collective-permute-start(bf16[32,512]{1,0:T(8,128)(2,1)S(1)} %constant_dynamic-update-slice_fusion.both), channel_id=1, source_target_pairs={{1,2},{2,1},{3,4},{4,3},{5,6},{6,5},{7,8},{8,7},{9,10},{10,9},{11,... | collective-permute-start | bytes 98312 | tf_op jit(solution)/shard_map/ppermute | solution.py:387
  10.3 3.5 %copy-start.2 = (f32[32]{0:T(128)S(1)}, f32[32]{0:T(128)}, u32[]{:S(2)}) copy-start(f32[32]{0:T(128)} %param.13) | copy-start | bytes 388
  10.3 3.5 %copy-start.1 = (f32[3,32]{1,0:T(4,128)S(1)}, f32[3,32]{1,0:T(4,128)}, u32[]{:S(2)}) copy-start(f32[3,32]{1,0:T(4,128)} %param.15) | copy-start | bytes 1156
  10.3 14.8 %copy-start = (bf16[3,3,3,32,32]{4,3,2,1,0:T(8,128)(2,1)S(1)}, bf16[3,3,3,32,32]{4,3,2,1,0:T(8,128)(2,1)}, u32[]{:S(2)}) copy-start(bf16[3,3,3,32,32]{4,3,2,1,0:T(8,128)(2,1)} %param.14) | copy-start | bytes 165892
  10.3 1.3 %collective-permute-start.2 = (bf16[32,512]{1,0:T(8,128)(2,1)S(1)}, bf16[32,512]{1,0:T(8,128)(2,1)S(1)}, u32[]{:S(2)}, u32[]{:S(2)}) collective-permute-start(bf16[32,512]{1,0:T(8,128)(2,1)S(1)} %collective-permute-done.1.outer), channel_id=1, source_target_pairs={{0,1},{1,0},{2,3},{3,2},{4,5},{5,4},{6,7},{7,6},{8,9},{9,8},{10,11... | collective-permute-start | bytes 98312 | tf_op jit(solution)/shard_map/ppermute | solution.py:396
  13.8 21.8 %all-to-all-start = ((bf16[128,8,128]{2,1,0:T(8,128)(2,1)}), bf16[128,8,128]{2,1,0:T(8,128)(2,1)S(1)}, u32[]{:S(2)}, u32[]{:S(2)}) async-start(bf16[128,8,128]{2,1,0:T(8,128)(2,1)} %get-tuple-element.24), calls=%async_computation | async-start | bytes 524288 | tf_op jit(solution)/shard_map/all_to_all | solution.py:424

commit v14 on v13

--- a/solution.py
+++ b/solution.py
@@ -158,7 +158,7 @@
     gain_wide = jnp.broadcast_to(gain[...], (chans, LANES))
     lane16 = lax.broadcasted_iota(jnp.int16, (chans, 128), 1)
 
-    def keep(field, d, masked):
+    def keep(field, d, masked, narrow=False):
         back = 128 - d
         at_left = lane16 < d.astype(jnp.int16)
         at_right = lane16 >= back.astype(jnp.int16)
@@ -169,13 +169,15 @@
             if masked:
                 high = high * inside_high
             field[i, chans : 2 * chans, :128] = low
-            field[i, chans : 2 * chans, 128:] = high
             turned_low, turned_high = pltpu.roll(low, d, 1), pltpu.roll(high, d, 1)
             field[i, :chans, :128] = jnp.where(at_left, turned_high, turned_low)
-            field[i, :chans, 128:] = jnp.where(at_left, turned_low, turned_high)
+            if not narrow:
+                field[i, chans : 2 * chans, 128:] = high
+                field[i, :chans, 128:] = jnp.where(at_left, turned_low, turned_high)
             turned_low, turned_high = pltpu.roll(low, back, 1), pltpu.roll(high, back, 1)
             field[i, 2 * chans :, :128] = jnp.where(at_right, turned_high, turned_low)
-            field[i, 2 * chans :, 128:] = jnp.where(at_right, turned_low, turned_high)
+            if not narrow:
+                field[i, 2 * chans :, 128:] = jnp.where(at_right, turned_low, turned_high)
 
         return store
 
@@ -293,7 +295,7 @@
 
     tower(0, field_a, 2 * DMAX2, dils[1] + dils[2], keep(field_b, dils[1], True))
     clear(field_b, 2 * DMAX2)
-    tower(1, field_b, DMAX2, dils[2], keep(field_a, dils[2], True))
+    tower(1, field_b, DMAX2, dils[2], keep(field_a, dils[2], True, True))
     clear(field_a, DMAX2)
     tower(2, field_a, 0, 0, keep_last, turn_early)
 

time: 65.1 us -> 65 us (level); the launches traced: 65.5 us -> 64.4 us
  Pallas kernels: 34 us -> 32.9 us
    pallas_call x1, Pallas kernels: 29.9 us -> 28.8 us  [pair_call(): pl.pallas_call(functools.partial(pair_kernel, gathered.shape[0], place.sh...]
where the time goes in v14:
time: 65 us; the launch traced here: 64.4 us
  Pallas kernels  32.9 us (51%)
  starting transfers between devices  15.4 us (24%)
  waiting for transfers between devices  11.1 us (17%)
  local copies, waits for them, and re-layouts  3.11 us (5%)
  other arithmetic  1.21 us (2%)
  between operations  0.79 us (1%)
    pallas_call x1, Pallas kernels, pair_call(): pl.pallas_call(functools.partial(pair_kernel, gathered.shape[0], place.sh...  28.8 us
    all_to_all x1, starting transfers between devices, on_device(): lax.all_to_all(parts, AXES, split_axis=0, concat_axis=0, tiled=True)  10.8 us
    all_to_all x1, waiting for transfers between devices, on_device(): lax.all_to_all(parts, AXES, split_axis=0, concat_axis=0, tiled=True)  9.87 us
    ppermute x1, starting transfers between devices, on_device(): from_outer = lax.ppermute(both, AXES, outer)  3.08 us
    pallas_call x1, Pallas kernels, on_device(): pl.pallas_call(functools.partial(encode_kernel, total), out_shape=[jax.Sh...  2.17 us
    pallas_call x1, Pallas kernels, fetch_call(): pl.pallas_call(fetch_kernel, out_shape=jax.ShapeDtypeStruct(far.shape, fa...  1.88 us
    ppermute x1, starting transfers between devices, on_device(): brought = lax.ppermute(features, AXES, inner)  1.42 us
  transfers between devices with their start and end apart: 4, of which 2 were waited for; matrix products, arithmetic and copies ran while one was open for 7% of the time, Pallas kernels for 3%

profile of v14, /device:TPU:1, one launch (start us, length us, event | category | flops | bytes accessed | tf_op | source)
XLA Modules:
  0.0 64.4 jit_solution(12415339545991014892)
XLA Ops:
  0.0 1.4 %collective-permute-start = (bf16[16,512]{1,0:T(8,128)(2,1)}, bf16[16,512]{1,0:T(8,128)(2,1)S(1)}, u32[]{:S(2)}, u32[]{:S(2)}) collective-permute-start(bf16[16,512]{1,0:T(8,128)(2,1)} %param.9), channel_id=1, source_target_pairs={{0,1},{1,0},{2,3},{3,2},{4,5},{5,4},{6,7},{7,6},{8,9},{9,8},{10,11... | collective-permute-start | bytes 49160 | tf_op jit(solution)/shard_map/ppermute | solution.py:386
  2.1 0.1 multiply_cosine_fusion
  2.2 0.1 select_maximum_fusion
  2.3 0.7 %constant_dynamic-update-slice_fusion.1 = bf16[32,512]{1,0:T(8,128)(2,1)S(1)} fusion(bf16[16,512]{1,0:T(8,128)(2,1)} %param.9), kind=kLoop, calls=%fused_computation.41 | loop fusion | bytes 32768
  3.0 0.0 collective-permute-done
  3.0 3.1 %collective-permute-start.1 = (bf16[32,512]{1,0:T(8,128)(2,1)S(1)}, bf16[32,512]{1,0:T(8,128)(2,1)S(1)}, u32[]{:S(2)}, u32[]{:S(2)}) collective-permute-start(bf16[32,512]{1,0:T(8,128)(2,1)S(1)} %constant_dynamic-update-slice_fusion.both), channel_id=1, source_target_pairs={{1,2},{2,1},{3,4},{4,3},{5,6},{6,5},{7,8},{8,7},{9,10},{10,9},{11,... | collective-permute-start | bytes 98312 | tf_op jit(solution)/shard_map/ppermute | solution.py:389
  6.1 0.7 %pad_maximum_fusion.extra = f32[18,512]{1,0:T(8,128)S(1)} fusion(f32[16,512]{1,0:T(8,128)S(1)} %select_maximum_fusion, f32[2,512]{1,0:T(2,128)} %param.11), kind=kLoop, calls=%fused_computation.33 | loop fusion | flops 9216 | bytes 73728 | tf_op jit(solution)/shard_map/concatenate | solution.py:392
  6.8 0.8 %pad.32.proj = bf16[128,512]{1,0:T(8,128)(2,1)S(1)} pad(bf16[64,512]{1,0:T(8,128)(2,1)} %bitcast.20, bf16[]{:T(256)} %constant.34.clone.1), padding=0_64x0_0 | pad | bytes 196610 | tf_op jit(solution)/shard_map/jit(_pad)/pad | solution.py:393
  7.7 0.7 %concatenate.30.place = s32[10]{0:T(128)S(1)} concatenate(s32[1]{0:T(128)} %bitcast.2, s32[1]{0:T(128)} %bitcast.3, s32[1]{0:T(128)} %bitcast.4, s32[1]{0:T(128)} %constant.35.clone.1, s32[1]{0:T(128)} %constant.36.clone.1, s32[5]{0:T(128)} %param.16), dimensions={0} | concatenate | bytes 80 | tf_op jit(solution)/shard_map/concatenate | solution.py:382
  8.4 1.9 %fetch.1.weight = bf16[2,3,512,512]{3,2,1,0:T(8,128)(2,1)S(1)} custom-call(bf16[2,3,512,512]{3,2,1,0:T(8,128)(2,1)} %far), custom_call_target="tpu_custom_call" | custom-call | tf_op jit(solution)/shard_map/fetch/pallas_call | solution.py:46
  10.3 0.0 copy-start.2
  10.3 0.0 copy-start.1
  10.3 0.0 copy-start
  10.3 0.0 collective-permute-done.1.outer
  10.3 0.1 collective-permute-start.2
  10.4 1.2 %collective-permute-done.2.inner = bf16[32,512]{1,0:T(8,128)(2,1)S(1)} collective-permute-done((bf16[32,512]{1,0:T(8,128)(2,1)S(1)}, bf16[32,512]{1,0:T(8,128)(2,1)S(1)}, u32[]{:S(2)}, u32[]{:S(2)}) %collective-permute-start.2) | collective-permute-done | bytes 32800 | tf_op jit(solution)/shard_map/ppermute | solution.py:398
  11.6 2.2 %encode.1 = (bf16[128,8,128]{2,1,0:T(8,128)(2,1)}, bf16[3,3,3,32,32]{4,3,2,1,0:T(8,128)(2,1)S(1)}, f32[4,32]{1,0:T(4,128)S(1)}) custom-call(s32[10]{0:T(128)S(1)} %concatenate.30.place, bf16[32,512]{1,0:T(8,128)(2,1)S(1)} %constant_dynamic-update-slice_fusion.both, bf16[32,512]{1,0:T(8,128)(2,1)S(1)} %collective-permute-done.1.outer, ...), custom_call_target="tpu_custom_call" | custom-call | flops 100663296 | bytes 3145728 | tf_op jit(solution)/shard_map/encode/pallas_call | solution.py:402
  13.8 0.0 copy-done.2
  13.8 0.0 copy-done.1
  13.8 10.8 %all-to-all-start = ((bf16[128,8,128]{2,1,0:T(8,128)(2,1)}), bf16[128,8,128]{2,1,0:T(8,128)(2,1)S(1)}, u32[]{:S(2)}, u32[]{:S(2)}) async-start(bf16[128,8,128]{2,1,0:T(8,128)(2,1)} %get-tuple-element.24), calls=%async_computation | async-start | bytes 524288 | tf_op jit(solution)/shard_map/all_to_all | solution.py:426
  24.7 0.1 copy.30.gain
  24.7 0.1 copy.27
  24.9 0.1 copy.28
  25.0 0.1 copy.29
  25.1 0.0 copy-done
  25.1 0.2 copy.26
  25.3 0.2 reshape.31
  25.5 0.1 fusion.25
  25.6 0.2 fusion.19.weight
  25.8 9.9 %all-to-all-done.parts = bf16[128,8,128]{2,1,0:T(8,128)(2,1)S(1)} async-done(((bf16[128,8,128]{2,1,0:T(8,128)(2,1)}), bf16[128,8,128]{2,1,0:T(8,128)(2,1)S(1)}, u32[]{:S(2)}, u32[]{:S(2)}) %all-to-all-start) | async-done | bytes 262176 | tf_op jit(solution)/shard_map/all_to_all | solution.py:426
  35.6 28.8 %pair_tower.1 = bf16[32,256,128]{2,1,0:T(8,128)(2,1)} custom-call(s32[10]{0:T(128)S(1)} %concatenate.30.place, bf16[128,8,128]{2,1,0:T(8,128)(2,1)S(1)} %all-to-all-done.parts, f32[32,1]{1,0:T(8,128)S(1)} %copy.30.gain, bf16[3,128,608]{2,1,0:T(8,128)(2,1)S(1)} %fusion.19.weight), custom_call_target="tpu_custom_call" | custom-call | flops 3623878656 | bytes 2097152 | tf_op jit(solution)/shard_map/pair_tower/pallas_call | solution.py:332
  (6 shorter events, 0.1 us)
Async XLA Ops:
  0.0 3.0 %collective-permute-start = (bf16[16,512]{1,0:T(8,128)(2,1)}, bf16[16,512]{1,0:T(8,128)(2,1)S(1)}, u32[]{:S(2)}, u32[]{:S(2)}) collective-permute-start(bf16[16,512]{1,0:T(8,128)(2,1)} %param.9), channel_id=1, source_target_pairs={{0,1},{1,0},{2,3},{3,2},{4,5},{5,4},{6,7},{7,6},{8,9},{9,8},{10,11... | collective-permute-start | bytes 49160 | tf_op jit(solution)/shard_map/ppermute | solution.py:386
  3.0 7.3 %collective-permute-start.1 = (bf16[32,512]{1,0:T(8,128)(2,1)S(1)}, bf16[32,512]{1,0:T(8,128)(2,1)S(1)}, u32[]{:S(2)}, u32[]{:S(2)}) collective-permute-start(bf16[32,512]{1,0:T(8,128)(2,1)S(1)} %constant_dynamic-update-slice_fusion.both), channel_id=1, source_target_pairs={{1,2},{2,1},{3,4},{4,3},{5,6},{6,5},{7,8},{8,7},{9,10},{10,9},{11,... | collective-permute-start | bytes 98312 | tf_op jit(solution)/shard_map/ppermute | solution.py:389
  10.3 3.5 %copy-start.2 = (f32[32]{0:T(128)S(1)}, f32[32]{0:T(128)}, u32[]{:S(2)}) copy-start(f32[32]{0:T(128)} %param.13) | copy-start | bytes 388
  10.3 3.5 %copy-start.1 = (f32[3,32]{1,0:T(4,128)S(1)}, f32[3,32]{1,0:T(4,128)}, u32[]{:S(2)}) copy-start(f32[3,32]{1,0:T(4,128)} %param.15) | copy-start | bytes 1156
  10.3 14.8 %copy-start = (bf16[3,3,3,32,32]{4,3,2,1,0:T(8,128)(2,1)S(1)}, bf16[3,3,3,32,32]{4,3,2,1,0:T(8,128)(2,1)}, u32[]{:S(2)}) copy-start(bf16[3,3,3,32,32]{4,3,2,1,0:T(8,128)(2,1)} %param.14) | copy-start | bytes 165892
  10.3 1.3 %collective-permute-start.2 = (bf16[32,512]{1,0:T(8,128)(2,1)S(1)}, bf16[32,512]{1,0:T(8,128)(2,1)S(1)}, u32[]{:S(2)}, u32[]{:S(2)}) collective-permute-start(bf16[32,512]{1,0:T(8,128)(2,1)S(1)} %collective-permute-done.1.outer), channel_id=1, source_target_pairs={{0,1},{1,0},{2,3},{3,2},{4,5},{5,4},{6,7},{7,6},{8,9},{9,8},{10,11... | collective-permute-start | bytes 98312 | tf_op jit(solution)/shard_map/ppermute | solution.py:398
  13.8 21.8 %all-to-all-start = ((bf16[128,8,128]{2,1,0:T(8,128)(2,1)}), bf16[128,8,128]{2,1,0:T(8,128)(2,1)S(1)}, u32[]{:S(2)}, u32[]{:S(2)}) async-start(bf16[128,8,128]{2,1,0:T(8,128)(2,1)} %get-tuple-element.24), calls=%async_computation | async-start | bytes 524288 | tf_op jit(solution)/shard_map/all_to_all | solution.py:426

commit v15 on v14

--- a/solution.py
+++ b/solution.py
@@ -13,7 +13,7 @@
 GROUP = 4
 TAIL = 32
 WIDE = 2
-UNROLL = 4
+UNROLL = (6, 6, 4)
 LANES = 256
 PITCH = 40
 FETCH_LIMIT = 50
@@ -258,7 +258,7 @@
             if first_in_step is not None:
                 first_in_step(index)
             sums = held
-            for k in range(UNROLL):
+            for _ in range(UNROLL[layer]):
                 next_bases, start, phase = walk(start, phase)
                 next_sums = product(next_bases)
                 finish(bases, sums)
@@ -268,7 +268,8 @@
 
         zero = jnp.int32(0)
         total = (count + span - 1) // span * d
-        steps = (total + UNROLL * each - 1) // (UNROLL * each)
+        together = UNROLL[layer] * each
+        steps = (total + together - 1) // together
         carry = lax.fori_loop(0, steps, step, (zero, zero, walk(zero, zero)[0]))
         finish(carry[2], held)
 

time: 65 us -> 63.8 us (0.982); the launches traced: 64.4 us -> 64.1 us
  no operation moved by 1% of the time
where the time goes in v15:
time: 63.8 us; the launch traced here: 64.1 us
  Pallas kernels  32.5 us (51%)
  starting transfers between devices  15.4 us (24%)
  waiting for transfers between devices  11.1 us (17%)
  local copies, waits for them, and re-layouts  3.11 us (5%)
  other arithmetic  1.21 us (2%)
  between operations  0.79 us (1%)
    pallas_call x1, Pallas kernels, pair_call(): pl.pallas_call(functools.partial(pair_kernel, gathered.shape[0], place.sh...  28.5 us
    all_to_all x1, starting transfers between devices, on_device(): lax.all_to_all(parts, AXES, split_axis=0, concat_axis=0, tiled=True)  10.8 us
    all_to_all x1, waiting for transfers between devices, on_device(): lax.all_to_all(parts, AXES, split_axis=0, concat_axis=0, tiled=True)  9.87 us
    ppermute x1, starting transfers between devices, on_device(): from_outer = lax.ppermute(both, AXES, outer)  3.08 us
    pallas_call x1, Pallas kernels, on_device(): pl.pallas_call(functools.partial(encode_kernel, total), out_shape=[jax.Sh...  2.17 us
    pallas_call x1, Pallas kernels, fetch_call(): pl.pallas_call(fetch_kernel, out_shape=jax.ShapeDtypeStruct(far.shape, fa...  1.88 us
    ppermute x1, starting transfers between devices, on_device(): brought = lax.ppermute(features, AXES, inner)  1.42 us
  transfers between devices with their start and end apart: 4, of which 2 were waited for; matrix products, arithmetic and copies ran while one was open for 7% of the time, Pallas kernels for 3%

profile of v15, /device:TPU:1, one launch (start us, length us, event | category | flops | bytes accessed | tf_op | source)
XLA Modules:
  0.0 64.1 jit_solution(13267753091520435193)
XLA Ops:
  0.0 1.4 %collective-permute-start = (bf16[16,512]{1,0:T(8,128)(2,1)}, bf16[16,512]{1,0:T(8,128)(2,1)S(1)}, u32[]{:S(2)}, u32[]{:S(2)}) collective-permute-start(bf16[16,512]{1,0:T(8,128)(2,1)} %param.9), channel_id=1, source_target_pairs={{0,1},{1,0},{2,3},{3,2},{4,5},{5,4},{6,7},{7,6},{8,9},{9,8},{10,11... | collective-permute-start | bytes 49160 | tf_op jit(solution)/shard_map/ppermute | solution.py:387
  2.1 0.1 multiply_cosine_fusion
  2.2 0.1 select_maximum_fusion
  2.3 0.7 %constant_dynamic-update-slice_fusion.1 = bf16[32,512]{1,0:T(8,128)(2,1)S(1)} fusion(bf16[16,512]{1,0:T(8,128)(2,1)} %param.9), kind=kLoop, calls=%fused_computation.41 | loop fusion | bytes 32768
  3.0 0.0 collective-permute-done
  3.0 3.1 %collective-permute-start.1 = (bf16[32,512]{1,0:T(8,128)(2,1)S(1)}, bf16[32,512]{1,0:T(8,128)(2,1)S(1)}, u32[]{:S(2)}, u32[]{:S(2)}) collective-permute-start(bf16[32,512]{1,0:T(8,128)(2,1)S(1)} %constant_dynamic-update-slice_fusion.both), channel_id=1, source_target_pairs={{1,2},{2,1},{3,4},{4,3},{5,6},{6,5},{7,8},{8,7},{9,10},{10,9},{11,... | collective-permute-start | bytes 98312 | tf_op jit(solution)/shard_map/ppermute | solution.py:390
  6.1 0.7 %pad_maximum_fusion.extra = f32[18,512]{1,0:T(8,128)S(1)} fusion(f32[16,512]{1,0:T(8,128)S(1)} %select_maximum_fusion, f32[2,512]{1,0:T(2,128)} %param.11), kind=kLoop, calls=%fused_computation.33 | loop fusion | flops 9216 | bytes 73728 | tf_op jit(solution)/shard_map/concatenate | solution.py:393
  6.8 0.8 %pad.32.proj = bf16[128,512]{1,0:T(8,128)(2,1)S(1)} pad(bf16[64,512]{1,0:T(8,128)(2,1)} %bitcast.20, bf16[]{:T(256)} %constant.34.clone.1), padding=0_64x0_0 | pad | bytes 196610 | tf_op jit(solution)/shard_map/jit(_pad)/pad | solution.py:394
  7.7 0.7 %concatenate.30.place = s32[10]{0:T(128)S(1)} concatenate(s32[1]{0:T(128)} %bitcast.2, s32[1]{0:T(128)} %bitcast.3, s32[1]{0:T(128)} %bitcast.4, s32[1]{0:T(128)} %constant.35.clone.1, s32[1]{0:T(128)} %constant.36.clone.1, s32[5]{0:T(128)} %param.16), dimensions={0} | concatenate | bytes 80 | tf_op jit(solution)/shard_map/concatenate | solution.py:383
  8.4 1.9 %fetch.1.weight = bf16[2,3,512,512]{3,2,1,0:T(8,128)(2,1)S(1)} custom-call(bf16[2,3,512,512]{3,2,1,0:T(8,128)(2,1)} %far), custom_call_target="tpu_custom_call" | custom-call | tf_op jit(solution)/shard_map/fetch/pallas_call | solution.py:46
  10.3 0.0 copy-start.2
  10.3 0.0 copy-start.1
  10.3 0.0 copy-start
  10.3 0.0 collective-permute-done.1.outer
  10.3 0.1 collective-permute-start.2
  10.4 1.2 %collective-permute-done.2.inner = bf16[32,512]{1,0:T(8,128)(2,1)S(1)} collective-permute-done((bf16[32,512]{1,0:T(8,128)(2,1)S(1)}, bf16[32,512]{1,0:T(8,128)(2,1)S(1)}, u32[]{:S(2)}, u32[]{:S(2)}) %collective-permute-start.2) | collective-permute-done | bytes 32800 | tf_op jit(solution)/shard_map/ppermute | solution.py:399
  11.6 2.2 %encode.1 = (bf16[128,8,128]{2,1,0:T(8,128)(2,1)}, bf16[3,3,3,32,32]{4,3,2,1,0:T(8,128)(2,1)S(1)}, f32[4,32]{1,0:T(4,128)S(1)}) custom-call(s32[10]{0:T(128)S(1)} %concatenate.30.place, bf16[32,512]{1,0:T(8,128)(2,1)S(1)} %constant_dynamic-update-slice_fusion.both, bf16[32,512]{1,0:T(8,128)(2,1)S(1)} %collective-permute-done.1.outer, ...), custom_call_target="tpu_custom_call" | custom-call | flops 100663296 | bytes 3145728 | tf_op jit(solution)/shard_map/encode/pallas_call | solution.py:403
  13.8 0.0 copy-done.2
  13.8 0.0 copy-done.1
  13.8 10.8 %all-to-all-start = ((bf16[128,8,128]{2,1,0:T(8,128)(2,1)}), bf16[128,8,128]{2,1,0:T(8,128)(2,1)S(1)}, u32[]{:S(2)}, u32[]{:S(2)}) async-start(bf16[128,8,128]{2,1,0:T(8,128)(2,1)} %get-tuple-element.24), calls=%async_computation | async-start | bytes 524288 | tf_op jit(solution)/shard_map/all_to_all | solution.py:427
  24.6 0.1 copy.30.gain
  24.7 0.1 copy.27
  24.9 0.1 copy.28
  25.0 0.1 copy.29
  25.1 0.0 copy-done
  25.1 0.2 copy.26
  25.3 0.2 reshape.31
  25.5 0.1 fusion.25
  25.6 0.2 fusion.19.weight
  25.8 9.9 %all-to-all-done.parts = bf16[128,8,128]{2,1,0:T(8,128)(2,1)S(1)} async-done(((bf16[128,8,128]{2,1,0:T(8,128)(2,1)}), bf16[128,8,128]{2,1,0:T(8,128)(2,1)S(1)}, u32[]{:S(2)}, u32[]{:S(2)}) %all-to-all-start) | async-done | bytes 262176 | tf_op jit(solution)/shard_map/all_to_all | solution.py:427
  35.6 28.5 %pair_tower.1 = bf16[32,256,128]{2,1,0:T(8,128)(2,1)} custom-call(s32[10]{0:T(128)S(1)} %concatenate.30.place, bf16[128,8,128]{2,1,0:T(8,128)(2,1)S(1)} %all-to-all-done.parts, f32[32,1]{1,0:T(8,128)S(1)} %copy.30.gain, bf16[3,128,608]{2,1,0:T(8,128)(2,1)S(1)} %fusion.19.weight), custom_call_target="tpu_custom_call" | custom-call | flops 3623878656 | bytes 2097152 | tf_op jit(solution)/shard_map/pair_tower/pallas_call | solution.py:333
  (6 shorter events, 0.1 us)
Async XLA Ops:
  0.0 3.0 %collective-permute-start = (bf16[16,512]{1,0:T(8,128)(2,1)}, bf16[16,512]{1,0:T(8,128)(2,1)S(1)}, u32[]{:S(2)}, u32[]{:S(2)}) collective-permute-start(bf16[16,512]{1,0:T(8,128)(2,1)} %param.9), channel_id=1, source_target_pairs={{0,1},{1,0},{2,3},{3,2},{4,5},{5,4},{6,7},{7,6},{8,9},{9,8},{10,11... | collective-permute-start | bytes 49160 | tf_op jit(solution)/shard_map/ppermute | solution.py:387
  3.0 7.3 %collective-permute-start.1 = (bf16[32,512]{1,0:T(8,128)(2,1)S(1)}, bf16[32,512]{1,0:T(8,128)(2,1)S(1)}, u32[]{:S(2)}, u32[]{:S(2)}) collective-permute-start(bf16[32,512]{1,0:T(8,128)(2,1)S(1)} %constant_dynamic-update-slice_fusion.both), channel_id=1, source_target_pairs={{1,2},{2,1},{3,4},{4,3},{5,6},{6,5},{7,8},{8,7},{9,10},{10,9},{11,... | collective-permute-start | bytes 98312 | tf_op jit(solution)/shard_map/ppermute | solution.py:390
  10.3 3.5 %copy-start.2 = (f32[32]{0:T(128)S(1)}, f32[32]{0:T(128)}, u32[]{:S(2)}) copy-start(f32[32]{0:T(128)} %param.13) | copy-start | bytes 388
  10.3 3.5 %copy-start.1 = (f32[3,32]{1,0:T(4,128)S(1)}, f32[3,32]{1,0:T(4,128)}, u32[]{:S(2)}) copy-start(f32[3,32]{1,0:T(4,128)} %param.15) | copy-start | bytes 1156
  10.3 14.8 %copy-start = (bf16[3,3,3,32,32]{4,3,2,1,0:T(8,128)(2,1)S(1)}, bf16[3,3,3,32,32]{4,3,2,1,0:T(8,128)(2,1)}, u32[]{:S(2)}) copy-start(bf16[3,3,3,32,32]{4,3,2,1,0:T(8,128)(2,1)} %param.14) | copy-start | bytes 165892
  10.3 1.3 %collective-permute-start.2 = (bf16[32,512]{1,0:T(8,128)(2,1)S(1)}, bf16[32,512]{1,0:T(8,128)(2,1)S(1)}, u32[]{:S(2)}, u32[]{:S(2)}) collective-permute-start(bf16[32,512]{1,0:T(8,128)(2,1)S(1)} %collective-permute-done.1.outer), channel_id=1, source_target_pairs={{0,1},{1,0},{2,3},{3,2},{4,5},{5,4},{6,7},{7,6},{8,9},{9,8},{10,11... | collective-permute-start | bytes 98312 | tf_op jit(solution)/shard_map/ppermute | solution.py:399
  13.8 21.8 %all-to-all-start = ((bf16[128,8,128]{2,1,0:T(8,128)(2,1)}), bf16[128,8,128]{2,1,0:T(8,128)(2,1)S(1)}, u32[]{:S(2)}, u32[]{:S(2)}) async-start(bf16[128,8,128]{2,1,0:T(8,128)(2,1)} %get-tuple-element.24), calls=%async_computation | async-start | bytes 524288 | tf_op jit(solution)/shard_map/all_to_all | solution.py:427

commit v16 on v15

--- a/solution.py
+++ b/solution.py
@@ -13,7 +13,7 @@
 GROUP = 4
 TAIL = 32
 WIDE = 2
-UNROLL = (6, 6, 4)
+UNROLL = (8, 8, 4)
 LANES = 256
 PITCH = 40
 FETCH_LIMIT = 50

time: 63.8 us -> 62.7 us (0.983)
  Pallas kernels: 32.5 us -> 31 us
    pallas_call x1, Pallas kernels: 28.5 us -> 27 us  [pair_call(): pl.pallas_call(functools.partial(pair_kernel, gathered.shape[0], place.sh...]
where the time goes in v16:
time: 62.7 us; the launch traced here: 62.6 us
  Pallas kernels  31 us (49%)
  starting transfers between devices  15.4 us (25%)
  waiting for transfers between devices  11.1 us (18%)
  local copies, waits for them, and re-layouts  3.11 us (5%)
  other arithmetic  1.21 us (2%)
  between operations  0.79 us (1%)
    pallas_call x1, Pallas kernels, pair_call(): pl.pallas_call(functools.partial(pair_kernel, gathered.shape[0], place.sh...  27 us
    all_to_all x1, starting transfers between devices, on_device(): lax.all_to_all(parts, AXES, split_axis=0, concat_axis=0, tiled=True)  10.8 us
    all_to_all x1, waiting for transfers between devices, on_device(): lax.all_to_all(parts, AXES, split_axis=0, concat_axis=0, tiled=True)  9.87 us
    ppermute x1, starting transfers between devices, on_device(): from_outer = lax.ppermute(both, AXES, outer)  3.08 us
    pallas_call x1, Pallas kernels, on_device(): pl.pallas_call(functools.partial(encode_kernel, total), out_shape=[jax.Sh...  2.17 us
    pallas_call x1, Pallas kernels, fetch_call(): pl.pallas_call(fetch_kernel, out_shape=jax.ShapeDtypeStruct(far.shape, fa...  1.88 us
    ppermute x1, starting transfers between devices, on_device(): brought = lax.ppermute(features, AXES, inner)  1.42 us
  transfers between devices with their start and end apart: 4, of which 2 were waited for; matrix products, arithmetic and copies ran while one was open for 7% of the time, Pallas kernels for 3%

profile of v16, /device:TPU:1, one launch (start us, length us, event | category | flops | bytes accessed | tf_op | source)
XLA Modules:
  0.0 62.6 jit_solution(17541942357513143205)
XLA Ops:
  0.0 1.4 %collective-permute-start = (bf16[16,512]{1,0:T(8,128)(2,1)}, bf16[16,512]{1,0:T(8,128)(2,1)S(1)}, u32[]{:S(2)}, u32[]{:S(2)}) collective-permute-start(bf16[16,512]{1,0:T(8,128)(2,1)} %param.9), channel_id=1, source_target_pairs={{0,1},{1,0},{2,3},{3,2},{4,5},{5,4},{6,7},{7,6},{8,9},{9,8},{10,11... | collective-permute-start | bytes 49160 | tf_op jit(solution)/shard_map/ppermute | solution.py:387
  2.1 0.1 multiply_cosine_fusion
  2.2 0.1 select_maximum_fusion
  2.3 0.7 %constant_dynamic-update-slice_fusion.1 = bf16[32,512]{1,0:T(8,128)(2,1)S(1)} fusion(bf16[16,512]{1,0:T(8,128)(2,1)} %param.9), kind=kLoop, calls=%fused_computation.41 | loop fusion | bytes 32768
  3.0 0.0 collective-permute-done
  3.0 3.1 %collective-permute-start.1 = (bf16[32,512]{1,0:T(8,128)(2,1)S(1)}, bf16[32,512]{1,0:T(8,128)(2,1)S(1)}, u32[]{:S(2)}, u32[]{:S(2)}) collective-permute-start(bf16[32,512]{1,0:T(8,128)(2,1)S(1)} %constant_dynamic-update-slice_fusion.both), channel_id=1, source_target_pairs={{1,2},{2,1},{3,4},{4,3},{5,6},{6,5},{7,8},{8,7},{9,10},{10,9},{11,... | collective-permute-start | bytes 98312 | tf_op jit(solution)/shard_map/ppermute | solution.py:390
  6.1 0.7 %pad_maximum_fusion.extra = f32[18,512]{1,0:T(8,128)S(1)} fusion(f32[16,512]{1,0:T(8,128)S(1)} %select_maximum_fusion, f32[2,512]{1,0:T(2,128)} %param.11), kind=kLoop, calls=%fused_computation.33 | loop fusion | flops 9216 | bytes 73728 | tf_op jit(solution)/shard_map/concatenate | solution.py:393
  6.8 0.8 %pad.32.proj = bf16[128,512]{1,0:T(8,128)(2,1)S(1)} pad(bf16[64,512]{1,0:T(8,128)(2,1)} %bitcast.20, bf16[]{:T(256)} %constant.34.clone.1), padding=0_64x0_0 | pad | bytes 196610 | tf_op jit(solution)/shard_map/jit(_pad)/pad | solution.py:394
  7.7 0.7 %concatenate.30.place = s32[10]{0:T(128)S(1)} concatenate(s32[1]{0:T(128)} %bitcast.2, s32[1]{0:T(128)} %bitcast.3, s32[1]{0:T(128)} %bitcast.4, s32[1]{0:T(128)} %constant.35.clone.1, s32[1]{0:T(128)} %constant.36.clone.1, s32[5]{0:T(128)} %param.16), dimensions={0} | concatenate | bytes 80 | tf_op jit(solution)/shard_map/concatenate | solution.py:383
  8.4 1.9 %fetch.1.weight = bf16[2,3,512,512]{3,2,1,0:T(8,128)(2,1)S(1)} custom-call(bf16[2,3,512,512]{3,2,1,0:T(8,128)(2,1)} %far), custom_call_target="tpu_custom_call" | custom-call | tf_op jit(solution)/shard_map/fetch/pallas_call | solution.py:46
  10.3 0.0 copy-start.2
  10.3 0.0 copy-start.1
  10.3 0.0 copy-start
  10.3 0.0 collective-permute-done.1.outer
  10.3 0.1 collective-permute-start.2
  10.4 1.2 %collective-permute-done.2.inner = bf16[32,512]{1,0:T(8,128)(2,1)S(1)} collective-permute-done((bf16[32,512]{1,0:T(8,128)(2,1)S(1)}, bf16[32,512]{1,0:T(8,128)(2,1)S(1)}, u32[]{:S(2)}, u32[]{:S(2)}) %collective-permute-start.2) | collective-permute-done | bytes 32800 | tf_op jit(solution)/shard_map/ppermute | solution.py:399
  11.6 2.2 %encode.1 = (bf16[128,8,128]{2,1,0:T(8,128)(2,1)}, bf16[3,3,3,32,32]{4,3,2,1,0:T(8,128)(2,1)S(1)}, f32[4,32]{1,0:T(4,128)S(1)}) custom-call(s32[10]{0:T(128)S(1)} %concatenate.30.place, bf16[32,512]{1,0:T(8,128)(2,1)S(1)} %constant_dynamic-update-slice_fusion.both, bf16[32,512]{1,0:T(8,128)(2,1)S(1)} %collective-permute-done.1.outer, ...), custom_call_target="tpu_custom_call" | custom-call | flops 100663296 | bytes 3145728 | tf_op jit(solution)/shard_map/encode/pallas_call | solution.py:403
  13.8 0.0 copy-done.2
  13.8 0.0 copy-done.1
  13.8 10.8 %all-to-all-start = ((bf16[128,8,128]{2,1,0:T(8,128)(2,1)}), bf16[128,8,128]{2,1,0:T(8,128)(2,1)S(1)}, u32[]{:S(2)}, u32[]{:S(2)}) async-start(bf16[128,8,128]{2,1,0:T(8,128)(2,1)} %get-tuple-element.24), calls=%async_computation | async-start | bytes 524288 | tf_op jit(solution)/shard_map/all_to_all | solution.py:427
  24.7 0.1 copy.30.gain
  24.7 0.1 copy.27
  24.9 0.1 copy.28
  25.0 0.1 copy.29
  25.1 0.0 copy-done
  25.1 0.2 copy.26
  25.3 0.2 reshape.31
  25.5 0.1 fusion.25
  25.6 0.2 fusion.19.weight
  25.8 9.9 %all-to-all-done.parts = bf16[128,8,128]{2,1,0:T(8,128)(2,1)S(1)} async-done(((bf16[128,8,128]{2,1,0:T(8,128)(2,1)}), bf16[128,8,128]{2,1,0:T(8,128)(2,1)S(1)}, u32[]{:S(2)}, u32[]{:S(2)}) %all-to-all-start) | async-done | bytes 262176 | tf_op jit(solution)/shard_map/all_to_all | solution.py:427
  35.6 27.0 %pair_tower.1 = bf16[32,256,128]{2,1,0:T(8,128)(2,1)} custom-call(s32[10]{0:T(128)S(1)} %concatenate.30.place, bf16[128,8,128]{2,1,0:T(8,128)(2,1)S(1)} %all-to-all-done.parts, f32[32,1]{1,0:T(8,128)S(1)} %copy.30.gain, bf16[3,128,608]{2,1,0:T(8,128)(2,1)S(1)} %fusion.19.weight), custom_call_target="tpu_custom_call" | custom-call | flops 3623878656 | bytes 2097152 | tf_op jit(solution)/shard_map/pair_tower/pallas_call | solution.py:333
  (6 shorter events, 0.1 us)
Async XLA Ops:
  0.0 3.0 %collective-permute-start = (bf16[16,512]{1,0:T(8,128)(2,1)}, bf16[16,512]{1,0:T(8,128)(2,1)S(1)}, u32[]{:S(2)}, u32[]{:S(2)}) collective-permute-start(bf16[16,512]{1,0:T(8,128)(2,1)} %param.9), channel_id=1, source_target_pairs={{0,1},{1,0},{2,3},{3,2},{4,5},{5,4},{6,7},{7,6},{8,9},{9,8},{10,11... | collective-permute-start | bytes 49160 | tf_op jit(solution)/shard_map/ppermute | solution.py:387
  3.0 7.3 %collective-permute-start.1 = (bf16[32,512]{1,0:T(8,128)(2,1)S(1)}, bf16[32,512]{1,0:T(8,128)(2,1)S(1)}, u32[]{:S(2)}, u32[]{:S(2)}) collective-permute-start(bf16[32,512]{1,0:T(8,128)(2,1)S(1)} %constant_dynamic-update-slice_fusion.both), channel_id=1, source_target_pairs={{1,2},{2,1},{3,4},{4,3},{5,6},{6,5},{7,8},{8,7},{9,10},{10,9},{11,... | collective-permute-start | bytes 98312 | tf_op jit(solution)/shard_map/ppermute | solution.py:390
  10.3 3.5 %copy-start.2 = (f32[32]{0:T(128)S(1)}, f32[32]{0:T(128)}, u32[]{:S(2)}) copy-start(f32[32]{0:T(128)} %param.13) | copy-start | bytes 388
  10.3 3.5 %copy-start.1 = (f32[3,32]{1,0:T(4,128)S(1)}, f32[3,32]{1,0:T(4,128)}, u32[]{:S(2)}) copy-start(f32[3,32]{1,0:T(4,128)} %param.15) | copy-start | bytes 1156
  10.3 14.8 %copy-start = (bf16[3,3,3,32,32]{4,3,2,1,0:T(8,128)(2,1)S(1)}, bf16[3,3,3,32,32]{4,3,2,1,0:T(8,128)(2,1)}, u32[]{:S(2)}) copy-start(bf16[3,3,3,32,32]{4,3,2,1,0:T(8,128)(2,1)} %param.14) | copy-start | bytes 165892
  10.3 1.3 %collective-permute-start.2 = (bf16[32,512]{1,0:T(8,128)(2,1)S(1)}, bf16[32,512]{1,0:T(8,128)(2,1)S(1)}, u32[]{:S(2)}, u32[]{:S(2)}) collective-permute-start(bf16[32,512]{1,0:T(8,128)(2,1)S(1)} %collective-permute-done.1.outer), channel_id=1, source_target_pairs={{0,1},{1,0},{2,3},{3,2},{4,5},{5,4},{6,7},{7,6},{8,9},{9,8},{10,11... | collective-permute-start | bytes 98312 | tf_op jit(solution)/shard_map/ppermute | solution.py:399
  13.8 21.8 %all-to-all-start = ((bf16[128,8,128]{2,1,0:T(8,128)(2,1)}), bf16[128,8,128]{2,1,0:T(8,128)(2,1)S(1)}, u32[]{:S(2)}, u32[]{:S(2)}) async-start(bf16[128,8,128]{2,1,0:T(8,128)(2,1)} %get-tuple-element.24), calls=%async_computation | async-start | bytes 524288 | tf_op jit(solution)/shard_map/all_to_all | solution.py:427

commit v17 on v15

--- a/solution.py
+++ b/solution.py
@@ -198,14 +198,14 @@
     store_first = keep(field_a, dils[0], False)
     first_row, last_row_needed = margin - need, margin + tile_rows + need - 1
 
-    @pl.loop(first_row // half, last_row_needed // half + 1)
+    @pl.loop(first_row // shard, last_row_needed // shard + 1)
     def _(block):
-        first = pl.multiple_of(block * half, half)
-        spot = block // 2 * half
-        turned = row_turned[block % 2 * 2 + spot // 128]
-        apart = distance[pl.ds(first, half), :]
-        for k in range(half):
-            pick = jnp.full((chans, 128), spot % 128 + k, jnp.int32)
+        first = pl.multiple_of(block * shard, shard)
+        spot = block * half
+        apart = distance[pl.ds(first, shard), :]
+        for k in range(shard):
+            turned = row_turned[k // half * 2 + spot // 128]
+            pick = jnp.full((chans, 128), spot % 128 + k % half, jnp.int32)
             row_term = jnp.take_along_axis(turned, pick, axis=1)
             row_term = jnp.concatenate([row_term, row_term], axis=1)
             value = row_term + col_turned + gain_wide * apart[k : k + 1, :]

time: 63.8 us -> 70.9 us (1.11); the launches traced: 64.1 us -> 72.2 us
  Pallas kernels: 32.5 us -> 40.7 us
    pallas_call x1, Pallas kernels: 28.5 us -> 36.6 us  [pair_call(): pl.pallas_call(functools.partial(pair_kernel, gathered.shape[0], place.sh...]
  transfers between devices with their start and end apart: 4 -> 4, of which waited for: 2 -> 2; matrix products, arithmetic and copies ran while one was open for 7% -> 6% of each run, Pallas kernels for 3% -> 3%
where the time goes in v17:
time: 70.9 us; the launch traced here: 72.2 us
  Pallas kernels  40.7 us (57%)
  starting transfers between devices  15.4 us (22%)
  waiting for transfers between devices  11.1 us (16%)
  local copies, waits for them, and re-layouts  3.11 us (4%)
  other arithmetic  1.21 us (2%)
  between operations  0.79 us (1%)
    pallas_call x1, Pallas kernels, pair_call(): pl.pallas_call(functools.partial(pair_kernel, gathered.shape[0], place.sh...  36.6 us
    all_to_all x1, starting transfers between devices, on_device(): lax.all_to_all(parts, AXES, split_axis=0, concat_axis=0, tiled=True)  10.8 us
    all_to_all x1, waiting for transfers between devices, on_device(): lax.all_to_all(parts, AXES, split_axis=0, concat_axis=0, tiled=True)  9.87 us
    ppermute x1, starting transfers between devices, on_device(): from_outer = lax.ppermute(both, AXES, outer)  3.08 us
    pallas_call x1, Pallas kernels, on_device(): pl.pallas_call(functools.partial(encode_kernel, total), out_shape=[jax.Sh...  2.17 us
    pallas_call x1, Pallas kernels, fetch_call(): pl.pallas_call(fetch_kernel, out_shape=jax.ShapeDtypeStruct(far.shape, fa...  1.88 us
    ppermute x1, starting transfers between devices, on_device(): brought = lax.ppermute(features, AXES, inner)  1.42 us
  transfers between devices with their start and end apart: 4, of which 2 were waited for; matrix products, arithmetic and copies ran while one was open for 6% of the time, Pallas kernels for 3%

profile of v17, /device:TPU:1, one launch (start us, length us, event | category | flops | bytes accessed | tf_op | source)
XLA Modules:
  0.0 72.2 jit_solution(12796218912128032782)
XLA Ops:
  0.0 1.4 %collective-permute-start = (bf16[16,512]{1,0:T(8,128)(2,1)}, bf16[16,512]{1,0:T(8,128)(2,1)S(1)}, u32[]{:S(2)}, u32[]{:S(2)}) collective-permute-start(bf16[16,512]{1,0:T(8,128)(2,1)} %param.9), channel_id=1, source_target_pairs={{0,1},{1,0},{2,3},{3,2},{4,5},{5,4},{6,7},{7,6},{8,9},{9,8},{10,11... | collective-permute-start | bytes 49160 | tf_op jit(solution)/shard_map/ppermute | solution.py:387
  2.1 0.1 multiply_cosine_fusion
  2.2 0.1 select_maximum_fusion
  2.3 0.7 constant_dynamic-update-slice_fusion.1
  3.0 0.0 collective-permute-done
  3.0 3.1 %collective-permute-start.1 = (bf16[32,512]{1,0:T(8,128)(2,1)S(1)}, bf16[32,512]{1,0:T(8,128)(2,1)S(1)}, u32[]{:S(2)}, u32[]{:S(2)}) collective-permute-start(bf16[32,512]{1,0:T(8,128)(2,1)S(1)} %constant_dynamic-update-slice_fusion.both), channel_id=1, source_target_pairs={{1,2},{2,1},{3,4},{4,3},{5,6},{6,5},{7,8},{8,7},{9,10},{10,9},{11,... | collective-permute-start | bytes 98312 | tf_op jit(solution)/shard_map/ppermute | solution.py:390
  6.1 0.7 pad_maximum_fusion.extra
  6.8 0.8 %pad.32.proj = bf16[128,512]{1,0:T(8,128)(2,1)S(1)} pad(bf16[64,512]{1,0:T(8,128)(2,1)} %bitcast.20, bf16[]{:T(256)} %constant.34.clone.1), padding=0_64x0_0 | pad | bytes 196610 | tf_op jit(solution)/shard_map/jit(_pad)/pad | solution.py:394
  7.7 0.7 %concatenate.30.place = s32[10]{0:T(128)S(1)} concatenate(s32[1]{0:T(128)} %bitcast.2, s32[1]{0:T(128)} %bitcast.3, s32[1]{0:T(128)} %bitcast.4, s32[1]{0:T(128)} %constant.35.clone.1, s32[1]{0:T(128)} %constant.36.clone.1, s32[5]{0:T(128)} %param.16), dimensions={0} | concatenate | bytes 80 | tf_op jit(solution)/shard_map/concatenate | solution.py:383
  8.4 1.9 %fetch.1.weight = bf16[2,3,512,512]{3,2,1,0:T(8,128)(2,1)S(1)} custom-call(bf16[2,3,512,512]{3,2,1,0:T(8,128)(2,1)} %far), custom_call_target="tpu_custom_call" | custom-call | tf_op jit(solution)/shard_map/fetch/pallas_call | solution.py:46
  10.3 0.0 copy-start.2
  10.3 0.0 copy-start.1
  10.3 0.0 copy-start
  10.3 0.0 collective-permute-done.1.outer
  10.3 0.1 collective-permute-start.2
  10.4 1.2 %collective-permute-done.2.inner = bf16[32,512]{1,0:T(8,128)(2,1)S(1)} collective-permute-done((bf16[32,512]{1,0:T(8,128)(2,1)S(1)}, bf16[32,512]{1,0:T(8,128)(2,1)S(1)}, u32[]{:S(2)}, u32[]{:S(2)}) %collective-permute-start.2) | collective-permute-done | bytes 32800 | tf_op jit(solution)/shard_map/ppermute | solution.py:399
  11.6 2.2 %encode.1 = (bf16[128,8,128]{2,1,0:T(8,128)(2,1)}, bf16[3,3,3,32,32]{4,3,2,1,0:T(8,128)(2,1)S(1)}, f32[4,32]{1,0:T(4,128)S(1)}) custom-call(s32[10]{0:T(128)S(1)} %concatenate.30.place, bf16[32,512]{1,0:T(8,128)(2,1)S(1)} %constant_dynamic-update-slice_fusion.both, bf16[32,512]{1,0:T(8,128)(2,1)S(1)} %collective-permute-done.1.outer, ...), custom_call_target="tpu_custom_call" | custom-call | flops 100663296 | bytes 3145728 | tf_op jit(solution)/shard_map/encode/pallas_call | solution.py:403
  13.8 0.0 copy-done.2
  13.8 0.0 copy-done.1
  13.8 10.8 %all-to-all-start = ((bf16[128,8,128]{2,1,0:T(8,128)(2,1)}), bf16[128,8,128]{2,1,0:T(8,128)(2,1)S(1)}, u32[]{:S(2)}, u32[]{:S(2)}) async-start(bf16[128,8,128]{2,1,0:T(8,128)(2,1)} %get-tuple-element.24), calls=%async_computation | async-start | bytes 524288 | tf_op jit(solution)/shard_map/all_to_all | solution.py:427
  24.6 0.1 copy.30.gain
  24.7 0.1 copy.27
  24.9 0.1 copy.28
  25.0 0.1 copy.29
  25.1 0.0 copy-done
  25.1 0.2 copy.26
  25.3 0.2 reshape.31
  25.5 0.1 fusion.25
  25.6 0.2 fusion.19.weight
  25.8 9.9 %all-to-all-done.parts = bf16[128,8,128]{2,1,0:T(8,128)(2,1)S(1)} async-done(((bf16[128,8,128]{2,1,0:T(8,128)(2,1)}), bf16[128,8,128]{2,1,0:T(8,128)(2,1)S(1)}, u32[]{:S(2)}, u32[]{:S(2)}) %all-to-all-start) | async-done | bytes 262176 | tf_op jit(solution)/shard_map/all_to_all | solution.py:427
  35.6 36.6 %pair_tower.1 = bf16[32,256,128]{2,1,0:T(8,128)(2,1)} custom-call(s32[10]{0:T(128)S(1)} %concatenate.30.place, bf16[128,8,128]{2,1,0:T(8,128)(2,1)S(1)} %all-to-all-done.parts, f32[32,1]{1,0:T(8,128)S(1)} %copy.30.gain, bf16[3,128,608]{2,1,0:T(8,128)(2,1)S(1)} %fusion.19.weight), custom_call_target="tpu_custom_call" | custom-call | flops 3623878656 | bytes 2097152 | tf_op jit(solution)/shard_map/pair_tower/pallas_call | solution.py:333
  (6 shorter events, 0.1 us)
Async XLA Ops:
  0.0 3.0 %collective-permute-start = (bf16[16,512]{1,0:T(8,128)(2,1)}, bf16[16,512]{1,0:T(8,128)(2,1)S(1)}, u32[]{:S(2)}, u32[]{:S(2)}) collective-permute-start(bf16[16,512]{1,0:T(8,128)(2,1)} %param.9), channel_id=1, source_target_pairs={{0,1},{1,0},{2,3},{3,2},{4,5},{5,4},{6,7},{7,6},{8,9},{9,8},{10,11... | collective-permute-start | bytes 49160 | tf_op jit(solution)/shard_map/ppermute | solution.py:387
  3.0 7.3 %collective-permute-start.1 = (bf16[32,512]{1,0:T(8,128)(2,1)S(1)}, bf16[32,512]{1,0:T(8,128)(2,1)S(1)}, u32[]{:S(2)}, u32[]{:S(2)}) collective-permute-start(bf16[32,512]{1,0:T(8,128)(2,1)S(1)} %constant_dynamic-update-slice_fusion.both), channel_id=1, source_target_pairs={{1,2},{2,1},{3,4},{4,3},{5,6},{6,5},{7,8},{8,7},{9,10},{10,9},{11,... | collective-permute-start | bytes 98312 | tf_op jit(solution)/shard_map/ppermute | solution.py:390
  10.3 3.5 %copy-start.2 = (f32[32]{0:T(128)S(1)}, f32[32]{0:T(128)}, u32[]{:S(2)}) copy-start(f32[32]{0:T(128)} %param.13) | copy-start | bytes 388
  10.3 3.5 %copy-start.1 = (f32[3,32]{1,0:T(4,128)S(1)}, f32[3,32]{1,0:T(4,128)}, u32[]{:S(2)}) copy-start(f32[3,32]{1,0:T(4,128)} %param.15) | copy-start | bytes 1156
  10.3 14.8 %copy-start = (bf16[3,3,3,32,32]{4,3,2,1,0:T(8,128)(2,1)S(1)}, bf16[3,3,3,32,32]{4,3,2,1,0:T(8,128)(2,1)}, u32[]{:S(2)}) copy-start(bf16[3,3,3,32,32]{4,3,2,1,0:T(8,128)(2,1)} %param.14) | copy-start | bytes 165892
  10.3 1.3 %collective-permute-start.2 = (bf16[32,512]{1,0:T(8,128)(2,1)S(1)}, bf16[32,512]{1,0:T(8,128)(2,1)S(1)}, u32[]{:S(2)}, u32[]{:S(2)}) collective-permute-start(bf16[32,512]{1,0:T(8,128)(2,1)S(1)} %collective-permute-done.1.outer), channel_id=1, source_target_pairs={{0,1},{1,0},{2,3},{3,2},{4,5},{5,4},{6,7},{7,6},{8,9},{9,8},{10,11... | collective-permute-start | bytes 98312 | tf_op jit(solution)/shard_map/ppermute | solution.py:399
  13.8 21.8 %all-to-all-start = ((bf16[128,8,128]{2,1,0:T(8,128)(2,1)}), bf16[128,8,128]{2,1,0:T(8,128)(2,1)S(1)}, u32[]{:S(2)}, u32[]{:S(2)}) async-start(bf16[128,8,128]{2,1,0:T(8,128)(2,1)} %get-tuple-element.24), calls=%async_computation | async-start | bytes 524288 | tf_op jit(solution)/shard_map/all_to_all | solution.py:427

commit v18 on v15

--- a/solution.py
+++ b/solution.py
@@ -198,17 +198,16 @@
     store_first = keep(field_a, dils[0], False)
     first_row, last_row_needed = margin - need, margin + tile_rows + need - 1
 
-    @pl.loop(first_row // half, last_row_needed // half + 1)
+    @pl.loop(first_row // 4, last_row_needed // 4 + 1)
     def _(block):
-        first = pl.multiple_of(block * half, half)
-        spot = block // 2 * half
-        turned = row_turned[block % 2 * 2 + spot // 128]
-        apart = distance[pl.ds(first, half), :]
-        for k in range(half):
+        first = block * 4
+        spot = block // 4 * half + block % 2 * 4
+        turned = row_turned[block // 2 % 2 * 2 + spot // 128]
+        for k in range(4):
             pick = jnp.full((chans, 128), spot % 128 + k, jnp.int32)
             row_term = jnp.take_along_axis(turned, pick, axis=1)
             row_term = jnp.concatenate([row_term, row_term], axis=1)
-            value = row_term + col_turned + gain_wide * apart[k : k + 1, :]
+            value = row_term + col_turned + gain_wide * distance[pl.ds(first + k, 1), :]
             value = jnp.maximum(value, 0.0)
             store_first(first + k, value[:, :128], value[:, 128:])
 

time: 63.8 us -> 69.8 us (1.094)
  Pallas kernels: 32.5 us -> 38.2 us
    pallas_call x1, Pallas kernels: 28.5 us -> 34.1 us  [pair_call(): pl.pallas_call(functools.partial(pair_kernel, gathered.shape[0], place.sh...]
  transfers between devices with their start and end apart: 4 -> 4, of which waited for: 2 -> 2; matrix products, arithmetic and copies ran while one was open for 7% -> 6% of each run, Pallas kernels for 3% -> 3%
where the time goes in v18:
time: 69.8 us
  Pallas kernels  38.2 us (55%)
  starting transfers between devices  15.4 us (22%)
  waiting for transfers between devices  11.1 us (16%)
  local copies, waits for them, and re-layouts  3.11 us (4%)
  other arithmetic  1.21 us (2%)
  between operations  0.79 us (1%)
    pallas_call x1, Pallas kernels, pair_call(): pl.pallas_call(functools.partial(pair_kernel, gathered.shape[0], place.sh...  34.1 us
    all_to_all x1, starting transfers between devices, on_device(): lax.all_to_all(parts, AXES, split_axis=0, concat_axis=0, tiled=True)  10.8 us
    all_to_all x1, waiting for transfers between devices, on_device(): lax.all_to_all(parts, AXES, split_axis=0, concat_axis=0, tiled=True)  9.87 us
    ppermute x1, starting transfers between devices, on_device(): from_outer = lax.ppermute(both, AXES, outer)  3.08 us
    pallas_call x1, Pallas kernels, on_device(): pl.pallas_call(functools.partial(encode_kernel, total), out_shape=[jax.Sh...  2.17 us
    pallas_call x1, Pallas kernels, fetch_call(): pl.pallas_call(fetch_kernel, out_shape=jax.ShapeDtypeStruct(far.shape, fa...  1.88 us
    ppermute x1, starting transfers between devices, on_device(): brought = lax.ppermute(features, AXES, inner)  1.42 us
  transfers between devices with their start and end apart: 4, of which 2 were waited for; matrix products, arithmetic and copies ran while one was open for 6% of the time, Pallas kernels for 3%

profile of v18, /device:TPU:1, one launch (start us, length us, event | category | flops | bytes accessed | tf_op | source)
XLA Modules:
  0.0 69.8 jit_solution(15714500575124094835)
XLA Ops:
  0.0 1.4 %collective-permute-start = (bf16[16,512]{1,0:T(8,128)(2,1)}, bf16[16,512]{1,0:T(8,128)(2,1)S(1)}, u32[]{:S(2)}, u32[]{:S(2)}) collective-permute-start(bf16[16,512]{1,0:T(8,128)(2,1)} %param.9), channel_id=1, source_target_pairs={{0,1},{1,0},{2,3},{3,2},{4,5},{5,4},{6,7},{7,6},{8,9},{9,8},{10,11... | collective-permute-start | bytes 49160 | tf_op jit(solution)/shard_map/ppermute | solution.py:386
  2.1 0.1 multiply_cosine_fusion
  2.2 0.1 select_maximum_fusion
  2.3 0.7 %constant_dynamic-update-slice_fusion.1 = bf16[32,512]{1,0:T(8,128)(2,1)S(1)} fusion(bf16[16,512]{1,0:T(8,128)(2,1)} %param.9), kind=kLoop, calls=%fused_computation.41 | loop fusion | bytes 32768
  3.0 0.0 collective-permute-done
  3.0 3.1 %collective-permute-start.1 = (bf16[32,512]{1,0:T(8,128)(2,1)S(1)}, bf16[32,512]{1,0:T(8,128)(2,1)S(1)}, u32[]{:S(2)}, u32[]{:S(2)}) collective-permute-start(bf16[32,512]{1,0:T(8,128)(2,1)S(1)} %constant_dynamic-update-slice_fusion.both), channel_id=1, source_target_pairs={{1,2},{2,1},{3,4},{4,3},{5,6},{6,5},{7,8},{8,7},{9,10},{10,9},{11,... | collective-permute-start | bytes 98312 | tf_op jit(solution)/shard_map/ppermute | solution.py:389
  6.1 0.7 pad_maximum_fusion.extra
  6.8 0.8 %pad.32.proj = bf16[128,512]{1,0:T(8,128)(2,1)S(1)} pad(bf16[64,512]{1,0:T(8,128)(2,1)} %bitcast.20, bf16[]{:T(256)} %constant.34.clone.1), padding=0_64x0_0 | pad | bytes 196610 | tf_op jit(solution)/shard_map/jit(_pad)/pad | solution.py:393
  7.7 0.7 %concatenate.30.place = s32[10]{0:T(128)S(1)} concatenate(s32[1]{0:T(128)} %bitcast.2, s32[1]{0:T(128)} %bitcast.3, s32[1]{0:T(128)} %bitcast.4, s32[1]{0:T(128)} %constant.35.clone.1, s32[1]{0:T(128)} %constant.36.clone.1, s32[5]{0:T(128)} %param.16), dimensions={0} | concatenate | bytes 80 | tf_op jit(solution)/shard_map/concatenate | solution.py:382
  8.4 1.9 %fetch.1.weight = bf16[2,3,512,512]{3,2,1,0:T(8,128)(2,1)S(1)} custom-call(bf16[2,3,512,512]{3,2,1,0:T(8,128)(2,1)} %far), custom_call_target="tpu_custom_call" | custom-call | tf_op jit(solution)/shard_map/fetch/pallas_call | solution.py:46
  10.3 0.0 copy-start.2
  10.3 0.0 copy-start.1
  10.3 0.0 copy-start
  10.3 0.0 collective-permute-done.1.outer
  10.3 0.1 collective-permute-start.2
  10.4 1.2 %collective-permute-done.2.inner = bf16[32,512]{1,0:T(8,128)(2,1)S(1)} collective-permute-done((bf16[32,512]{1,0:T(8,128)(2,1)S(1)}, bf16[32,512]{1,0:T(8,128)(2,1)S(1)}, u32[]{:S(2)}, u32[]{:S(2)}) %collective-permute-start.2) | collective-permute-done | bytes 32800 | tf_op jit(solution)/shard_map/ppermute | solution.py:398
  11.6 2.2 %encode.1 = (bf16[128,8,128]{2,1,0:T(8,128)(2,1)}, bf16[3,3,3,32,32]{4,3,2,1,0:T(8,128)(2,1)S(1)}, f32[4,32]{1,0:T(4,128)S(1)}) custom-call(s32[10]{0:T(128)S(1)} %concatenate.30.place, bf16[32,512]{1,0:T(8,128)(2,1)S(1)} %constant_dynamic-update-slice_fusion.both, bf16[32,512]{1,0:T(8,128)(2,1)S(1)} %collective-permute-done.1.outer, ...), custom_call_target="tpu_custom_call" | custom-call | flops 100663296 | bytes 3145728 | tf_op jit(solution)/shard_map/encode/pallas_call | solution.py:402
  13.8 0.0 copy-done.2
  13.8 0.0 copy-done.1
  13.8 10.8 %all-to-all-start = ((bf16[128,8,128]{2,1,0:T(8,128)(2,1)}), bf16[128,8,128]{2,1,0:T(8,128)(2,1)S(1)}, u32[]{:S(2)}, u32[]{:S(2)}) async-start(bf16[128,8,128]{2,1,0:T(8,128)(2,1)} %get-tuple-element.24), calls=%async_computation | async-start | bytes 524288 | tf_op jit(solution)/shard_map/all_to_all | solution.py:426
  24.6 0.1 copy.30.gain
  24.7 0.1 copy.27
  24.9 0.1 copy.28
  25.0 0.1 copy.29
  25.1 0.0 copy-done
  25.1 0.2 copy.26
  25.3 0.2 reshape.31
  25.5 0.1 fusion.25
  25.6 0.2 fusion.19.weight
  25.8 9.9 %all-to-all-done.parts = bf16[128,8,128]{2,1,0:T(8,128)(2,1)S(1)} async-done(((bf16[128,8,128]{2,1,0:T(8,128)(2,1)}), bf16[128,8,128]{2,1,0:T(8,128)(2,1)S(1)}, u32[]{:S(2)}, u32[]{:S(2)}) %all-to-all-start) | async-done | bytes 262176 | tf_op jit(solution)/shard_map/all_to_all | solution.py:426
  35.6 34.1 %pair_tower.1 = bf16[32,256,128]{2,1,0:T(8,128)(2,1)} custom-call(s32[10]{0:T(128)S(1)} %concatenate.30.place, bf16[128,8,128]{2,1,0:T(8,128)(2,1)S(1)} %all-to-all-done.parts, f32[32,1]{1,0:T(8,128)S(1)} %copy.30.gain, bf16[3,128,608]{2,1,0:T(8,128)(2,1)S(1)} %fusion.19.weight), custom_call_target="tpu_custom_call" | custom-call | flops 3623878656 | bytes 2097152 | tf_op jit(solution)/shard_map/pair_tower/pallas_call | solution.py:332
  (6 shorter events, 0.1 us)
Async XLA Ops:
  0.0 3.0 %collective-permute-start = (bf16[16,512]{1,0:T(8,128)(2,1)}, bf16[16,512]{1,0:T(8,128)(2,1)S(1)}, u32[]{:S(2)}, u32[]{:S(2)}) collective-permute-start(bf16[16,512]{1,0:T(8,128)(2,1)} %param.9), channel_id=1, source_target_pairs={{0,1},{1,0},{2,3},{3,2},{4,5},{5,4},{6,7},{7,6},{8,9},{9,8},{10,11... | collective-permute-start | bytes 49160 | tf_op jit(solution)/shard_map/ppermute | solution.py:386
  3.0 7.3 %collective-permute-start.1 = (bf16[32,512]{1,0:T(8,128)(2,1)S(1)}, bf16[32,512]{1,0:T(8,128)(2,1)S(1)}, u32[]{:S(2)}, u32[]{:S(2)}) collective-permute-start(bf16[32,512]{1,0:T(8,128)(2,1)S(1)} %constant_dynamic-update-slice_fusion.both), channel_id=1, source_target_pairs={{1,2},{2,1},{3,4},{4,3},{5,6},{6,5},{7,8},{8,7},{9,10},{10,9},{11,... | collective-permute-start | bytes 98312 | tf_op jit(solution)/shard_map/ppermute | solution.py:389
  10.3 3.5 %copy-start.2 = (f32[32]{0:T(128)S(1)}, f32[32]{0:T(128)}, u32[]{:S(2)}) copy-start(f32[32]{0:T(128)} %param.13) | copy-start | bytes 388
  10.3 3.5 %copy-start.1 = (f32[3,32]{1,0:T(4,128)S(1)}, f32[3,32]{1,0:T(4,128)}, u32[]{:S(2)}) copy-start(f32[3,32]{1,0:T(4,128)} %param.15) | copy-start | bytes 1156
  10.3 14.8 %copy-start = (bf16[3,3,3,32,32]{4,3,2,1,0:T(8,128)(2,1)S(1)}, bf16[3,3,3,32,32]{4,3,2,1,0:T(8,128)(2,1)}, u32[]{:S(2)}) copy-start(bf16[3,3,3,32,32]{4,3,2,1,0:T(8,128)(2,1)} %param.14) | copy-start | bytes 165892
  10.3 1.3 %collective-permute-start.2 = (bf16[32,512]{1,0:T(8,128)(2,1)S(1)}, bf16[32,512]{1,0:T(8,128)(2,1)S(1)}, u32[]{:S(2)}, u32[]{:S(2)}) collective-permute-start(bf16[32,512]{1,0:T(8,128)(2,1)S(1)} %collective-permute-done.1.outer), channel_id=1, source_target_pairs={{0,1},{1,0},{2,3},{3,2},{4,5},{5,4},{6,7},{7,6},{8,9},{9,8},{10,11... | collective-permute-start | bytes 98312 | tf_op jit(solution)/shard_map/ppermute | solution.py:398
  13.8 21.8 %all-to-all-start = ((bf16[128,8,128]{2,1,0:T(8,128)(2,1)}), bf16[128,8,128]{2,1,0:T(8,128)(2,1)S(1)}, u32[]{:S(2)}, u32[]{:S(2)}) async-start(bf16[128,8,128]{2,1,0:T(8,128)(2,1)} %get-tuple-element.24), calls=%async_computation | async-start | bytes 524288 | tf_op jit(solution)/shard_map/all_to_all | solution.py:426
